TPU v7x, 256 devices: a whole 4x4x8 slice. The times are simulated.
256 devices in a mesh: cell: 32 (over x_hi, z, core), chrom: 8 (over x_lo, y).
Axes of the slice: x: 4 (x_hi: 2, x_lo: 2; x = x_hi * 2 + x_lo), y: 4, z: 8, core: 2. Of those that a mesh axis runs over, the one named last changes fastest.
Arguments:
- cell_factors: bfloat16 [32768, 256], P('cell'), may hold values from -6 to 6
- peak_factors: bfloat16 [524288, 256], P(('cell', 'chrom')), may hold values from -6 to 6
- tile_values: bfloat16 [96, 256, 128, 128], P('cell', 'chrom'), may hold values from -6 to 6
- tile_index: int32 [96, 256], P('cell', 'chrom'), may hold values from 0 to 127, as said below
- tile_counts: int32 [96, 8], P('cell', 'chrom'), may hold values from 8 to 32, as said below
Outputs:
- peak_out: bfloat16 [524288, 256], P(('cell', 'chrom'))
- cell_grads: float32 [32768, 256], P(('cell', 'chrom'))
Inputs may be any that keep to these rules, and one draw needn't show every extreme that they name: `tile_index`: within one cell index, stratum and chrom group the 32 numbers are distinct. `tile_counts`: in every stratum one cell index has 32 live slots in every chrom group; every other count is 32, 16 or 8.
All inputs are finite; a program needn't handle non-finite values.
Results may differ from a plain program's by a relative error of at most 0.015.
Values may be sent and summed in bfloat16 or wider, within the bound.
No kernel may reach another device: no remote copies, remote signals or barrier semaphores. Data moves between devices by JAX's collectives and lax.ppermute only.
A program may use at most 64 MiB of HBM per device.

v0:
```python
import math

import jax
import jax.numpy as jnp
from jax import lax
from jax.sharding import PartitionSpec as P

learning_rate = 0.15
gradient_scale = 0.1


def passed_along(value, axis, by):
    count = lax.axis_size(axis)
    return lax.ppermute(value, axis, [(i, (i + by) % count) for i in range(count)])


def stratum_update(cell_blocks, peak_block, values, index, live_count):
    row_tiles, tile_size, rank_width = cell_blocks.shape
    peak_tiles = peak_block.shape[0]
    slot_count = index.shape[0]
    scaling = 1.0 / math.sqrt(rank_width)
    cell_rows = index // peak_tiles
    peak_cols = index % peak_tiles
    left_tiles = jnp.take(cell_blocks, cell_rows, axis=0)
    right_tiles = jnp.take(peak_block, peak_cols, axis=0)
    predicted = (
        jnp.einsum("tak,tbk->tab", left_tiles, right_tiles, preferred_element_type=jnp.float32)
        * scaling
    )
    live_mask = jnp.arange(slot_count, dtype=jnp.int32) < live_count
    residual = jnp.where(
        live_mask[:, None, None], predicted - values.astype(jnp.float32), 0.0
    ).astype(jnp.bfloat16)
    dense_resid = jnp.zeros((row_tiles, peak_tiles, tile_size, tile_size), jnp.bfloat16)
    dense_resid = dense_resid.at[cell_rows, peak_cols].set(residual)
    peak_grad = (
        jnp.einsum("rcab,rak->cbk", dense_resid, cell_blocks, preferred_element_type=jnp.float32)
        * scaling
    )
    cell_grad = (
        jnp.einsum("rcab,cbk->rak", dense_resid, peak_block, preferred_element_type=jnp.float32)
        * scaling
    )
    new_block = (peak_block.astype(jnp.float32) - learning_rate * peak_grad).astype(jnp.bfloat16)
    return (new_block, cell_grad)


def per_device(cell_factors, peak_factors, tile_values, tile_index, tile_counts):
    cell_dev, rank_width = cell_factors.shape
    tile_size = tile_values.shape[-1]
    strata = tile_values.shape[0]
    block_rows = peak_factors.shape[0]
    row_tiles = cell_dev // tile_size
    peak_tiles = block_rows // tile_size
    share_rows = cell_dev // lax.axis_size("chrom")
    cell_blocks = cell_factors.reshape(row_tiles, tile_size, rank_width)
    peak_block = peak_factors.reshape(peak_tiles, tile_size, rank_width)
    local_sum = jnp.zeros((cell_dev, rank_width), jnp.float32)
    for stratum in range(strata):
        if stratum > 0:
            peak_block = passed_along(peak_block, "cell", -1)
        peak_block, cell_grad = stratum_update(
            cell_blocks,
            peak_block,
            tile_values[stratum],
            tile_index[stratum],
            tile_counts[stratum, 0],
        )
        cell_term = cell_grad.reshape(cell_dev, rank_width) * gradient_scale
        local_sum = local_sum + cell_term
    whole_sum = lax.psum(local_sum.astype(jnp.bfloat16), "chrom").astype(jnp.float32)
    summed = lax.dynamic_slice_in_dim(
        whole_sum, lax.axis_index("chrom") * share_rows, share_rows, 0
    )
    peak_block = passed_along(peak_block, "cell", strata - 1)
    return (peak_block.reshape(block_rows, rank_width), summed)


def solution(mesh):
    in_specs = (
        P("cell", None),
        P(("cell", "chrom"), None),
        P("cell", "chrom", None, None),
        P("cell", "chrom"),
        P("cell", "chrom"),
    )
    out_specs = (P(("cell", "chrom"), None), P(("cell", "chrom"), None))
    return jax.shard_map(
        per_device, mesh=mesh, in_specs=in_specs, out_specs=out_specs, check_vma=False
    )
```

profile of v0, /device:TPU:4, one launch (start us, length us, event | category | flops | bytes accessed | tf_op | source)
XLA Modules:
  0.0 207.0 jit_solution(7965982034249529058)
XLA Ops:
  7.2 0.0 copy-start
  7.2 0.0 all-reduce.2.cloned.1.call-start
  7.2 1.4 fusion.57
  8.6 0.8 fusion.51
  9.4 1.5 compare_and_fusion.1
  10.9 0.0 copy-done
  10.9 0.0 copy-start.3
  10.9 2.0 gather_fusion
  12.9 0.0 copy-done.3
  12.9 2.0 gather_fusion.1
  14.9 3.3 %fusion.5 = bf16[32,128,128]{2,1,0:T(8,128)(2,1)S(1)} fusion(bf16[32,128,256]{2,1,0:T(8,128)(2,1)} %gather_fusion.1, pred[32]{0:T(512)(128)(4,1)S(1)} %get-tuple-element.17, bf16[32,128,256]{2,1,0:T(8,128)(2,1)} %gather_fusion, pred[32]{0:T(512)(128)(4,1)S(1)} %get-tuple-element.22, bf16[3,32,128,128]{3,2,1,0:T(8,128)(2,1)} %param.11, ...), kind=kOutput, calls=%fused_computation.17 | convolution fusion | flops 273154048 | bytes 6291552 | tf_op jit(solution)/shard_map/tak,tbk->tab/dot_general | solution.py:27
  18.3 3.0 %broadcast.375.clone = bf16[8,16,128,128]{3,2,1,0:T(8,128)(2,1)} broadcast(bf16[]{:T(256)} %constant.94.clone.1), dimensions={} | broadcast | bytes 4194306 | tf_op jit(solution)/shard_map/broadcast.18
  21.3 5.0 %scatter_fusion = bf16[8,16,128,128]{3,2,1,0:T(8,128)(2,1)} fusion(bf16[8,16,128,128]{3,2,1,0:T(8,128)(2,1)} %broadcast.375.clone, s32[32]{0:T(128)S(1)} %get-tuple-element.26, bf16[32,128,128]{2,1,0:T(8,128)(2,1)S(1)} %fusion.5), kind=kCustom, calls=%fused_computation.6 | custom fusion | bytes 3145984 | tf_op jit(solution)/shard_map/scatter | solution.py:35
  26.3 4.5 %fusion.11 = bf16[16,128,256]{2,1,0:T(8,128)(2,1)} fusion(bf16[16,128,256]{2,1,0:T(8,128)(2,1)S(1)} %bitcast.179, bf16[8,16,128,128]{3,2,1,0:T(8,128)(2,1)} %scatter_fusion, bf16[8,128,256,1]{2,1,3,0:T(8,128)(2,1)S(1)} %bitcast.175), kind=kOutput, calls=%fused_computation.26 | convolution fusion | flops 1075838976 | bytes 6815744 | tf_op jit(solution)/shard_map/rcab,rak->cbk/dot_general | solution.py:37
  30.7 5.2 %collective-permute-start = (bf16[16,128,256]{2,1,0:T(8,128)(2,1)}, bf16[16,128,256]{2,1,0:T(8,128)(2,1)S(1)}, u32[]{:S(2)}, u32[]{:S(2)}) collective-permute-start(bf16[16,128,256]{2,1,0:T(8,128)(2,1)} %fusion.11), channel_id=1, source_target_pairs={{0,248},{8,0},{16,8},{24,16},{32,24},{40,32},{48,40},{56,48},{64,5... | collective-permute-start | bytes 3145736 | tf_op jit(solution)/shard_map/ppermute | solution.py:14
  36.0 2.0 gather_fusion.2
  38.0 0.6 iota_compare_fusion.1
  38.7 10.0 %collective-permute-done = bf16[16,128,256]{2,1,0:T(8,128)(2,1)S(1)} collective-permute-done((bf16[16,128,256]{2,1,0:T(8,128)(2,1)}, bf16[16,128,256]{2,1,0:T(8,128)(2,1)S(1)}, u32[]{:S(2)}, u32[]{:S(2)}) %collective-permute-start) | collective-permute-done | bytes 1048608 | tf_op jit(solution)/shard_map/ppermute | solution.py:14
  48.6 2.0 gather_fusion.3
  50.7 4.3 %fusion.3 = bf16[32,128,128]{2,1,0:T(8,128)(2,1)} fusion(bf16[32,128,256]{2,1,0:T(8,128)(2,1)} %gather_fusion.3, pred[32]{0:T(512)(128)(4,1)S(1)} %get-tuple-element.12, bf16[32,128,256]{2,1,0:T(8,128)(2,1)} %gather_fusion.2, pred[32]{0:T(512)(128)(4,1)S(1)} %get-tuple-element.19, bf16[3,32,128,128]{3,2,1,0:T(8,128)(2,1)} %param.11, ...), kind=kOutput, calls=%fused_computation.14 | convolution fusion | flops 273154048 | bytes 6291552 | tf_op jit(solution)/shard_map/tak,tbk->tab/dot_general | solution.py:27
  55.0 3.0 %broadcast.375.clone.1 = bf16[8,16,128,128]{3,2,1,0:T(8,128)(2,1)} broadcast(bf16[]{:T(256)} %constant.94.clone.1), dimensions={} | broadcast | bytes 4194306 | tf_op jit(solution)/shard_map/broadcast.18
  58.0 5.7 %scatter_fusion.1 = bf16[8,16,128,128]{3,2,1,0:T(8,128)(2,1)} fusion(bf16[8,16,128,128]{3,2,1,0:T(8,128)(2,1)} %broadcast.375.clone.1, s32[32]{0:T(128)S(1)} %get-tuple-element.27, bf16[32,128,128]{2,1,0:T(8,128)(2,1)} %fusion.3), kind=kCustom, calls=%fused_computation.7 | custom fusion | bytes 3145984 | tf_op jit(solution)/shard_map/scatter | solution.py:35
  63.7 4.5 %fusion.9 = bf16[16,128,256]{2,1,0:T(8,128)(2,1)} fusion(bf16[16,128,256]{2,1,0:T(8,128)(2,1)S(1)} %collective-permute-done, bf16[8,16,128,128]{3,2,1,0:T(8,128)(2,1)} %scatter_fusion.1, bf16[8,128,256,1]{2,1,3,0:T(8,128)(2,1)S(1)} %bitcast.176), kind=kOutput, calls=%fused_computation.23 | convolution fusion | flops 1075838976 | bytes 6815744 | tf_op jit(solution)/shard_map/rcab,rak->cbk/dot_general | solution.py:37
  68.1 5.5 %collective-permute-start.1 = (bf16[16,128,256]{2,1,0:T(8,128)(2,1)}, bf16[16,128,256]{2,1,0:T(8,128)(2,1)}, u32[]{:S(2)}, u32[]{:S(2)}) collective-permute-start(bf16[16,128,256]{2,1,0:T(8,128)(2,1)} %fusion.9), channel_id=1, source_target_pairs={{0,248},{8,0},{16,8},{24,16},{32,24},{40,32},{48,40},{56,48},{64,5... | collective-permute-start | bytes 3145736 | tf_op jit(solution)/shard_map/ppermute | solution.py:14
  73.6 2.0 gather_fusion.4
  75.7 0.6 iota_compare_fusion
  76.3 4.4 %convolution_bitcast_fusion.2 = f32[8,128,256]{2,1,0:T(8,128)} fusion(bf16[8,16,128,128]{3,2,1,0:T(8,128)(2,1)} %scatter_fusion, bf16[16,128,256,1]{2,1,0,3:T(8,128)(2,1)S(1)} %bitcast.180), kind=kOutput, calls=%fused_computation.44 | convolution fusion | flops 1073741824 | bytes 6291456 | tf_op jit(solution)/shard_map/rcab,cbk->rak/dot_general | solution.py:41
  80.8 5.5 %collective-permute-done.1 = bf16[16,128,256]{2,1,0:T(8,128)(2,1)} collective-permute-done((bf16[16,128,256]{2,1,0:T(8,128)(2,1)}, bf16[16,128,256]{2,1,0:T(8,128)(2,1)}, u32[]{:S(2)}, u32[]{:S(2)}) %collective-permute-start.1) | collective-permute-done | bytes 1048608 | tf_op jit(solution)/shard_map/ppermute | solution.py:14
  86.2 3.2 %gather_fusion.5 = bf16[32,128,256]{2,1,0:T(8,128)(2,1)} fusion(bf16[16,128,256]{2,1,0:T(8,128)(2,1)} %collective-permute-done.1, s32[1024]{0:T(1024)S(1)} %pad_clamp_fusion), kind=kCustom, calls=%fused_computation.5.clone | custom fusion | bytes 4194432 | tf_op jit(solution)/shard_map/jit(_take)/gather | solution.py:25
  89.5 3.3 %fusion.1 = bf16[32,128,128]{2,1,0:T(8,128)(2,1)S(1)} fusion(bf16[32,128,256]{2,1,0:T(8,128)(2,1)} %gather_fusion.5, pred[32]{0:T(512)(128)(4,1)S(1)} %get-tuple-element.7, bf16[32,128,256]{2,1,0:T(8,128)(2,1)} %gather_fusion.4, pred[32]{0:T(512)(128)(4,1)S(1)} %get-tuple-element.4, bf16[3,32,128,128]{3,2,1,0:T(8,128)(2,1)} %param.11, ...), kind=kOutput, calls=%fused_computation.11 | convolution fusion | flops 273154048 | bytes 6291552 | tf_op jit(solution)/shard_map/tak,tbk->tab/dot_general | solution.py:27
  92.8 3.0 %broadcast.375 = bf16[8,16,128,128]{3,2,1,0:T(8,128)(2,1)} broadcast(bf16[]{:T(256)} %constant.94.clone.1), dimensions={} | broadcast | bytes 4194306 | tf_op jit(solution)/shard_map/broadcast.18
  95.8 5.0 %scatter_fusion.2 = bf16[8,16,128,128]{3,2,1,0:T(8,128)(2,1)} fusion(bf16[8,16,128,128]{3,2,1,0:T(8,128)(2,1)} %broadcast.375, s32[32]{0:T(128)S(1)} %get-tuple-element.25, bf16[32,128,128]{2,1,0:T(8,128)(2,1)S(1)} %fusion.1), kind=kCustom, calls=%fused_computation.8 | custom fusion | bytes 3145984 | tf_op jit(solution)/shard_map/scatter | solution.py:35
  100.9 0.0 copy-start.1
  100.9 4.9 %fusion.7 = bf16[16,128,256]{2,1,0:T(8,128)(2,1)} fusion(bf16[16,128,256]{2,1,0:T(8,128)(2,1)} %collective-permute-done.1, bf16[8,16,128,128]{3,2,1,0:T(8,128)(2,1)} %scatter_fusion.2, bf16[8,128,256,1]{2,1,3,0:T(8,128)(2,1)S(1)} %bitcast.177), kind=kOutput, calls=%fused_computation.20 | convolution fusion | flops 1075838976 | bytes 6815744 | tf_op jit(solution)/shard_map/rcab,rak->cbk/dot_general | solution.py:37
  105.8 0.0 copy-start.2
  105.8 0.0 copy-start.4
  105.8 0.0 collective-permute-start.2
  105.8 0.0 copy-done.1
  105.8 2.6 %convolution_bitcast_fusion = f32[8,128,256]{2,1,0:T(8,128)S(1)} fusion(bf16[8,16,128,128]{3,2,1,0:T(8,128)(2,1)S(1)} %copy-done.1, bf16[16,128,256]{2,1,0:T(8,128)(2,1)} %collective-permute-done.1), kind=kOutput, calls=%fused_computation.42 | convolution fusion | flops 1073741824 | bytes 6291456 | tf_op jit(solution)/shard_map/rcab,cbk->rak/dot_general | solution.py:41
  108.4 0.0 copy-done.2
  108.4 0.1 copy-done.4
  108.6 2.1 fusion.30
  110.7 0.0 all-reduce.2.cloned.1.call-update
  110.7 87.0 %all-reduce.2.cloned.1.call-done = bf16[1024,256]{1,0:T(8,128)(2,1)} async-done(((bf16[1024,256]{1,0:T(8,128)(2,1)}), bf16[1024,256]{1,0:T(8,128)(2,1)}) %all-reduce.2.cloned.1.call-update) | async-done | bytes 524304 | tf_op jit(solution)/shard_map/psum | solution.py:71
  197.7 1.5 dynamic-slice_convert_fusion
  199.2 0.0 collective-permute-done.2
  199.2 1.0 copy.22
  (9 shorter events, 0.1 us)
Async XLA Ops:
  7.2 3.7 %copy-start = (bf16[1024,256]{1,0:T(8,128)(2,1)S(1)}, bf16[1024,256]{1,0:T(8,128)(2,1)}, u32[]{:S(2)}) copy-start(bf16[1024,256]{1,0:T(8,128)(2,1)} %param.9) | copy-start | bytes 1572868
  7.2 190.5 %all-reduce.2.cloned.1.call-start = ((), (), s32[]{:S(2)}) async-start(), calls=%async_computation | async-start | bytes 1048576 | tf_op jit(solution)/shard_map/psum | solution.py:71
  10.9 2.0 copy-start.3
  30.7 17.9 %collective-permute-start = (bf16[16,128,256]{2,1,0:T(8,128)(2,1)}, bf16[16,128,256]{2,1,0:T(8,128)(2,1)S(1)}, u32[]{:S(2)}, u32[]{:S(2)}) collective-permute-start(bf16[16,128,256]{2,1,0:T(8,128)(2,1)} %fusion.11), channel_id=1, source_target_pairs={{0,248},{8,0},{16,8},{24,16},{32,24},{40,32},{48,40},{56,48},{64,5... | collective-permute-start | bytes 3145736 | tf_op jit(solution)/shard_map/ppermute | solution.py:14
  68.1 18.1 %collective-permute-start.1 = (bf16[16,128,256]{2,1,0:T(8,128)(2,1)}, bf16[16,128,256]{2,1,0:T(8,128)(2,1)}, u32[]{:S(2)}, u32[]{:S(2)}) collective-permute-start(bf16[16,128,256]{2,1,0:T(8,128)(2,1)} %fusion.9), channel_id=1, source_target_pairs={{0,248},{8,0},{16,8},{24,16},{32,24},{40,32},{48,40},{56,48},{64,5... | collective-permute-start | bytes 3145736 | tf_op jit(solution)/shard_map/ppermute | solution.py:14
  100.9 4.9 %copy-start.1 = (bf16[8,16,128,128]{3,2,1,0:T(8,128)(2,1)S(1)}, bf16[8,16,128,128]{3,2,1,0:T(8,128)(2,1)}, u32[]{:S(2)}) copy-start(bf16[8,16,128,128]{3,2,1,0:T(8,128)(2,1)} %scatter_fusion.2) | copy-start | bytes 12582916
  105.8 2.7 %copy-start.2 = (bf16[8,16,128,128]{3,2,1,0:T(8,128)(2,1)S(1)}, bf16[8,16,128,128]{3,2,1,0:T(8,128)(2,1)}, u32[]{:S(2)}) copy-start(bf16[8,16,128,128]{3,2,1,0:T(8,128)(2,1)} %scatter_fusion.1) | copy-start | bytes 12582916
  105.8 2.8 %copy-start.4 = (f32[8,128,256]{2,1,0:T(8,128)S(1)}, f32[8,128,256]{2,1,0:T(8,128)}, u32[]{:S(2)}) copy-start(f32[8,128,256]{2,1,0:T(8,128)} %convolution_bitcast_fusion.2) | copy-start | bytes 3145732
  105.8 93.4 %collective-permute-start.2 = (bf16[16,128,256]{2,1,0:T(8,128)(2,1)}, bf16[16,128,256]{2,1,0:T(8,128)(2,1)S(1)}, u32[]{:S(2)}, u32[]{:S(2)}) collective-permute-start(bf16[16,128,256]{2,1,0:T(8,128)(2,1)} %fusion.7), channel_id=1, source_target_pairs={{0,16},{8,24},{16,32},{24,40},{32,48},{40,56},{48,64},{56,72},{64,... | collective-permute-start | bytes 3145736 | tf_op jit(solution)/shard_map/ppermute | solution.py:14
Sparse Core Ops, SparseCore 0:
  110.8 86.8 all-reduce.1
where the time goes:
time: 208 us; the launch traced here: 207 us
  waiting for transfers between devices  102 us (49%)
  local copies, waits for them, and re-layouts  40.5 us (19%)
  matrix products  34 us (16%)
  between operations  14.2 us (7%)
  starting transfers between devices  10.8 us (5%)
  other arithmetic  5.11 us (2%)
    psum x1, waiting for transfers between devices, per_device(): lax.psum(local_sum.astype(jnp.bfloat16), 'chrom').astype(jnp.float32)  87 us
    scatter x3, local copies, waits for them, and re-layouts, stratum_update(): dense_resid = dense_resid.at[cell_rows, peak_cols].set(residual)  15.7 us
    ppermute x3, waiting for transfers between devices, passed_along(): lax.ppermute(value, axis, [(i, (i + by) % count) for i in range(count)])  15.4 us
    dot_general x3, matrix products, stratum_update(): jnp.einsum('rcab,rak->cbk', dense_resid, cell_blocks, preferred_element_t...  13.8 us
    dot_general x3, matrix products, stratum_update(): jnp.einsum('tak,tbk->tab', left_tiles, right_tiles, preferred_element_typ...  11 us
    ppermute x3, starting transfers between devices, passed_along(): lax.ppermute(value, axis, [(i, (i + by) % count) for i in range(count)])  10.7 us
    dot_general x3, matrix products, stratum_update(): jnp.einsum('rcab,cbk->rak', dense_resid, peak_block, preferred_element_ty...  9.12 us
    another operation x3, local copies, waits for them, and re-layouts  8.99 us
  transfers between devices with their start and end apart: 4, of which 3 were waited for; matrix products, arithmetic and copies ran while one was open for 8% of the time, Pallas kernels for 0%

commit v1 on v0

v1 whole, which is shorter than its diff:
```python
import math

import jax
import jax.numpy as jnp
from jax import lax
from jax.experimental import pallas as pl
from jax.experimental.pallas import tpu as pltpu
from jax.sharding import PartitionSpec as P

learning_rate = 0.15
gradient_scale = 0.1


def passed_along(value, axis, by):
    count = lax.axis_size(axis)
    return lax.ppermute(value, axis, [(i, (i + by) % count) for i in range(count)])


def stratum_kernel(scaling, first, count_ref, index_ref, cell_ref, peak_ref, values_ref, *refs):
    if first:
        new_ref, grad_ref, peak_grad = refs
    else:
        old_ref, new_ref, grad_ref, peak_grad = refs
    peak_tiles = peak_ref.shape[0]
    peak_grad[...] = jnp.zeros_like(peak_grad)
    grad_ref[...] = jnp.zeros_like(grad_ref) if first else old_ref[...]
    unroll = 4

    def group(g, carry):
        for k in range(unroll):
            t = g * unroll + k
            place = index_ref[0, t]
            row = place // peak_tiles
            col = place % peak_tiles
            left = cell_ref[row]
            right = peak_ref[col]
            predicted = lax.dot_general(
                left, right, (((1,), (1,)), ((), ())), preferred_element_type=jnp.float32
            )
            resid = (predicted * scaling - values_ref[0, t].astype(jnp.float32)).astype(jnp.bfloat16)
            peak_grad[col] += lax.dot_general(
                resid, left, (((0,), (0,)), ((), ())), preferred_element_type=jnp.float32
            )
            grad_ref[row] += lax.dot_general(
                resid, right, (((1,), (0,)), ((), ())), preferred_element_type=jnp.float32
            )
        return carry

    lax.fori_loop(0, count_ref[0, 0] // unroll, group, 0)
    for c in range(peak_tiles):
        new_ref[c] = (
            peak_ref[c].astype(jnp.float32) - learning_rate * (peak_grad[c] * scaling)
        ).astype(new_ref.dtype)


def stratum_update(cell_blocks, peak_block, values, index, counts, grad, stratum):
    row_tiles, tile_size, rank_width = cell_blocks.shape
    slots = values.shape[1]
    scaling = 1.0 / math.sqrt(rank_width)
    first = grad is None
    smem = pl.BlockSpec(memory_space=pltpu.SMEM)
    vmem = pl.BlockSpec(memory_space=pltpu.VMEM)
    in_specs = [
        smem,
        smem,
        vmem,
        vmem,
        pl.BlockSpec((1,) + values.shape[1:], lambda i: (stratum, 0, 0, 0)),
    ]
    args = [counts[stratum : stratum + 1], index[stratum : stratum + 1], cell_blocks, peak_block, values]
    if not first:
        in_specs.append(vmem)
        args.append(grad)
    flops = 6 * slots * tile_size * tile_size * rank_width
    return pl.pallas_call(
        lambda *refs: stratum_kernel(scaling, first, *refs),
        grid=(1,),
        out_shape=(
            jax.ShapeDtypeStruct(peak_block.shape, peak_block.dtype),
            jax.ShapeDtypeStruct(cell_blocks.shape, jnp.float32),
        ),
        in_specs=in_specs,
        out_specs=(vmem, vmem),
        scratch_shapes=[pltpu.VMEM(peak_block.shape, jnp.float32)],
        compiler_params=pltpu.CompilerParams(vmem_limit_bytes=24 * 1024 * 1024),
        cost_estimate=pl.CostEstimate(flops=flops, bytes_accessed=4 << 20, transcendentals=0),
    )(*args)


def per_device(cell_factors, peak_factors, tile_values, tile_index, tile_counts):
    cell_dev, rank_width = cell_factors.shape
    tile_size = tile_values.shape[-1]
    strata = tile_values.shape[0]
    block_rows = peak_factors.shape[0]
    row_tiles = cell_dev // tile_size
    peak_tiles = block_rows // tile_size
    chroms = lax.axis_size("chrom")
    share_rows = cell_dev // chroms
    cell_blocks = cell_factors.reshape(row_tiles, tile_size, rank_width)
    peak_block = peak_factors.reshape(peak_tiles, tile_size, rank_width)
    grad = None
    for stratum in range(strata):
        if stratum > 0:
            peak_block = passed_along(peak_block, "cell", -1)
        peak_block, grad = stratum_update(
            cell_blocks, peak_block, tile_values, tile_index, tile_counts, grad, stratum
        )
    peak_block = passed_along(peak_block, "cell", strata - 1)
    scale = gradient_scale / math.sqrt(rank_width)
    local_sum = (grad.reshape(cell_dev, rank_width) * scale).astype(jnp.bfloat16)
    shares = lax.all_to_all(local_sum, "chrom", 0, 0, tiled=True)
    summed = jnp.sum(shares.reshape(chroms, share_rows, rank_width).astype(jnp.float32), axis=0)
    return (peak_block.reshape(block_rows, rank_width), summed)


def solution(mesh):
    in_specs = (
        P("cell", None),
        P(("cell", "chrom"), None),
        P("cell", "chrom", None, None),
        P("cell", "chrom"),
        P("cell", "chrom"),
    )
    out_specs = (P(("cell", "chrom"), None), P(("cell", "chrom"), None))
    return jax.shard_map(
        per_device, mesh=mesh, in_specs=in_specs, out_specs=out_specs, check_vma=False
    )
```

time: 208 us -> 101 us (0.49)
  the two profiles are of different devices: /device:TPU:4 before, /device:TPU:1 now
where the time goes in v1:
time: 101 us
  blocking collectives  38.7 us (38%)
  waiting for transfers between devices  31.9 us (32%)
  Pallas kernels  17.9 us (18%)
  local copies, waits for them, and re-layouts  7.33 us (7%)
  starting transfers between devices  3.48 us (3%)
    all_to_all x1, blocking collectives, per_device(): shares = lax.all_to_all(local_sum, 'chrom', 0, 0, tiled=True)  38.7 us
    ppermute x3, waiting for transfers between devices, passed_along(): lax.ppermute(value, axis, [(i, (i + by) % count) for i in range(count)])  31.9 us
    pallas_call x3, Pallas kernels, stratum_update(): pl.pallas_call(lambda *refs: stratum_kernel(scaling, first, *refs), grid=...  17.9 us
    unnamed x9, local copies, waits for them, and re-layouts  5.13 us
    ppermute x3, starting transfers between devices, passed_along(): lax.ppermute(value, axis, [(i, (i + by) % count) for i in range(count)])  3.48 us
  transfers between devices with their start and end apart: 3, of which 2 were waited for; matrix products, arithmetic and copies ran while one was open for 1% of the time, Pallas kernels for 0%

profile of v1, /device:TPU:1, one launch (start us, length us, event | category | flops | bytes accessed | tf_op | source)
XLA Modules:
  0.0 100.8 jit_solution(4825738808197382746)
XLA Ops:
  0.6 0.8 fusion
  1.4 1.4 %fusion.1 = (s32[1,1]{0,1:T(1,128)}, s32[1,1]{0,1:T(1,128)}, s32[1,1]{0,1:T(1,128)}) fusion(s32[3,1]{0,1:T(1,128)} %param.9), kind=kLoop, calls=%fused_computation.3 | loop fusion | bytes 24 | tf_op jit(solution)/shard_map/slice | solution.py:70
  2.8 0.0 copy-start
  2.8 1.9 %copy-done = bf16[3,32,128,128]{3,2,1,0:T(8,128)(2,1)S(1)} copy-done((bf16[3,32,128,128]{3,2,1,0:T(8,128)(2,1)S(1)}, bf16[3,32,128,128]{3,2,1,0:T(8,128)(2,1)}, u32[]{:S(2)}) %copy-start) | copy-done | bytes 3145752
  4.7 0.0 copy-start.2
  4.7 1.0 %copy-done.2 = bf16[1024,256]{1,0:T(8,128)(2,1)S(1)} copy-done((bf16[1024,256]{1,0:T(8,128)(2,1)S(1)}, bf16[1024,256]{1,0:T(8,128)(2,1)}, u32[]{:S(2)}) %copy-start.2) | copy-done | bytes 524312
  5.8 0.0 copy-start.3
  5.8 1.2 %copy-done.3 = bf16[2048,256]{1,0:T(8,128)(2,1)S(1)} copy-done((bf16[2048,256]{1,0:T(8,128)(2,1)S(1)}, bf16[2048,256]{1,0:T(8,128)(2,1)}, u32[]{:S(2)}) %copy-start.3) | copy-done | bytes 1048600
  7.0 0.0 copy-start.1
  7.0 3.7 %shard_map.68 = (bf16[16,128,256]{2,1,0:T(8,128)(2,1)S(1)}, f32[8,128,256]{2,1,0:T(8,128)S(1)}) custom-call(s32[1,1]{1,0:T(1,128)} %bitcast.5.refs_0_, s32[1,32]{1,0:T(1,128)S(1)} %get-tuple-element.14.refs_1_, bf16[8,128,256]{2,1,0:T(8,128)(2,1)S(1)} %bitcast.6, bf16[16,128,256]{2,1,0:T(8,128)(2,1)S(1)} %bitcast.9, bf16[3,32,128,128]{3,2,1,0:T(8,128)(2,1)S(1)} %copy-done), custom_call_target="tpu_custom_call" | custom-call | flops 805306368 | bytes 4194304 | tf_op jit(solution)/shard_map/pallas_call | solution.py:75
  10.7 3.3 %collective-permute-start = (bf16[16,128,256]{2,1,0:T(8,128)(2,1)S(1)}, bf16[16,128,256]{2,1,0:T(8,128)(2,1)S(1)}, u32[]{:S(2)}, u32[]{:S(2)}) collective-permute-start(bf16[16,128,256]{2,1,0:T(8,128)(2,1)S(1)} %get-tuple-element.8), channel_id=1, source_target_pairs={{0,248},{8,0},{16,8},{24,16},{32,24},{40,32},{48,40},{56,48},{64,5... | collective-permute-start | bytes 3145736 | tf_op jit(solution)/shard_map/ppermute | solution.py:16
  14.0 17.7 %collective-permute-done.refs_3_ = bf16[16,128,256]{2,1,0:T(8,128)(2,1)S(1)} collective-permute-done((bf16[16,128,256]{2,1,0:T(8,128)(2,1)S(1)}, bf16[16,128,256]{2,1,0:T(8,128)(2,1)S(1)}, u32[]{:S(2)}, u32[]{:S(2)}) %collective-permute-start) | collective-permute-done | bytes 1048608 | tf_op jit(solution)/shard_map/ppermute | solution.py:16
  31.6 0.0 copy-done.1
  31.6 5.3 %shard_map.69 = (bf16[16,128,256]{2,1,0:T(8,128)(2,1)S(1)}, f32[8,128,256]{2,1,0:T(8,128)S(1)}) custom-call(s32[1,1]{1,0:T(1,128)} %bitcast.4.refs_0_, s32[1,32]{1,0:T(1,128)S(1)} %get-tuple-element.16.refs_1_, bf16[8,128,256]{2,1,0:T(8,128)(2,1)S(1)} %bitcast.7, bf16[16,128,256]{2,1,0:T(8,128)(2,1)S(1)} %collective-permute-done.refs_3_, ...), custom_call_target="tpu_custom_call" | custom-call | flops 805306368 | bytes 4194304 | tf_op jit(solution)/shard_map/pallas_call | solution.py:75
  37.0 0.1 collective-permute-start.1
  37.1 14.2 %collective-permute-done.1.refs_3_ = bf16[16,128,256]{2,1,0:T(8,128)(2,1)S(1)} collective-permute-done((bf16[16,128,256]{2,1,0:T(8,128)(2,1)S(1)}, bf16[16,128,256]{2,1,0:T(8,128)(2,1)S(1)}, u32[]{:S(2)}, u32[]{:S(2)}) %collective-permute-start.1) | collective-permute-done | bytes 1048608 | tf_op jit(solution)/shard_map/ppermute | solution.py:16
  51.3 8.9 %shard_map.70 = (bf16[16,128,256]{2,1,0:T(8,128)(2,1)S(1)}, f32[8,128,256]{2,1,0:T(8,128)S(1)}) custom-call(s32[1,1]{1,0:T(1,128)} %bitcast.3.refs_0_, s32[1,32]{1,0:T(1,128)S(1)} %get-tuple-element.15.refs_1_, bf16[8,128,256]{2,1,0:T(8,128)(2,1)S(1)} %bitcast.8, bf16[16,128,256]{2,1,0:T(8,128)(2,1)S(1)} %collective-permute-done.1.refs_3_, ...), custom_call_target="tpu_custom_call" | custom-call | flops 805306368 | bytes 4194304 | tf_op jit(solution)/shard_map/pallas_call | solution.py:75
  60.2 0.1 collective-permute-start.2
  60.3 0.1 multiply_convert_fusion
  60.4 38.7 %all_to_all.6 = bf16[8,128,256]{2,1,0:T(8,128)(2,1)S(1)} all-to-all(bf16[8,128,256]{2,1,0:T(8,128)(2,1)S(1)} %multiply_convert_fusion), channel_id=1, replica_groups=mesh['cell'=32,'chrom'=8] {'chrom'}, dimensions={0} | all-to-all | bytes 1048576 | tf_op jit(solution)/shard_map/all_to_all | solution.py:111
  99.1 0.7 convert_reduce_fusion
  99.8 0.0 collective-permute-done.2
  99.8 1.0 copy.14
Async XLA Ops:
  2.8 1.9 %copy-start = (bf16[3,32,128,128]{3,2,1,0:T(8,128)(2,1)S(1)}, bf16[3,32,128,128]{3,2,1,0:T(8,128)(2,1)}, u32[]{:S(2)}) copy-start(bf16[3,32,128,128]{3,2,1,0:T(8,128)(2,1)} %refs_4_.5) | copy-start | bytes 9437188
  4.7 1.0 %copy-start.2 = (bf16[1024,256]{1,0:T(8,128)(2,1)S(1)}, bf16[1024,256]{1,0:T(8,128)(2,1)}, u32[]{:S(2)}) copy-start(bf16[1024,256]{1,0:T(8,128)(2,1)} %param.5) | copy-start | bytes 1572868
  5.8 1.2 %copy-start.3 = (bf16[2048,256]{1,0:T(8,128)(2,1)S(1)}, bf16[2048,256]{1,0:T(8,128)(2,1)}, u32[]{:S(2)}) copy-start(bf16[2048,256]{1,0:T(8,128)(2,1)} %param.6) | copy-start | bytes 3145732
  7.0 24.7 %copy-start.1 = (bf16[3,32,128,128]{3,2,1,0:T(8,128)(2,1)S(1)}, bf16[3,32,128,128]{3,2,1,0:T(8,128)(2,1)}, u32[]{:S(2)}) copy-start(bf16[3,32,128,128]{3,2,1,0:T(8,128)(2,1)} %refs_4_.5) | copy-start | bytes 9437188
  10.7 21.0 %collective-permute-start = (bf16[16,128,256]{2,1,0:T(8,128)(2,1)S(1)}, bf16[16,128,256]{2,1,0:T(8,128)(2,1)S(1)}, u32[]{:S(2)}, u32[]{:S(2)}) collective-permute-start(bf16[16,128,256]{2,1,0:T(8,128)(2,1)S(1)} %get-tuple-element.8), channel_id=1, source_target_pairs={{0,248},{8,0},{16,8},{24,16},{32,24},{40,32},{48,40},{56,48},{64,5... | collective-permute-start | bytes 3145736 | tf_op jit(solution)/shard_map/ppermute | solution.py:16
  37.0 14.3 %collective-permute-start.1 = (bf16[16,128,256]{2,1,0:T(8,128)(2,1)S(1)}, bf16[16,128,256]{2,1,0:T(8,128)(2,1)S(1)}, u32[]{:S(2)}, u32[]{:S(2)}) collective-permute-start(bf16[16,128,256]{2,1,0:T(8,128)(2,1)S(1)} %get-tuple-element.10), channel_id=1, source_target_pairs={{0,248},{8,0},{16,8},{24,16},{32,24},{40,32},{48,40},{56,48},{64,5... | collective-permute-start | bytes 3145736 | tf_op jit(solution)/shard_map/ppermute | solution.py:16
  60.2 39.7 %collective-permute-start.2 = (bf16[16,128,256]{2,1,0:T(8,128)(2,1)S(1)}, bf16[16,128,256]{2,1,0:T(8,128)(2,1)S(1)}, u32[]{:S(2)}, u32[]{:S(2)}) collective-permute-start(bf16[16,128,256]{2,1,0:T(8,128)(2,1)S(1)} %get-tuple-element.12), channel_id=1, source_target_pairs={{0,16},{8,24},{16,32},{24,40},{32,48},{40,56},{48,64},{56,72},{64,... | collective-permute-start | bytes 3145736 | tf_op jit(solution)/shard_map/ppermute | solution.py:16

commit v2 on v1

v2 whole, which is shorter than its diff:
```python
import functools
import math

import jax
import jax.numpy as jnp
from jax import lax
from jax.experimental import pallas as pl
from jax.experimental.pallas import tpu as pltpu
from jax.sharding import PartitionSpec as P

learning_rate = 0.15
gradient_scale = 0.1
parts = 2
group_size = 8


def passed_along(value, axis, by):
    count = lax.axis_size(axis)
    return lax.ppermute(value, axis, [(i, (i + by) % count) for i in range(count)])


def contract(left, right, dims):
    return lax.dot_general(left, right, ((dims[:1], dims[1:]), ((), ())), preferred_element_type=jnp.float32)


def part_kernel(scaling, stratum, part, peak_tiles, load, fresh, *refs):
    count_ref, index_ref, cell_in, peak_in, values_in = refs[:5]
    rest = refs[5:] if fresh else refs[6:]
    new_ref, grad_ref, peak_grad, places = rest[:4]
    own_tiles = peak_tiles // parts
    row_tiles = grad_ref.shape[0] - 1
    live = count_ref[0, stratum]
    slots = index_ref.shape[1]
    if load:
        cell_ref, peak_ref, values_ref, sems = rest[4:]
        copies = [
            pltpu.make_async_copy(peak_in.at[pl.ds(part * own_tiles, own_tiles)], peak_ref, sems.at[0]),
            pltpu.make_async_copy(cell_in, cell_ref, sems.at[1]),
            pltpu.make_async_copy(values_in.at[stratum], values_ref, sems.at[2]),
        ]
        for copy in copies:
            copy.start()
    else:
        cell_ref, peak_ref = cell_in, peak_in
        values_ref = values_in.at[0]

    def note(t, found):
        place = index_ref[stratum, t]
        places[found] = place * slots + t
        mine = (place % peak_tiles) // own_tiles == part
        return found + jnp.where(mine, 1, 0)

    found = lax.fori_loop(0, live, note, 0)
    for k in range(group_size):
        places[found + k] = -1
    peak_grad[...] = jnp.zeros_like(peak_grad)
    grad_ref[...] = jnp.zeros_like(grad_ref) if fresh else refs[5][...]
    if load:
        for copy in copies:
            copy.wait()

    def group(g, carry):
        rows, cols, to_rows, to_cols, lefts, rights, resids = [], [], [], [], [], [], []
        for k in range(group_size):
            code = places[g * group_size + k]
            used = code >= 0
            code = jnp.maximum(code, 0)
            t = code % slots
            place = code // slots
            row = place // peak_tiles
            col = place % own_tiles
            left, right = cell_ref[row], peak_ref[col]
            predicted = contract(left, right, (1, 1))
            resids.append((predicted * scaling - values_ref[t].astype(jnp.float32)).astype(jnp.bfloat16))
            rows.append(row)
            cols.append(col)
            to_rows.append(jnp.where(used, row, row_tiles))
            to_cols.append(jnp.where(used, col, own_tiles))
        terms = [contract(resids[k], cell_ref[rows[k]], (0, 0)) for k in range(group_size)]
        for k in range(group_size):
            peak_grad[to_cols[k]] += terms[k]
        terms = [contract(resids[k], peak_ref[cols[k]], (1, 0)) for k in range(group_size)]
        for k in range(group_size):
            grad_ref[to_rows[k]] += terms[k]
        return carry

    lax.fori_loop(0, (found + group_size - 1) // group_size, group, 0)
    for c in range(own_tiles):
        new_ref[c] = (
            peak_ref[c].astype(jnp.float32) - learning_rate * (peak_grad[c] * scaling)
        ).astype(new_ref.dtype)


def part_update(counts, index, cell_blocks, peaks, values, grad, stratum, part, peak_tiles, load):
    row_tiles, tile_size, rank_width = cell_blocks.shape
    slots = values.shape[1]
    own_tiles = peak_tiles // parts
    fresh = grad is None
    smem = pl.BlockSpec(memory_space=pltpu.SMEM)
    vmem = pl.BlockSpec(memory_space=pltpu.VMEM)
    far = pl.BlockSpec(memory_space=pltpu.HBM)
    if load:
        in_specs = [smem, smem, far, far, far]
    else:
        own_values = pl.BlockSpec((1,) + values.shape[1:], lambda i: (stratum, 0, 0, 0))
        in_specs = [smem, smem, vmem, vmem, own_values]
    args = [counts, index, cell_blocks, peaks, values]
    if not fresh:
        in_specs.append(vmem)
        args.append(grad)
    scratch = [
        pltpu.VMEM((own_tiles + 1, tile_size, rank_width), jnp.float32),
        pltpu.SMEM((slots + group_size,), jnp.int32),
    ]
    if load:
        scratch += [
            pltpu.VMEM(cell_blocks.shape, cell_blocks.dtype),
            pltpu.VMEM((own_tiles, tile_size, rank_width), peaks.dtype),
            pltpu.VMEM(values.shape[1:], values.dtype),
            pltpu.SemaphoreType.DMA((3,)),
        ]
    flops = 6 * slots * tile_size * tile_size * rank_width // parts
    return pl.pallas_call(
        functools.partial(
            part_kernel, 1.0 / math.sqrt(rank_width), stratum, part, peak_tiles, load, fresh
        ),
        grid=(1,),
        out_shape=(
            jax.ShapeDtypeStruct((own_tiles, tile_size, rank_width), peaks.dtype),
            jax.ShapeDtypeStruct((row_tiles + 1, tile_size, rank_width), jnp.float32),
        ),
        in_specs=in_specs,
        out_specs=(vmem, vmem),
        scratch_shapes=scratch,
        compiler_params=pltpu.CompilerParams(vmem_limit_bytes=(60 if load else 12) * 1024 * 1024),
        cost_estimate=pl.CostEstimate(flops=flops, bytes_accessed=4 << 20, transcendentals=0),
    )(*args)


def per_device(cell_factors, peak_factors, tile_values, tile_index, tile_counts):
    cell_dev, rank_width = cell_factors.shape
    tile_size = tile_values.shape[-1]
    strata = tile_values.shape[0]
    block_rows = peak_factors.shape[0]
    row_tiles = cell_dev // tile_size
    peak_tiles = block_rows // tile_size
    chroms = lax.axis_size("chrom")
    share_rows = cell_dev // chroms
    cell_blocks = cell_factors.reshape(row_tiles, tile_size, rank_width)
    peak_block = peak_factors.reshape(peak_tiles, tile_size, rank_width)
    counts = tile_counts.T
    pieces = [peak_block] * parts
    grad = None
    for stratum in range(strata):
        for part in range(parts):
            piece, grad = part_update(
                counts, tile_index, cell_blocks, pieces[part], tile_values, grad,
                stratum, part, peak_tiles, stratum == 0,
            )
            by = -1 if stratum < strata - 1 else strata - 1
            pieces[part] = passed_along(piece, "cell", by)
    scale = gradient_scale / math.sqrt(rank_width)
    local_sum = (grad[:row_tiles].reshape(cell_dev, rank_width) * scale).astype(jnp.bfloat16)
    shares = lax.all_to_all(local_sum, "chrom", 0, 0, tiled=True)
    peak_out = jnp.concatenate(pieces, axis=0)
    peak_out, shares = lax.optimization_barrier((peak_out, shares))
    summed = jnp.sum(shares.reshape(chroms, share_rows, rank_width).astype(jnp.float32), axis=0)
    return (peak_out.reshape(block_rows, rank_width), summed)


def solution(mesh):
    in_specs = (
        P("cell", None),
        P(("cell", "chrom"), None),
        P("cell", "chrom", None, None),
        P("cell", "chrom"),
        P("cell", "chrom"),
    )
    out_specs = (P(("cell", "chrom"), None), P(("cell", "chrom"), None))
    return jax.shard_map(
        per_device, mesh=mesh, in_specs=in_specs, out_specs=out_specs, check_vma=False
    )
```

time: 101 us -> 77 us (0.76)
  blocking collectives: 38.7 us -> 0 us
  starting transfers between devices: 3.48 us -> 19.6 us
  local copies, waits for them, and re-layouts: 7.33 us -> 1.28 us
  Pallas kernels: 17.9 us -> 23.9 us
  waiting for transfers between devices: 31.9 us -> 27.8 us
  other arithmetic: 0.84 us -> 3.74 us
    all_to_all x1 -> x0, blocking collectives: 38.7 us -> none  [per_device(): shares = lax.all_to_all(local_sum, 'chrom', 0, 0, tiled=True)]
    ppermute x3 -> x6, starting transfers between devices: 3.48 us -> 16.1 us  [passed_along(): lax.ppermute(value, axis, [(i, (i + by) % count) for i in range(count)])]
    ppermute x3 -> x6, waiting for transfers between devices: 31.9 us -> 23.8 us  [passed_along(): lax.ppermute(value, axis, [(i, (i + by) % count) for i in range(count)])]
    pallas_call x3 -> x6, Pallas kernels: 17.9 us -> 23.9 us  [part_update(): pl.pallas_call(functools.partial(part_kernel, 1.0 / math.sqrt(rank_width)...]
    all_to_all x0 -> x1, waiting for transfers between devices: none -> 4.08 us  [per_device(): shares = lax.all_to_all(local_sum, 'chrom', 0, 0, tiled=True)]
    unnamed x9 -> x10, local copies, waits for them, and re-layouts: 5.13 us -> 1.28 us
    all_to_all x0 -> x1, starting transfers between devices: none -> 3.55 us  [per_device(): shares = lax.all_to_all(local_sum, 'chrom', 0, 0, tiled=True)]
    slice x2 -> x0, local copies, waits for them, and re-layouts: 2.2 us -> none  [the longest x1 1.4 us: stratum_update(): counts[stratum:stratum + 1]]
  transfers between devices with their start and end apart: 3 -> 7, of which waited for: 2 -> 4; matrix products, arithmetic and copies ran while one was open for 1% -> 4% of each run, Pallas kernels for 0% -> 26%
where the time goes in v2:
time: 77 us; the launch traced here: 77.2 us
  waiting for transfers between devices  27.8 us (36%)
  Pallas kernels  23.9 us (31%)
  starting transfers between devices  19.6 us (25%)
  other arithmetic  3.74 us (5%)
  local copies, waits for them, and re-layouts  1.28 us (2%)
    pallas_call x6, Pallas kernels, part_update(): pl.pallas_call(functools.partial(part_kernel, 1.0 / math.sqrt(rank_width)...  23.9 us
    ppermute x6, waiting for transfers between devices, passed_along(): lax.ppermute(value, axis, [(i, (i + by) % count) for i in range(count)])  23.8 us
    ppermute x6, starting transfers between devices, passed_along(): lax.ppermute(value, axis, [(i, (i + by) % count) for i in range(count)])  16.1 us
    all_to_all x1, waiting for transfers between devices, per_device(): shares = lax.all_to_all(local_sum, 'chrom', 0, 0, tiled=True)  4.08 us
    all_to_all x1, starting transfers between devices, per_device(): shares = lax.all_to_all(local_sum, 'chrom', 0, 0, tiled=True)  3.55 us
    concatenate x1, other arithmetic, per_device(): peak_out = jnp.concatenate(pieces, axis=0)  2.1 us
  transfers between devices with their start and end apart: 7, of which 4 were waited for; matrix products, arithmetic and copies ran while one was open for 4% of the time, Pallas kernels for 26%

profile of v2, /device:TPU:1, one launch (start us, length us, event | category | flops | bytes accessed | tf_op | source)
XLA Modules:
  0.0 77.2 jit_solution(4569709624915868716)
XLA Ops:
  0.6 4.1 %shard_map.68 = (bf16[8,128,256]{2,1,0:T(8,128)(2,1)}, f32[9,128,256]{2,1,0:T(8,128)}) custom-call(s32[1,3]{1,0:T(1,128)} %bitcast.13, s32[3,32]{1,0:T(4,128)} %refs_1_.11, bf16[8,128,256]{2,1,0:T(8,128)(2,1)} %bitcast.7, bf16[16,128,256]{2,1,0:T(8,128)(2,1)} %bitcast.19, bf16[3,32,128,128]{3,2,1,0:T(8,128)(2,1)} %refs_4_.11), custom_call_target="tpu_custom_call" | custom-call | flops 402653184 | bytes 4194304 | tf_op jit(solution)/shard_map/pallas_call | solution.py:123
  4.8 4.7 %collective-permute-start = (bf16[8,128,256]{2,1,0:T(8,128)(2,1)}, bf16[8,128,256]{2,1,0:T(8,128)(2,1)}, u32[]{:S(2)}, u32[]{:S(2)}) collective-permute-start(bf16[8,128,256]{2,1,0:T(8,128)(2,1)} %get-tuple-element.16), channel_id=1, source_target_pairs={{0,248},{8,0},{16,8},{24,16},{32,24},{40,32},{48,40},{56,48},{64,5... | collective-permute-start | bytes 1572872 | tf_op jit(solution)/shard_map/ppermute | solution.py:19
  9.4 0.0 copy-start
  9.4 0.0 copy-start.1
  9.4 0.0 copy-start.3
  9.4 0.0 copy-start.4
  9.5 4.9 %shard_map.69 = (bf16[8,128,256]{2,1,0:T(8,128)(2,1)}, f32[9,128,256]{2,1,0:T(8,128)}) custom-call(s32[1,3]{1,0:T(1,128)} %bitcast.14, s32[3,32]{1,0:T(4,128)} %refs_1_.11, bf16[8,128,256]{2,1,0:T(8,128)(2,1)} %bitcast.8, bf16[16,128,256]{2,1,0:T(8,128)(2,1)} %bitcast.20, bf16[3,32,128,128]{3,2,1,0:T(8,128)(2,1)} %refs_4_.11, ...), custom_call_target="tpu_custom_call" | custom-call | flops 402653184 | bytes 4194304 | tf_op jit(solution)/shard_map/pallas_call | solution.py:123
  14.4 6.1 %collective-permute-start.2 = (bf16[8,128,256]{2,1,0:T(8,128)(2,1)}, bf16[8,128,256]{2,1,0:T(8,128)(2,1)S(1)}, u32[]{:S(2)}, u32[]{:S(2)}) collective-permute-start(bf16[8,128,256]{2,1,0:T(8,128)(2,1)} %get-tuple-element.20), channel_id=1, source_target_pairs={{0,248},{8,0},{16,8},{24,16},{32,24},{40,32},{48,40},{56,48},{64,5... | collective-permute-start | bytes 1572872 | tf_op jit(solution)/shard_map/ppermute | solution.py:19
  20.5 0.0 collective-permute-done.refs_3_
  20.5 0.0 copy-done
  20.5 0.0 copy-done.1
  20.5 0.0 copy-done.3
  20.5 0.0 copy-done.4
  20.5 0.0 copy-start.2
  20.5 1.3 %copy-done.2 = f32[9,128,256]{2,1,0:T(8,128)S(1)} copy-done((f32[9,128,256]{2,1,0:T(8,128)S(1)}, f32[9,128,256]{2,1,0:T(8,128)}, u32[]{:S(2)}) %copy-start.2) | copy-done | bytes 1179672
  21.8 3.3 %shard_map.70 = (bf16[8,128,256]{2,1,0:T(8,128)(2,1)S(1)}, f32[9,128,256]{2,1,0:T(8,128)S(1)}) custom-call(s32[1,3]{1,0:T(1,128)S(1)} %bitcast.15, s32[3,32]{1,0:T(4,128)S(1)} %copy-done.3, bf16[8,128,256]{2,1,0:T(8,128)(2,1)S(1)} %bitcast.9, bf16[8,128,256]{2,1,0:T(8,128)(2,1)} %collective-permute-done.refs_3_, bf16[3,32,128,128]{3,2,1,0:T(8,128)(2,1)S(1)} %copy-done, ...), custom_call_target="tpu_custom_call" | custom-call | flops 402653184 | bytes 4194304 | tf_op jit(solution)/shard_map/pallas_call | solution.py:123
  25.1 1.1 %collective-permute-start.1 = (bf16[8,128,256]{2,1,0:T(8,128)(2,1)S(1)}, bf16[8,128,256]{2,1,0:T(8,128)(2,1)S(1)}, u32[]{:S(2)}, u32[]{:S(2)}) collective-permute-start(bf16[8,128,256]{2,1,0:T(8,128)(2,1)S(1)} %get-tuple-element.19), channel_id=1, source_target_pairs={{0,248},{8,0},{16,8},{24,16},{32,24},{40,32},{48,40},{56,48},{64,5... | collective-permute-start | bytes 1572872 | tf_op jit(solution)/shard_map/ppermute | solution.py:19
  26.2 0.0 collective-permute-done.2.refs_3_
  26.2 3.5 %shard_map.71 = (bf16[8,128,256]{2,1,0:T(8,128)(2,1)S(1)}, f32[9,128,256]{2,1,0:T(8,128)S(1)}) custom-call(s32[1,3]{1,0:T(1,128)S(1)} %bitcast.16, s32[3,32]{1,0:T(4,128)S(1)} %copy-done.3, bf16[8,128,256]{2,1,0:T(8,128)(2,1)S(1)} %bitcast.10, bf16[8,128,256]{2,1,0:T(8,128)(2,1)S(1)} %collective-permute-done.2.refs_3_, ...), custom_call_target="tpu_custom_call" | custom-call | flops 402653184 | bytes 4194304 | tf_op jit(solution)/shard_map/pallas_call | solution.py:123
  29.8 4.2 %collective-permute-start.4 = (bf16[8,128,256]{2,1,0:T(8,128)(2,1)S(1)}, bf16[8,128,256]{2,1,0:T(8,128)(2,1)S(1)}, u32[]{:S(2)}, u32[]{:S(2)}) collective-permute-start(bf16[8,128,256]{2,1,0:T(8,128)(2,1)S(1)} %get-tuple-element.24), channel_id=1, source_target_pairs={{0,248},{8,0},{16,8},{24,16},{32,24},{40,32},{48,40},{56,48},{64,5... | collective-permute-start | bytes 1572872 | tf_op jit(solution)/shard_map/ppermute | solution.py:19
  34.0 0.0 collective-permute-done.1.refs_3_
  34.0 3.6 %shard_map.72 = (bf16[8,128,256]{2,1,0:T(8,128)(2,1)}, f32[9,128,256]{2,1,0:T(8,128)S(1)}) custom-call(s32[1,3]{1,0:T(1,128)S(1)} %bitcast.17, s32[3,32]{1,0:T(4,128)S(1)} %copy-done.3, bf16[8,128,256]{2,1,0:T(8,128)(2,1)S(1)} %bitcast.11, bf16[8,128,256]{2,1,0:T(8,128)(2,1)S(1)} %collective-permute-done.1.refs_3_, bf16[3,32,128,128]{3,2,1,0:T(8,128)(2,1)S(1)} %copy-done, ...), custom_call_target="tpu_custom_call" | custom-call | flops 402653184 | bytes 4194304 | tf_op jit(solution)/shard_map/pallas_call | solution.py:123
  37.6 0.0 collective-permute-start.3
  37.6 1.8 %collective-permute-done.4.refs_3_ = bf16[8,128,256]{2,1,0:T(8,128)(2,1)S(1)} collective-permute-done((bf16[8,128,256]{2,1,0:T(8,128)(2,1)S(1)}, bf16[8,128,256]{2,1,0:T(8,128)(2,1)S(1)}, u32[]{:S(2)}, u32[]{:S(2)}) %collective-permute-start.4) | collective-permute-done | bytes 524320 | tf_op jit(solution)/shard_map/ppermute | solution.py:19
  39.4 4.4 %shard_map.73 = (bf16[8,128,256]{2,1,0:T(8,128)(2,1)}, f32[9,128,256]{2,1,0:T(8,128)S(1)}) custom-call(s32[1,3]{1,0:T(1,128)S(1)} %bitcast.18, s32[3,32]{1,0:T(4,128)S(1)} %copy-done.3, bf16[8,128,256]{2,1,0:T(8,128)(2,1)S(1)} %bitcast.12, bf16[8,128,256]{2,1,0:T(8,128)(2,1)S(1)} %collective-permute-done.4.refs_3_, bf16[3,32,128,128]{3,2,1,0:T(8,128)(2,1)S(1)} %copy-done, ...), custom_call_target="tpu_custom_call" | custom-call | flops 402653184 | bytes 4194304 | tf_op jit(solution)/shard_map/pallas_call | solution.py:123
  43.8 0.0 collective-permute-start.5
  43.8 0.9 %multiply_convert_fusion = bf16[8,128,256]{2,1,0:T(8,128)(2,1)} fusion(f32[9,128,256]{2,1,0:T(8,128)S(1)} %get-tuple-element.27), kind=kLoop, calls=%fused_computation.2 | loop fusion | flops 524288 | bytes 1572864 | tf_op jit(solution)/shard_map/convert_element_type | solution.py:163
  44.7 3.6 %all-to-all-start = ((bf16[8,128,256]{2,1,0:T(8,128)(2,1)}), bf16[8,128,256]{2,1,0:T(8,128)(2,1)S(1)}, u32[]{:S(2)}, u32[]{:S(2)}) async-start(bf16[8,128,256]{2,1,0:T(8,128)(2,1)} %multiply_convert_fusion), calls=%async_computation | async-start | bytes 1048576 | tf_op jit(solution)/shard_map/all_to_all | solution.py:164
  48.3 10.8 %collective-permute-done.3 = bf16[8,128,256]{2,1,0:T(8,128)(2,1)} collective-permute-done((bf16[8,128,256]{2,1,0:T(8,128)(2,1)}, bf16[8,128,256]{2,1,0:T(8,128)(2,1)}, u32[]{:S(2)}, u32[]{:S(2)}) %collective-permute-start.3) | collective-permute-done | bytes 524320 | tf_op jit(solution)/shard_map/ppermute | solution.py:19
  59.1 11.1 %collective-permute-done.5 = bf16[8,128,256]{2,1,0:T(8,128)(2,1)S(1)} collective-permute-done((bf16[8,128,256]{2,1,0:T(8,128)(2,1)}, bf16[8,128,256]{2,1,0:T(8,128)(2,1)S(1)}, u32[]{:S(2)}, u32[]{:S(2)}) %collective-permute-start.5) | collective-permute-done | bytes 524320 | tf_op jit(solution)/shard_map/ppermute | solution.py:19
  70.2 2.1 %pad_maximum_fusion = bf16[16,128,256]{2,1,0:T(8,128)(2,1)} fusion(bf16[8,128,256]{2,1,0:T(8,128)(2,1)S(1)} %collective-permute-done.5, bf16[8,128,256]{2,1,0:T(8,128)(2,1)} %collective-permute-done.3), kind=kLoop, calls=%fused_computation | loop fusion | flops 524288 | bytes 2097152 | tf_op jit(solution)/shard_map/concatenate | solution.py:165
  72.3 4.1 %all-to-all-done = bf16[8,128,256]{2,1,0:T(8,128)(2,1)S(1)} async-done(((bf16[8,128,256]{2,1,0:T(8,128)(2,1)}), bf16[8,128,256]{2,1,0:T(8,128)(2,1)S(1)}, u32[]{:S(2)}, u32[]{:S(2)}) %all-to-all-start) | async-done | bytes 524320 | tf_op jit(solution)/shard_map/all_to_all | solution.py:164
  76.4 0.7 convert_reduce_fusion
Async XLA Ops:
  4.8 15.7 %collective-permute-start = (bf16[8,128,256]{2,1,0:T(8,128)(2,1)}, bf16[8,128,256]{2,1,0:T(8,128)(2,1)}, u32[]{:S(2)}, u32[]{:S(2)}) collective-permute-start(bf16[8,128,256]{2,1,0:T(8,128)(2,1)} %get-tuple-element.16), channel_id=1, source_target_pairs={{0,248},{8,0},{16,8},{24,16},{32,24},{40,32},{48,40},{56,48},{64,5... | collective-permute-start | bytes 1572872 | tf_op jit(solution)/shard_map/ppermute | solution.py:19
  9.4 11.1 %copy-start = (bf16[3,32,128,128]{3,2,1,0:T(8,128)(2,1)S(1)}, bf16[3,32,128,128]{3,2,1,0:T(8,128)(2,1)}, u32[]{:S(2)}) copy-start(bf16[3,32,128,128]{3,2,1,0:T(8,128)(2,1)} %refs_4_.11) | copy-start | bytes 9437188
  9.4 11.1 %copy-start.1 = (bf16[1024,256]{1,0:T(8,128)(2,1)S(1)}, bf16[1024,256]{1,0:T(8,128)(2,1)}, u32[]{:S(2)}) copy-start(bf16[1024,256]{1,0:T(8,128)(2,1)} %param.5) | copy-start | bytes 1572868
  9.4 11.1 %copy-start.3 = (s32[3,32]{1,0:T(4,128)S(1)}, s32[3,32]{1,0:T(4,128)}, u32[]{:S(2)}) copy-start(s32[3,32]{1,0:T(4,128)} %refs_1_.11) | copy-start | bytes 1156
  9.4 11.1 %copy-start.4 = (s32[3,1]{0,1:T(1,128)S(1)}, s32[3,1]{0,1:T(1,128)}, u32[]{:S(2)}) copy-start(s32[3,1]{0,1:T(1,128)} %param.9) | copy-start | bytes 40
  14.4 11.8 %collective-permute-start.2 = (bf16[8,128,256]{2,1,0:T(8,128)(2,1)}, bf16[8,128,256]{2,1,0:T(8,128)(2,1)S(1)}, u32[]{:S(2)}, u32[]{:S(2)}) collective-permute-start(bf16[8,128,256]{2,1,0:T(8,128)(2,1)} %get-tuple-element.20), channel_id=1, source_target_pairs={{0,248},{8,0},{16,8},{24,16},{32,24},{40,32},{48,40},{56,48},{64,5... | collective-permute-start | bytes 1572872 | tf_op jit(solution)/shard_map/ppermute | solution.py:19
  20.5 1.3 %copy-start.2 = (f32[9,128,256]{2,1,0:T(8,128)S(1)}, f32[9,128,256]{2,1,0:T(8,128)}, u32[]{:S(2)}) copy-start(f32[9,128,256]{2,1,0:T(8,128)} %get-tuple-element.18.refs_5_) | copy-start | bytes 3538948
  25.1 8.9 %collective-permute-start.1 = (bf16[8,128,256]{2,1,0:T(8,128)(2,1)S(1)}, bf16[8,128,256]{2,1,0:T(8,128)(2,1)S(1)}, u32[]{:S(2)}, u32[]{:S(2)}) collective-permute-start(bf16[8,128,256]{2,1,0:T(8,128)(2,1)S(1)} %get-tuple-element.19), channel_id=1, source_target_pairs={{0,248},{8,0},{16,8},{24,16},{32,24},{40,32},{48,40},{56,48},{64,5... | collective-permute-start | bytes 1572872 | tf_op jit(solution)/shard_map/ppermute | solution.py:19
  29.8 9.7 %collective-permute-start.4 = (bf16[8,128,256]{2,1,0:T(8,128)(2,1)S(1)}, bf16[8,128,256]{2,1,0:T(8,128)(2,1)S(1)}, u32[]{:S(2)}, u32[]{:S(2)}) collective-permute-start(bf16[8,128,256]{2,1,0:T(8,128)(2,1)S(1)} %get-tuple-element.24), channel_id=1, source_target_pairs={{0,248},{8,0},{16,8},{24,16},{32,24},{40,32},{48,40},{56,48},{64,5... | collective-permute-start | bytes 1572872 | tf_op jit(solution)/shard_map/ppermute | solution.py:19
  37.6 21.5 %collective-permute-start.3 = (bf16[8,128,256]{2,1,0:T(8,128)(2,1)}, bf16[8,128,256]{2,1,0:T(8,128)(2,1)}, u32[]{:S(2)}, u32[]{:S(2)}) collective-permute-start(bf16[8,128,256]{2,1,0:T(8,128)(2,1)} %get-tuple-element.23), channel_id=1, source_target_pairs={{0,16},{8,24},{16,32},{24,40},{32,48},{40,56},{48,64},{56,72},{64,... | collective-permute-start | bytes 1572872 | tf_op jit(solution)/shard_map/ppermute | solution.py:19
  43.8 26.4 %collective-permute-start.5 = (bf16[8,128,256]{2,1,0:T(8,128)(2,1)}, bf16[8,128,256]{2,1,0:T(8,128)(2,1)S(1)}, u32[]{:S(2)}, u32[]{:S(2)}) collective-permute-start(bf16[8,128,256]{2,1,0:T(8,128)(2,1)} %get-tuple-element.26), channel_id=1, source_target_pairs={{0,16},{8,24},{16,32},{24,40},{32,48},{40,56},{48,64},{56,72},{64,... | collective-permute-start | bytes 1572872 | tf_op jit(solution)/shard_map/ppermute | solution.py:19
  44.7 31.7 %all-to-all-start = ((bf16[8,128,256]{2,1,0:T(8,128)(2,1)}), bf16[8,128,256]{2,1,0:T(8,128)(2,1)S(1)}, u32[]{:S(2)}, u32[]{:S(2)}) async-start(bf16[8,128,256]{2,1,0:T(8,128)(2,1)} %multiply_convert_fusion), calls=%async_computation | async-start | bytes 1048576 | tf_op jit(solution)/shard_map/all_to_all | solution.py:164

commit v3 on v0

v3 whole, which is shorter than its diff:
```python
import functools
import math

import jax
import jax.numpy as jnp
from jax import lax
from jax.experimental import pallas as pl
from jax.experimental.pallas import tpu as pltpu
from jax.sharding import PartitionSpec as P

learning_rate = 0.15
gradient_scale = 0.1
parts = 2
group_size = 8
lanes = 128
mebi = 1024 * 1024

smem = pl.BlockSpec(memory_space=pltpu.SMEM)
vmem = pl.BlockSpec(memory_space=pltpu.VMEM)
far = pl.BlockSpec(memory_space=pltpu.HBM)


def contract(left, right, dims):
    return lax.dot_general(left, right, ((dims[:1], dims[1:]), ((), ())), preferred_element_type=jnp.float32)


def walk(groups, slot_of, cell_ref, peak_ref, values_at, peak_grad, grad_ref, scaling):
    def group(g, carry):
        found = [slot_of(g * group_size + k) for k in range(group_size)]
        resids = []
        for t, row, col, _, _ in found:
            predicted = contract(cell_ref[row], peak_ref[col], (1, 1))
            resids.append((predicted * scaling - values_at(t).astype(jnp.float32)).astype(jnp.bfloat16))
        terms = [contract(r, cell_ref[f[1]], (0, 0)) for r, f in zip(resids, found)]
        for term, f in zip(terms, found):
            peak_grad[f[4]] += term
        terms = [contract(r, peak_ref[f[2]], (1, 0)) for r, f in zip(resids, found)]
        for term, f in zip(terms, found):
            grad_ref[f[3]] += term
        return carry

    lax.fori_loop(0, groups, group, 0)


def stepped(peak, grad, scaling):
    return (peak.astype(jnp.float32) - learning_rate * (grad * scaling)).astype(jnp.bfloat16)


def first_kernel(scaling, last, counts, index, cell_in, peak_in, values_in, *refs):
    news, (grad_ref, pack, cell_ref, peak_ref, values_ref, meta, peak_grad, sems) = refs[:parts], refs[parts:]
    row_tiles, tile_size, _ = cell_ref.shape
    peak_tiles = peak_ref.shape[0]
    slots = values_ref.shape[0]
    loads = [
        pltpu.make_async_copy(cell_in, cell_ref, sems.at[0]),
        pltpu.make_async_copy(peak_in, peak_ref, sems.at[1]),
        pltpu.make_async_copy(values_in.at[0], values_ref, sems.at[2]),
    ]
    for copy in loads:
        copy.start()
    lane = lax.broadcasted_iota(jnp.int32, (tile_size, lanes), 1)
    coded = jnp.full((tile_size, lanes), counts[0, last], jnp.int32)
    for t in range(slots):
        coded = jnp.where(lane == t, index[last, t], coded)
    meta[...] = coded.astype(jnp.float32).astype(meta.dtype)
    sends = [
        pltpu.make_async_copy(cell_in, pack.at[pl.ds(0, row_tiles)], sems.at[3]),
        pltpu.make_async_copy(meta, pack.at[row_tiles, :, pl.ds(0, lanes)], sems.at[4]),
        pltpu.make_async_copy(meta, pack.at[row_tiles, :, pl.ds(lanes, lanes)], sems.at[5]),
    ]
    for t in range(slots):
        place = pack.at[row_tiles + 1 + t // 2, :, pl.ds((t % 2) * lanes, lanes)]
        sends.append(pltpu.make_async_copy(values_in.at[last, t], place, sems.at[6 + t]))
    for copy in sends:
        copy.start()
    peak_grad[...] = jnp.zeros_like(peak_grad)
    grad_ref[...] = jnp.zeros_like(grad_ref)
    for copy in loads:
        copy.wait()

    def slot_of(t):
        place = index[0, t]
        row, col = place // peak_tiles, place % peak_tiles
        return t, row, col, row, col

    groups = counts[0, 0] // group_size
    walk(groups, slot_of, cell_ref, peak_ref, lambda t: values_ref[t], peak_grad, grad_ref, scaling)
    own_tiles = peak_tiles // parts
    for c in range(peak_tiles):
        news[c // own_tiles][c % own_tiles] = stepped(peak_ref[c], peak_grad[c], scaling)
    for copy in sends:
        copy.wait()


def part_kernel(scaling, stratum, part, peak_tiles, packed, closing, fresh, *refs):
    if packed:
        meta, pack, peak_ref, *rest = refs
        cell_ref = pack
    else:
        counts, index, cell_ref, values, peak_ref, *rest = refs
    given = None
    if not fresh:
        given, *rest = rest
    if closing:
        early, new_ref, out_ref, grad_ref, peak_grad, places = rest
    else:
        new_ref, grad_ref, peak_grad, places = rest
    own_tiles = peak_ref.shape[0]
    row_tiles = grad_ref.shape[0] - 1
    slots = places.shape[0] - group_size
    live = meta[0, slots] if packed else counts[0, stratum]
    placed = (lambda t: meta[0, t]) if packed else (lambda t: index[stratum, t])

    def values_at(t):
        if not packed:
            return values[0, t]
        column = pl.multiple_of((t % 2) * lanes, lanes)
        return pack[row_tiles + 1 + t // 2, :, pl.ds(column, lanes)]

    def note(t, found):
        place = placed(t)
        places[found] = place * slots + t
        mine = (place % peak_tiles) // own_tiles == part
        return found + jnp.where(mine, 1, 0)

    found = lax.fori_loop(0, live, note, 0)
    for k in range(group_size):
        places[found + k] = -1
    peak_grad[...] = jnp.zeros_like(peak_grad)
    grad_ref[...] = jnp.zeros_like(grad_ref) if fresh else given[...]

    def slot_of(k):
        code = places[k]
        used = code >= 0
        code = jnp.maximum(code, 0)
        place = code // slots
        row, col = place // peak_tiles, place % own_tiles
        return code % slots, row, col, jnp.where(used, row, row_tiles), jnp.where(used, col, own_tiles)

    groups = (found + group_size - 1) // group_size
    walk(groups, slot_of, cell_ref, peak_ref, values_at, peak_grad, grad_ref, scaling)
    for c in range(own_tiles):
        new_ref[c] = stepped(peak_ref[c], peak_grad[c], scaling)
    if closing:
        for r in range(row_tiles):
            out_ref[r, 0] = (early[r] * (gradient_scale * scaling)).astype(out_ref.dtype)
            out_ref[r, 1] = (grad_ref[r] * (gradient_scale * scaling)).astype(out_ref.dtype)


def last_kernel(scaling, *refs):
    pieces, (shares, late, out_ref, sum_ref, sems) = refs[:parts], refs[parts:]
    own_tiles = pieces[0].shape[0]
    copies = [
        pltpu.make_async_copy(pieces[p], out_ref.at[pl.ds(p * own_tiles, own_tiles)], sems.at[p])
        for p in range(parts)
    ]
    for copy in copies:
        copy.start()
    total = late[...].astype(jnp.float32)
    for j in range(shares.shape[0]):
        total = total + shares[j, 0].astype(jnp.float32)
    sum_ref[...] = total
    for copy in copies:
        copy.wait()


def cost(flops, read):
    return pl.CostEstimate(flops=flops, bytes_accessed=read, transcendentals=0)


def per_device(cell_factors, peak_factors, tile_values, tile_index, tile_counts):
    cell_dev, rank_width = cell_factors.shape
    strata, slots, tile_size, _ = tile_values.shape
    block_rows = peak_factors.shape[0]
    row_tiles = cell_dev // tile_size
    peak_tiles = block_rows // tile_size
    own_tiles = peak_tiles // parts
    chroms = lax.axis_size("chrom")
    cells = lax.axis_size("cell")
    share_rows = cell_dev // chroms
    scaling = 1.0 / math.sqrt(rank_width)
    flops = 6 * slots * tile_size * tile_size * rank_width
    cell_blocks = cell_factors.reshape(row_tiles, tile_size, rank_width)
    peak_block = peak_factors.reshape(peak_tiles, tile_size, rank_width)
    counts = tile_counts.T
    last = strata - 1
    grid_spec = dict(grid=(1,))

    back_one = [(i, (i - 1) % cells) for i in range(cells)]
    swap = [(i, i ^ 1) for i in range(cells)]
    odd_on = [(i, (i + 2) % cells if i % 2 else i) for i in range(cells)]
    odd_back = [(i, (i - 2) % cells if i % 2 else i) for i in range(cells)]
    even_on = [(i, i if i % 2 else (i + 2) % cells) for i in range(cells)]

    piece_shape = (own_tiles, tile_size, rank_width)
    piece_out = jax.ShapeDtypeStruct(piece_shape, jnp.bfloat16)
    grad_out = jax.ShapeDtypeStruct((row_tiles + 1, tile_size, rank_width), jnp.float32)
    pack_out = jax.ShapeDtypeStruct((row_tiles + 1 + slots // 2, tile_size, rank_width), jnp.bfloat16)

    *pieces, grad, pack = pl.pallas_call(
        functools.partial(first_kernel, scaling, last),
        out_shape=(piece_out,) * parts + (grad_out, pack_out),
        in_specs=[smem, smem, far, far, far],
        out_specs=(vmem,) * parts + (vmem, far),
        scratch_shapes=[
            pltpu.VMEM(cell_blocks.shape, jnp.bfloat16),
            pltpu.VMEM(peak_block.shape, jnp.bfloat16),
            pltpu.VMEM(tile_values.shape[1:], jnp.bfloat16),
            pltpu.VMEM((tile_size, lanes), jnp.bfloat16),
            pltpu.VMEM(peak_block.shape, jnp.float32),
            pltpu.SemaphoreType.DMA((6 + slots,)),
        ],
        compiler_params=pltpu.CompilerParams(vmem_limit_bytes=60 * mebi),
        cost_estimate=cost(flops, 8 * mebi),
        **grid_spec,
    )(counts, tile_index, cell_blocks, peak_block, tile_values)
    pieces = [lax.ppermute(piece, "cell", back_one) for piece in pieces]
    pack = lax.ppermute(pack, "cell", odd_on)
    meta = pack[row_tiles, :1, :lanes].astype(jnp.int32)

    def part_call(stratum, part, piece, given, early):
        packed = stratum == last
        closing = early is not None
        if packed:
            args, in_specs = [meta, pack, piece], [smem, vmem, vmem]
        else:
            own_values = pl.BlockSpec((1,) + tile_values.shape[1:], lambda i: (stratum, 0, 0, 0))
            args = [counts, tile_index, cell_blocks, tile_values, piece]
            in_specs = [smem, smem, vmem, own_values, vmem]
        if given is not None:
            args.append(given)
        if closing:
            args.append(early)
        in_specs += [vmem] * (len(args) - len(in_specs))
        scratch = [
            pltpu.VMEM((own_tiles + 1, tile_size, rank_width), jnp.float32),
            pltpu.SMEM((slots + group_size,), jnp.int32),
        ]
        if closing:
            out_shape = (piece_out, jax.ShapeDtypeStruct((row_tiles, 2, tile_size, rank_width), jnp.bfloat16))
            scratch.insert(0, pltpu.VMEM(grad_out.shape, jnp.float32))
        else:
            out_shape = (piece_out, grad_out)
        return pl.pallas_call(
            functools.partial(
                part_kernel, scaling, stratum, part, peak_tiles, packed, closing, given is None
            ),
            out_shape=out_shape,
            in_specs=in_specs,
            out_specs=(vmem, vmem),
            scratch_shapes=scratch,
            compiler_params=pltpu.CompilerParams(vmem_limit_bytes=16 * mebi),
            cost_estimate=cost(flops // parts, 3 * mebi),
            **grid_spec,
        )(*args)

    for part in range(parts):
        pieces[part], grad = part_call(1, part, pieces[part], grad, None)
        pieces[part] = lax.ppermute(pieces[part], "cell", swap)
    early, late = grad, None
    for part in range(parts):
        pieces[part], late = part_call(
            last, part, pieces[part], late, early if part == parts - 1 else None
        )
        pieces[part] = lax.ppermute(pieces[part], "cell", even_on)
    shares = late.reshape(chroms, cell_dev // chroms // tile_size, 2, tile_size, rank_width)
    shares = shares.transpose(0, 2, 1, 3, 4).reshape(chroms, 2, share_rows, rank_width)
    shares = lax.all_to_all(shares, "chrom", 0, 0, tiled=True)
    owed = jnp.sum(shares[:, 1].astype(jnp.float32), axis=0).astype(jnp.bfloat16)
    owed = lax.ppermute(owed, "cell", odd_back)
    peak_out, summed = pl.pallas_call(
        functools.partial(last_kernel, scaling),
        out_shape=(
            jax.ShapeDtypeStruct(peak_block.shape, jnp.bfloat16),
            jax.ShapeDtypeStruct((share_rows, rank_width), jnp.float32),
        ),
        in_specs=[vmem] * (parts + 2),
        out_specs=(far, vmem),
        scratch_shapes=[pltpu.SemaphoreType.DMA((parts,))],
        compiler_params=pltpu.CompilerParams(vmem_limit_bytes=16 * mebi),
        cost_estimate=cost(0, 3 * mebi),
        **grid_spec,
    )(*pieces, shares, owed)
    return (peak_out.reshape(block_rows, rank_width), summed)


def solution(mesh):
    in_specs = (
        P("cell", None),
        P(("cell", "chrom"), None),
        P("cell", "chrom", None, None),
        P("cell", "chrom"),
        P("cell", "chrom"),
    )
    out_specs = (P(("cell", "chrom"), None), P(("cell", "chrom"), None))
    return jax.shard_map(
        per_device, mesh=mesh, in_specs=in_specs, out_specs=out_specs, check_vma=False
    )
```

time: 208 us -> 123 us (0.59)
  the two profiles are of different devices: /device:TPU:4 before, /device:TPU:1 now
where the time goes in v3:
time: 123 us; the launch traced here: 122 us
  Pallas kernels  62 us (50%)
  starting transfers between devices  29.2 us (24%)
  waiting for transfers between devices  28.4 us (23%)
  local copies, waits for them, and re-layouts  1.28 us (1%)
    pallas_call x1, Pallas kernels, per_device(): pl.pallas_call(functools.partial(first_kernel, scaling, last), out_shape=...  51.3 us
    all_to_all x1, waiting for transfers between devices, per_device(): shares = lax.all_to_all(shares, 'chrom', 0, 0, tiled=True)  20.7 us
    pallas_call x4, Pallas kernels, part_call(): pl.pallas_call(functools.partial(part_kernel, scaling, stratum, part, pea...  9.09 us
    ppermute x2, starting transfers between devices, per_device(): pieces[part] = lax.ppermute(pieces[part], 'cell', swap)  7.82 us
    ppermute x2, starting transfers between devices, per_device(): pieces = [lax.ppermute(piece, 'cell', back_one) for piece in pieces]  6.88 us
    all_to_all x1, starting transfers between devices, per_device(): shares = lax.all_to_all(shares, 'chrom', 0, 0, tiled=True)  6.87 us
    ppermute x1, starting transfers between devices, per_device(): pack = lax.ppermute(pack, 'cell', odd_on)  4.37 us
    ppermute x1, waiting for transfers between devices, per_device(): owed = lax.ppermute(owed, 'cell', odd_back)  3.06 us
  transfers between devices with their start and end apart: 9, of which 4 were waited for; matrix products, arithmetic and copies ran while one was open for 0% of the time, Pallas kernels for 5%

profile of v3, /device:TPU:1, one launch (start us, length us, event | category | flops | bytes accessed | tf_op | source)
XLA Modules:
  0.0 121.8 jit_solution(18225583856855500029)
XLA Ops:
  0.6 0.0 copy-start
  0.6 0.0 copy-start.1
  0.7 0.0 copy-start.3
  0.7 0.0 copy-start.4
  0.7 51.3 %shard_map.68 = (bf16[8,128,256]{2,1,0:T(8,128)(2,1)}, bf16[8,128,256]{2,1,0:T(8,128)(2,1)}, f32[9,128,256]{2,1,0:T(8,128)}, bf16[25,128,256]{2,1,0:T(8,128)(2,1)}) custom-call(s32[1,3]{1,0:T(1,128)} %bitcast.12, s32[3,32]{1,0:T(4,128)} %refs_1_.3, bf16[8,128,256]{2,1,0:T(8,128)(2,1)} %bitcast.9, bf16[16,128,256]{2,1,0:T(8,128)(2,1)} %bitcast.15, ...), custom_call_target="tpu_custom_call" | custom-call | flops 805306368 | bytes 8388608 | tf_op jit(solution)/shard_map/pallas_call | solution.py:200
  52.0 4.4 %collective-permute-start = (bf16[25,128,256]{2,1,0:T(8,128)(2,1)}, bf16[25,128,256]{2,1,0:T(8,128)(2,1)S(1)}, u32[]{:S(2)}, u32[]{:S(2)}) collective-permute-start(bf16[25,128,256]{2,1,0:T(8,128)(2,1)} %get-tuple-element.16), channel_id=1, source_target_pairs={{0,0},{8,24},{16,16},{24,40},{32,32},{40,56},{48,48},{56,72},{64,6... | collective-permute-start | bytes 4915208 | tf_op jit(solution)/shard_map/ppermute | solution.py:218
  56.4 0.9 collective-permute-start.1
  57.3 5.9 %collective-permute-start.4 = (bf16[8,128,256]{2,1,0:T(8,128)(2,1)}, bf16[8,128,256]{2,1,0:T(8,128)(2,1)S(1)}, u32[]{:S(2)}, u32[]{:S(2)}) collective-permute-start(bf16[8,128,256]{2,1,0:T(8,128)(2,1)} %get-tuple-element.21), channel_id=1, source_target_pairs={{0,248},{8,0},{16,8},{24,16},{32,24},{40,32},{48,40},{56,48},{64,5... | collective-permute-start | bytes 1572872 | tf_op jit(solution)/shard_map/ppermute | solution.py:217
  63.3 2.0 %collective-permute-done.1.refs_4_ = bf16[8,128,256]{2,1,0:T(8,128)(2,1)S(1)} collective-permute-done((bf16[8,128,256]{2,1,0:T(8,128)(2,1)}, bf16[8,128,256]{2,1,0:T(8,128)(2,1)S(1)}, u32[]{:S(2)}, u32[]{:S(2)}) %collective-permute-start.1) | collective-permute-done | bytes 524320 | tf_op jit(solution)/shard_map/ppermute | solution.py:217
  65.3 0.0 copy-done
  65.3 0.0 copy-done.1
  65.3 0.0 copy-done.3
  65.3 0.0 copy-done.4
  65.3 0.0 copy-start.2
  65.3 1.3 %copy-done.2 = f32[9,128,256]{2,1,0:T(8,128)S(1)} copy-done((f32[9,128,256]{2,1,0:T(8,128)S(1)}, f32[9,128,256]{2,1,0:T(8,128)}, u32[]{:S(2)}) %copy-start.2) | copy-done | bytes 1179672
  66.6 2.6 %shard_map.69 = (bf16[8,128,256]{2,1,0:T(8,128)(2,1)S(1)}, f32[9,128,256]{2,1,0:T(8,128)S(1)}) custom-call(s32[1,3]{1,0:T(1,128)S(1)} %bitcast.13, s32[3,32]{1,0:T(4,128)S(1)} %copy-done.3, bf16[8,128,256]{2,1,0:T(8,128)(2,1)S(1)} %bitcast.10, bf16[3,32,128,128]{3,2,1,0:T(8,128)(2,1)S(1)} %copy-done, ...), custom_call_target="tpu_custom_call" | custom-call | flops 402653184 | bytes 3145728 | tf_op jit(solution)/shard_map/pallas_call | solution.py:244
  69.2 6.1 %collective-permute-start.2 = (bf16[8,128,256]{2,1,0:T(8,128)(2,1)S(1)}, bf16[8,128,256]{2,1,0:T(8,128)(2,1)S(1)}, u32[]{:S(2)}, u32[]{:S(2)}) collective-permute-start(bf16[8,128,256]{2,1,0:T(8,128)(2,1)S(1)} %get-tuple-element.19), channel_id=1, source_target_pairs={{0,8},{8,0},{16,24},{24,16},{32,40},{40,32},{48,56},{56,48},{64,72... | collective-permute-start | bytes 1572872 | tf_op jit(solution)/shard_map/ppermute | solution.py:259
  75.2 0.0 collective-permute-done.4.refs_4_
  75.2 1.9 %shard_map.71 = (bf16[8,128,256]{2,1,0:T(8,128)(2,1)S(1)}, f32[9,128,256]{2,1,0:T(8,128)S(1)}) custom-call(s32[1,3]{1,0:T(1,128)S(1)} %bitcast.14, s32[3,32]{1,0:T(4,128)S(1)} %copy-done.3, bf16[8,128,256]{2,1,0:T(8,128)(2,1)S(1)} %bitcast.11, bf16[3,32,128,128]{3,2,1,0:T(8,128)(2,1)S(1)} %copy-done, ...), custom_call_target="tpu_custom_call" | custom-call | flops 402653184 | bytes 3145728 | tf_op jit(solution)/shard_map/pallas_call | solution.py:244
  77.1 1.7 %collective-permute-start.5 = (bf16[8,128,256]{2,1,0:T(8,128)(2,1)S(1)}, bf16[8,128,256]{2,1,0:T(8,128)(2,1)S(1)}, u32[]{:S(2)}, u32[]{:S(2)}) collective-permute-start(bf16[8,128,256]{2,1,0:T(8,128)(2,1)S(1)} %get-tuple-element.23), channel_id=1, source_target_pairs={{0,8},{8,0},{16,24},{24,16},{32,40},{40,32},{48,56},{56,48},{64,72... | collective-permute-start | bytes 1572872 | tf_op jit(solution)/shard_map/ppermute | solution.py:259
  78.9 2.6 %collective-permute-done.refs_1_ = bf16[25,128,256]{2,1,0:T(8,128)(2,1)S(1)} collective-permute-done((bf16[25,128,256]{2,1,0:T(8,128)(2,1)}, bf16[25,128,256]{2,1,0:T(8,128)(2,1)S(1)}, u32[]{:S(2)}, u32[]{:S(2)}) %collective-permute-start) | collective-permute-done | bytes 1638432 | tf_op jit(solution)/shard_map/ppermute | solution.py:218
  81.5 0.0 collective-permute-done.2.refs_2_
  81.5 1.8 %shard_map.70 = (bf16[8,128,256]{2,1,0:T(8,128)(2,1)S(1)}, f32[9,128,256]{2,1,0:T(8,128)S(1)}) custom-call(s32[1,128]{1,0:T(1,128)S(1)} %fusion.refs_0_, bf16[25,128,256]{2,1,0:T(8,128)(2,1)S(1)} %collective-permute-done.refs_1_, bf16[8,128,256]{2,1,0:T(8,128)(2,1)S(1)} %collective-permute-done.2.refs_2_), custom_call_target="tpu_custom_call" | custom-call | flops 402653184 | bytes 3145728 | tf_op jit(solution)/shard_map/pallas_call | solution.py:244
  83.3 0.0 collective-permute-done.5.refs_2_
  83.3 2.8 %shard_map.72 = (bf16[8,128,256]{2,1,0:T(8,128)(2,1)S(1)}, bf16[8,2,128,256]{3,2,1,0:T(8,128)(2,1)}) custom-call(s32[1,128]{1,0:T(1,128)S(1)} %fusion.refs_0_, bf16[25,128,256]{2,1,0:T(8,128)(2,1)S(1)} %collective-permute-done.refs_1_, bf16[8,128,256]{2,1,0:T(8,128)(2,1)S(1)} %collective-permute-done.5.refs_2_, ...), custom_call_target="tpu_custom_call" | custom-call | flops 402653184 | bytes 3145728 | tf_op jit(solution)/shard_map/pallas_call | solution.py:244
  86.1 6.9 %all-to-all-start = ((bf16[8,2,128,256]{3,2,1,0:T(8,128)(2,1)}), bf16[8,2,128,256]{3,2,1,0:T(8,128)(2,1)S(1)}, u32[]{:S(2)}, u32[]{:S(2)}) async-start(bf16[8,2,128,256]{3,2,1,0:T(8,128)(2,1)} %get-tuple-element.27), calls=%async_computation | async-start | bytes 2097152 | tf_op jit(solution)/shard_map/all_to_all | solution.py:268
  93.0 0.7 collective-permute-start.6
  93.7 0.7 collective-permute-start.3
  94.4 20.7 %all-to-all-done.refs_2_ = bf16[8,2,128,256]{3,2,1,0:T(8,128)(2,1)S(1)} async-done(((bf16[8,2,128,256]{3,2,1,0:T(8,128)(2,1)}), bf16[8,2,128,256]{3,2,1,0:T(8,128)(2,1)S(1)}, u32[]{:S(2)}, u32[]{:S(2)}) %all-to-all-start) | async-done | bytes 1048608 | tf_op jit(solution)/shard_map/all_to_all | solution.py:268
  115.1 0.1 slice_reduce_fusion
  115.2 1.9 %collective-permute-start.7 = (bf16[128,256]{1,0:T(8,128)(2,1)S(1)}, bf16[128,256]{1,0:T(8,128)(2,1)S(1)}, u32[]{:S(2)}, u32[]{:S(2)}) collective-permute-start(bf16[128,256]{1,0:T(8,128)(2,1)S(1)} %slice_reduce_fusion), channel_id=1, source_target_pairs={{0,0},{8,248},{16,16},{24,8},{32,32},{40,24},{48,48},{56,40},{64,6... | collective-permute-start | bytes 196616 | tf_op jit(solution)/shard_map/ppermute | solution.py:270
  117.1 0.0 collective-permute-done.6.refs_1_
  117.1 0.0 collective-permute-done.3.refs_0_
  117.1 3.1 %collective-permute-done.7.refs_3_ = bf16[128,256]{1,0:T(8,128)(2,1)S(1)} collective-permute-done((bf16[128,256]{1,0:T(8,128)(2,1)S(1)}, bf16[128,256]{1,0:T(8,128)(2,1)S(1)}, u32[]{:S(2)}, u32[]{:S(2)}) %collective-permute-start.7) | collective-permute-done | bytes 65568 | tf_op jit(solution)/shard_map/ppermute | solution.py:270
  120.2 1.6 %shard_map.73 = (bf16[16,128,256]{2,1,0:T(8,128)(2,1)}, f32[128,256]{1,0:T(8,128)}) custom-call(bf16[8,128,256]{2,1,0:T(8,128)(2,1)S(1)} %collective-permute-done.3.refs_0_, bf16[8,128,256]{2,1,0:T(8,128)(2,1)S(1)} %collective-permute-done.6.refs_1_, bf16[8,2,128,256]{3,2,1,0:T(8,128)(2,1)S(1)} %all-to-all-done.refs_2_, ...), custom_call_target="tpu_custom_call" | custom-call | bytes 3145728 | tf_op jit(solution)/shard_map/pallas_call | solution.py:271
  (1 shorter events, 0.0 us)
Async XLA Ops:
  0.6 64.6 %copy-start = (bf16[3,32,128,128]{3,2,1,0:T(8,128)(2,1)S(1)}, bf16[3,32,128,128]{3,2,1,0:T(8,128)(2,1)}, u32[]{:S(2)}) copy-start(bf16[3,32,128,128]{3,2,1,0:T(8,128)(2,1)} %refs_3_.3) | copy-start | bytes 9437188
  0.6 64.6 %copy-start.1 = (bf16[1024,256]{1,0:T(8,128)(2,1)S(1)}, bf16[1024,256]{1,0:T(8,128)(2,1)}, u32[]{:S(2)}) copy-start(bf16[1024,256]{1,0:T(8,128)(2,1)} %param.5) | copy-start | bytes 1572868
  0.7 64.6 %copy-start.3 = (s32[3,32]{1,0:T(4,128)S(1)}, s32[3,32]{1,0:T(4,128)}, u32[]{:S(2)}) copy-start(s32[3,32]{1,0:T(4,128)} %refs_1_.3) | copy-start | bytes 1156
  0.7 64.6 %copy-start.4 = (s32[3,1]{0,1:T(1,128)S(1)}, s32[3,1]{0,1:T(1,128)}, u32[]{:S(2)}) copy-start(s32[3,1]{0,1:T(1,128)} %param.9) | copy-start | bytes 40
  52.0 29.5 %collective-permute-start = (bf16[25,128,256]{2,1,0:T(8,128)(2,1)}, bf16[25,128,256]{2,1,0:T(8,128)(2,1)S(1)}, u32[]{:S(2)}, u32[]{:S(2)}) collective-permute-start(bf16[25,128,256]{2,1,0:T(8,128)(2,1)} %get-tuple-element.16), channel_id=1, source_target_pairs={{0,0},{8,24},{16,16},{24,40},{32,32},{40,56},{48,48},{56,72},{64,6... | collective-permute-start | bytes 4915208 | tf_op jit(solution)/shard_map/ppermute | solution.py:218
  56.4 8.9 %collective-permute-start.1 = (bf16[8,128,256]{2,1,0:T(8,128)(2,1)}, bf16[8,128,256]{2,1,0:T(8,128)(2,1)S(1)}, u32[]{:S(2)}, u32[]{:S(2)}) collective-permute-start(bf16[8,128,256]{2,1,0:T(8,128)(2,1)} %get-tuple-element.17), channel_id=1, source_target_pairs={{0,248},{8,0},{16,8},{24,16},{32,24},{40,32},{48,40},{56,48},{64,5... | collective-permute-start | bytes 1572872 | tf_op jit(solution)/shard_map/ppermute | solution.py:217
  57.3 17.9 %collective-permute-start.4 = (bf16[8,128,256]{2,1,0:T(8,128)(2,1)}, bf16[8,128,256]{2,1,0:T(8,128)(2,1)S(1)}, u32[]{:S(2)}, u32[]{:S(2)}) collective-permute-start(bf16[8,128,256]{2,1,0:T(8,128)(2,1)} %get-tuple-element.21), channel_id=1, source_target_pairs={{0,248},{8,0},{16,8},{24,16},{32,24},{40,32},{48,40},{56,48},{64,5... | collective-permute-start | bytes 1572872 | tf_op jit(solution)/shard_map/ppermute | solution.py:217
  65.3 1.3 %copy-start.2 = (f32[9,128,256]{2,1,0:T(8,128)S(1)}, f32[9,128,256]{2,1,0:T(8,128)}, u32[]{:S(2)}) copy-start(f32[9,128,256]{2,1,0:T(8,128)} %get-tuple-element.18.refs_5_) | copy-start | bytes 3538948
  69.2 12.3 %collective-permute-start.2 = (bf16[8,128,256]{2,1,0:T(8,128)(2,1)S(1)}, bf16[8,128,256]{2,1,0:T(8,128)(2,1)S(1)}, u32[]{:S(2)}, u32[]{:S(2)}) collective-permute-start(bf16[8,128,256]{2,1,0:T(8,128)(2,1)S(1)} %get-tuple-element.19), channel_id=1, source_target_pairs={{0,8},{8,0},{16,24},{24,16},{32,40},{40,32},{48,56},{56,48},{64,72... | collective-permute-start | bytes 1572872 | tf_op jit(solution)/shard_map/ppermute | solution.py:259
  77.1 6.2 %collective-permute-start.5 = (bf16[8,128,256]{2,1,0:T(8,128)(2,1)S(1)}, bf16[8,128,256]{2,1,0:T(8,128)(2,1)S(1)}, u32[]{:S(2)}, u32[]{:S(2)}) collective-permute-start(bf16[8,128,256]{2,1,0:T(8,128)(2,1)S(1)} %get-tuple-element.23), channel_id=1, source_target_pairs={{0,8},{8,0},{16,24},{24,16},{32,40},{40,32},{48,56},{56,48},{64,72... | collective-permute-start | bytes 1572872 | tf_op jit(solution)/shard_map/ppermute | solution.py:259
  86.1 29.0 %all-to-all-start = ((bf16[8,2,128,256]{3,2,1,0:T(8,128)(2,1)}), bf16[8,2,128,256]{3,2,1,0:T(8,128)(2,1)S(1)}, u32[]{:S(2)}, u32[]{:S(2)}) async-start(bf16[8,2,128,256]{3,2,1,0:T(8,128)(2,1)} %get-tuple-element.27), calls=%async_computation | async-start | bytes 2097152 | tf_op jit(solution)/shard_map/all_to_all | solution.py:268
  93.0 24.1 %collective-permute-start.6 = (bf16[8,128,256]{2,1,0:T(8,128)(2,1)S(1)}, bf16[8,128,256]{2,1,0:T(8,128)(2,1)S(1)}, u32[]{:S(2)}, u32[]{:S(2)}) collective-permute-start(bf16[8,128,256]{2,1,0:T(8,128)(2,1)S(1)} %get-tuple-element.26), channel_id=1, source_target_pairs={{0,16},{8,8},{16,32},{24,24},{32,48},{40,40},{48,64},{56,56},{64,8... | collective-permute-start | bytes 1572872 | tf_op jit(solution)/shard_map/ppermute | solution.py:265
  93.7 23.4 %collective-permute-start.3 = (bf16[8,128,256]{2,1,0:T(8,128)(2,1)S(1)}, bf16[8,128,256]{2,1,0:T(8,128)(2,1)S(1)}, u32[]{:S(2)}, u32[]{:S(2)}) collective-permute-start(bf16[8,128,256]{2,1,0:T(8,128)(2,1)S(1)} %get-tuple-element.20), channel_id=1, source_target_pairs={{0,16},{8,8},{16,32},{24,24},{32,48},{40,40},{48,64},{56,56},{64,8... | collective-permute-start | bytes 1572872 | tf_op jit(solution)/shard_map/ppermute | solution.py:265
  115.2 5.0 %collective-permute-start.7 = (bf16[128,256]{1,0:T(8,128)(2,1)S(1)}, bf16[128,256]{1,0:T(8,128)(2,1)S(1)}, u32[]{:S(2)}, u32[]{:S(2)}) collective-permute-start(bf16[128,256]{1,0:T(8,128)(2,1)S(1)} %slice_reduce_fusion), channel_id=1, source_target_pairs={{0,0},{8,248},{16,16},{24,8},{32,32},{40,24},{48,48},{56,40},{64,6... | collective-permute-start | bytes 196616 | tf_op jit(solution)/shard_map/ppermute | solution.py:270

commit v4 on v3

v4 whole, which is shorter than its diff:
```python
import functools
import math

import jax
import jax.numpy as jnp
from jax import lax
from jax.experimental import pallas as pl
from jax.experimental.pallas import tpu as pltpu
from jax.sharding import PartitionSpec as P

learning_rate = 0.15
gradient_scale = 0.1
parts = 2
group_size = 8
lanes = 128
mebi = 1024 * 1024

smem = pl.BlockSpec(memory_space=pltpu.SMEM)
vmem = pl.BlockSpec(memory_space=pltpu.VMEM)
far = pl.BlockSpec(memory_space=pltpu.HBM)


def contract(left, right, dims):
    return lax.dot_general(left, right, ((dims[:1], dims[1:]), ((), ())), preferred_element_type=jnp.float32)


def walk(groups, slot_of, cell_ref, peak_ref, values_at, peak_grad, grad_ref, scaling):
    def group(g, carry):
        found = [slot_of(g * group_size + k) for k in range(group_size)]
        resids = []
        for t, row, col, _, _ in found:
            predicted = contract(cell_ref[row], peak_ref[col], (1, 1))
            resids.append((predicted * scaling - values_at(t).astype(jnp.float32)).astype(jnp.bfloat16))
        terms = [contract(r, cell_ref[f[1]], (0, 0)) for r, f in zip(resids, found)]
        for term, f in zip(terms, found):
            peak_grad[f[4]] += term
        terms = [contract(r, peak_ref[f[2]], (1, 0)) for r, f in zip(resids, found)]
        for term, f in zip(terms, found):
            grad_ref[f[3]] += term
        return carry

    lax.fori_loop(0, groups, group, 0)


def stepped(peak, grad, scaling):
    return (peak.astype(jnp.float32) - learning_rate * (grad * scaling)).astype(jnp.bfloat16)


def first_kernel(scaling, counts, index, cell_in, peak_in, values_in, *refs):
    news, (grad_ref, cell_ref, peak_ref, values_ref, peak_grad, sems) = refs[:parts], refs[parts:]
    peak_tiles = peak_ref.shape[0]
    loads = [
        pltpu.make_async_copy(cell_in, cell_ref, sems.at[0]),
        pltpu.make_async_copy(peak_in, peak_ref, sems.at[1]),
        pltpu.make_async_copy(values_in.at[0], values_ref, sems.at[2]),
    ]
    for copy in loads:
        copy.start()
    peak_grad[...] = jnp.zeros_like(peak_grad)
    grad_ref[...] = jnp.zeros_like(grad_ref)
    for copy in loads:
        copy.wait()

    def slot_of(t):
        place = index[0, t]
        row, col = place // peak_tiles, place % peak_tiles
        return t, row, col, row, col

    groups = counts[0, 0] // group_size
    walk(groups, slot_of, cell_ref, peak_ref, lambda t: values_ref[t], peak_grad, grad_ref, scaling)
    own_tiles = peak_tiles // parts
    for c in range(peak_tiles):
        news[c // own_tiles][c % own_tiles] = stepped(peak_ref[c], peak_grad[c], scaling)


def part_kernel(scaling, stratum, part, peak_tiles, closing, fresh, *refs):
    counts, index, cell_ref, values, peak_ref, *rest = refs
    given = None
    if not fresh:
        given, *rest = rest
    if closing:
        early, new_ref, out_ref, grad_ref, peak_grad, places = rest
    else:
        new_ref, grad_ref, peak_grad, places = rest
    own_tiles = peak_ref.shape[0]
    row_tiles = grad_ref.shape[0] - 1
    slots = places.shape[0] - group_size

    def note(t, found):
        place = index[stratum, t]
        places[found] = place * slots + t
        mine = (place % peak_tiles) // own_tiles == part
        return found + jnp.where(mine, 1, 0)

    found = lax.fori_loop(0, counts[0, stratum], note, 0)
    for k in range(group_size):
        places[found + k] = -1
    peak_grad[...] = jnp.zeros_like(peak_grad)
    grad_ref[...] = jnp.zeros_like(grad_ref) if fresh else given[...]

    def slot_of(k):
        code = places[k]
        used = code >= 0
        code = jnp.maximum(code, 0)
        place = code // slots
        row, col = place // peak_tiles, place % own_tiles
        return code % slots, row, col, jnp.where(used, row, row_tiles), jnp.where(used, col, own_tiles)

    groups = (found + group_size - 1) // group_size
    walk(groups, slot_of, cell_ref, peak_ref, lambda t: values[0, t], peak_grad, grad_ref, scaling)
    for c in range(own_tiles):
        new_ref[c] = stepped(peak_ref[c], peak_grad[c], scaling)
    if closing:
        for r in range(row_tiles):
            out_ref[r] = ((early[r] + grad_ref[r]) * (gradient_scale * scaling)).astype(out_ref.dtype)


def place_kernel(*refs):
    pieces, (out_ref, sems) = refs[:parts], refs[parts:]
    own_tiles = pieces[0].shape[0]
    copies = [
        pltpu.make_async_copy(pieces[p], out_ref.at[pl.ds(p * own_tiles, own_tiles)], sems.at[p])
        for p in range(parts)
    ]
    for copy in copies:
        copy.start()
    for copy in copies:
        copy.wait()


def cost(flops, read):
    return pl.CostEstimate(flops=flops, bytes_accessed=read, transcendentals=0)


def per_device(cell_factors, peak_factors, tile_values, tile_index, tile_counts):
    cell_dev, rank_width = cell_factors.shape
    strata, slots, tile_size, _ = tile_values.shape
    block_rows = peak_factors.shape[0]
    row_tiles = cell_dev // tile_size
    peak_tiles = block_rows // tile_size
    own_tiles = peak_tiles // parts
    chroms = lax.axis_size("chrom")
    cells = lax.axis_size("cell")
    share_rows = cell_dev // chroms
    scaling = 1.0 / math.sqrt(rank_width)
    flops = 6 * slots * tile_size * tile_size * rank_width
    cell_blocks = cell_factors.reshape(row_tiles, tile_size, rank_width)
    peak_block = peak_factors.reshape(peak_tiles, tile_size, rank_width)
    counts = tile_counts.T
    last = strata - 1

    def moved(piece, by):
        return lax.ppermute(piece, "cell", [(i, (i + by) % cells) for i in range(cells)])

    piece_out = jax.ShapeDtypeStruct((own_tiles, tile_size, rank_width), jnp.bfloat16)
    grad_out = jax.ShapeDtypeStruct((row_tiles + 1, tile_size, rank_width), jnp.float32)

    *pieces, early = pl.pallas_call(
        functools.partial(first_kernel, scaling),
        grid=(1,),
        out_shape=(piece_out,) * parts + (jax.ShapeDtypeStruct(cell_blocks.shape, jnp.float32),),
        in_specs=[smem, smem, far, far, far],
        out_specs=(vmem,) * (parts + 1),
        scratch_shapes=[
            pltpu.VMEM(cell_blocks.shape, jnp.bfloat16),
            pltpu.VMEM(peak_block.shape, jnp.bfloat16),
            pltpu.VMEM(tile_values.shape[1:], jnp.bfloat16),
            pltpu.VMEM(peak_block.shape, jnp.float32),
            pltpu.SemaphoreType.DMA((3,)),
        ],
        compiler_params=pltpu.CompilerParams(vmem_limit_bytes=60 * mebi),
        cost_estimate=cost(flops, 4 * mebi),
    )(counts, tile_index, cell_blocks, peak_block, tile_values)
    pieces = [moved(piece, -1) for piece in pieces]

    def part_call(stratum, part, piece, given, closing):
        own_values = pl.BlockSpec((1,) + tile_values.shape[1:], lambda i: (stratum, 0, 0, 0))
        args = [counts, tile_index, cell_blocks, tile_values, piece]
        in_specs = [smem, smem, vmem, own_values, vmem]
        if given is not None:
            args.append(given)
        if closing:
            args.append(early)
        in_specs += [vmem] * (len(args) - len(in_specs))
        scratch = [
            pltpu.VMEM((own_tiles + 1, tile_size, rank_width), jnp.float32),
            pltpu.SMEM((slots + group_size,), jnp.int32),
        ]
        second = grad_out
        if closing:
            second = jax.ShapeDtypeStruct(cell_blocks.shape, jnp.bfloat16)
            scratch.insert(0, pltpu.VMEM(grad_out.shape, jnp.float32))
        return pl.pallas_call(
            functools.partial(part_kernel, scaling, stratum, part, peak_tiles, closing, given is None),
            grid=(1,),
            out_shape=(piece_out, second),
            in_specs=in_specs,
            out_specs=(vmem, vmem),
            scratch_shapes=scratch,
            compiler_params=pltpu.CompilerParams(vmem_limit_bytes=16 * mebi),
            cost_estimate=cost(flops // parts, 3 * mebi),
        )(*args)

    grad = None
    for stratum in range(1, strata):
        for part in range(parts):
            closing = stratum == last and part == parts - 1
            piece, grad = part_call(stratum, part, pieces[part], grad, closing)
            pieces[part] = moved(piece, last if stratum == last else -1)
    shares = lax.all_to_all(grad.reshape(cell_dev, rank_width), "chrom", 0, 0, tiled=True)
    peak_out = pl.pallas_call(
        place_kernel,
        grid=(1,),
        out_shape=jax.ShapeDtypeStruct(peak_block.shape, jnp.bfloat16),
        in_specs=[vmem] * parts,
        out_specs=far,
        scratch_shapes=[pltpu.SemaphoreType.DMA((parts,))],
        compiler_params=pltpu.CompilerParams(vmem_limit_bytes=16 * mebi),
        cost_estimate=cost(0, 8 * mebi),
    )(*pieces)
    peak_out, shares = lax.optimization_barrier((peak_out, shares))
    summed = jnp.sum(shares.reshape(chroms, share_rows, rank_width).astype(jnp.float32), axis=0)
    return (peak_out.reshape(block_rows, rank_width), summed)


def solution(mesh):
    in_specs = (
        P("cell", None),
        P(("cell", "chrom"), None),
        P("cell", "chrom", None, None),
        P("cell", "chrom"),
        P("cell", "chrom"),
    )
    out_specs = (P(("cell", "chrom"), None), P(("cell", "chrom"), None))
    return jax.shard_map(
        per_device, mesh=mesh, in_specs=in_specs, out_specs=out_specs, check_vma=False
    )
```

time: 123 us -> 77.1 us (0.63)
  Pallas kernels: 62 us -> 20.9 us
  starting transfers between devices: 29.2 us -> 25.2 us
    pallas_call x2, Pallas kernels: 53 us -> 6.98 us  [the longest x1 4.95 us: per_device(): pl.pallas_call(functools.partial(first_kernel, scaling), grid=(1,), out_s...]
    all_to_all x1, waiting for transfers between devices: 20.7 us -> 4.64 us  [per_device(): lax.all_to_all(grad.reshape(cell_dev, rank_width), 'chrom', 0, 0, tiled=T...]
    ppermute x8 -> x6, waiting for transfers between devices: 7.69 us -> 23.2 us  [moved(): lax.ppermute(piece, 'cell', [(i, (i + by) % cells) for i in range(cells)])]
    pallas_call x4, Pallas kernels: 9.09 us -> 13.9 us  [part_call(): pl.pallas_call(functools.partial(part_kernel, scaling, stratum, part, pea...]
    all_to_all x1, starting transfers between devices: 6.87 us -> 3.49 us  [per_device(): lax.all_to_all(grad.reshape(cell_dev, rank_width), 'chrom', 0, 0, tiled=T...]
    ppermute x8 -> x6, starting transfers between devices: 22.4 us -> 21.7 us  [moved(): lax.ppermute(piece, 'cell', [(i, (i + by) % cells) for i in range(cells)])]
  transfers between devices with their start and end apart: 9 -> 7, of which waited for: 4 -> 5; matrix products, arithmetic and copies ran while one was open for 0% -> 0% of each run, Pallas kernels for 5% -> 21%
where the time goes in v4:
time: 77.1 us; the launch traced here: 76.2 us
  waiting for transfers between devices  27.8 us (36%)
  starting transfers between devices  25.2 us (33%)
  Pallas kernels  20.9 us (27%)
  local copies, waits for them, and re-layouts  0.84 us (1%)
    ppermute x6, waiting for transfers between devices, moved(): lax.ppermute(piece, 'cell', [(i, (i + by) % cells) for i in range(cells)])  23.2 us
    ppermute x6, starting transfers between devices, moved(): lax.ppermute(piece, 'cell', [(i, (i + by) % cells) for i in range(cells)])  21.7 us
    pallas_call x4, Pallas kernels, part_call(): pl.pallas_call(functools.partial(part_kernel, scaling, stratum, part, pea...  13.9 us
    pallas_call x1, Pallas kernels, per_device(): pl.pallas_call(functools.partial(first_kernel, scaling), grid=(1,), out_s...  4.95 us
    all_to_all x1, waiting for transfers between devices, per_device(): lax.all_to_all(grad.reshape(cell_dev, rank_width), 'chrom', 0, 0, tiled=T...  4.64 us
    all_to_all x1, starting transfers between devices, per_device(): lax.all_to_all(grad.reshape(cell_dev, rank_width), 'chrom', 0, 0, tiled=T...  3.49 us
    pallas_call x1, Pallas kernels, per_device(): pl.pallas_call(place_kernel, grid=(1,), out_shape=jax.ShapeDtypeStruct(pe...  2.02 us
  transfers between devices with their start and end apart: 7, of which 5 were waited for; matrix products, arithmetic and copies ran while one was open for 0% of the time, Pallas kernels for 21%

profile of v4, /device:TPU:1, one launch (start us, length us, event | category | flops | bytes accessed | tf_op | source)
XLA Modules:
  0.0 76.2 jit_solution(10591177093746329794)
XLA Ops:
  0.6 0.0 copy-start
  0.6 0.0 copy-start.1
  0.7 0.0 copy-start.4
  0.7 0.0 copy-start.5
  0.7 5.0 %shard_map.68 = (bf16[8,128,256]{2,1,0:T(8,128)(2,1)}, bf16[8,128,256]{2,1,0:T(8,128)(2,1)}, f32[8,128,256]{2,1,0:T(8,128)}) custom-call(s32[1,3]{1,0:T(1,128)} %bitcast.12, s32[3,32]{1,0:T(4,128)} %refs_1_.7, bf16[8,128,256]{2,1,0:T(8,128)(2,1)} %bitcast.7, bf16[16,128,256]{2,1,0:T(8,128)(2,1)} %bitcast.18, bf16[3,32,128,128]{3,2,1,0:T(8,128)(2,1)} %refs_3_.7), custom_call_target="tpu_custom_call" | custom-call | flops 805306368 | bytes 4194304 | tf_op jit(solution)/shard_map/pallas_call | solution.py:158
  5.6 4.0 %collective-permute-start = (bf16[8,128,256]{2,1,0:T(8,128)(2,1)}, bf16[8,128,256]{2,1,0:T(8,128)(2,1)S(1)}, u32[]{:S(2)}, u32[]{:S(2)}) collective-permute-start(bf16[8,128,256]{2,1,0:T(8,128)(2,1)} %get-tuple-element.15), channel_id=1, source_target_pairs={{0,248},{8,0},{16,8},{24,16},{32,24},{40,32},{48,40},{56,48},{64,5... | collective-permute-start | bytes 1572872 | tf_op jit(solution)/shard_map/ppermute | solution.py:153
  9.6 6.0 %collective-permute-start.2 = (bf16[8,128,256]{2,1,0:T(8,128)(2,1)}, bf16[8,128,256]{2,1,0:T(8,128)(2,1)S(1)}, u32[]{:S(2)}, u32[]{:S(2)}) collective-permute-start(bf16[8,128,256]{2,1,0:T(8,128)(2,1)} %get-tuple-element.17), channel_id=1, source_target_pairs={{0,248},{8,0},{16,8},{24,16},{32,24},{40,32},{48,40},{56,48},{64,5... | collective-permute-start | bytes 1572872 | tf_op jit(solution)/shard_map/ppermute | solution.py:153
  15.6 0.2 collective-permute-done.refs_4_
  15.8 0.0 copy-done
  15.8 0.0 copy-done.1
  15.8 0.0 copy-done.4
  15.8 0.0 copy-done.5
  15.8 2.9 %shard_map.69 = (bf16[8,128,256]{2,1,0:T(8,128)(2,1)S(1)}, f32[9,128,256]{2,1,0:T(8,128)S(1)}) custom-call(s32[1,3]{1,0:T(1,128)S(1)} %bitcast.13, s32[3,32]{1,0:T(4,128)S(1)} %copy-done.4, bf16[8,128,256]{2,1,0:T(8,128)(2,1)S(1)} %bitcast.8, bf16[3,32,128,128]{3,2,1,0:T(8,128)(2,1)S(1)} %copy-done, bf16[8,128,256]{2,1,0:T(8,128)(2,1)S(1)} %collective-permute-done.refs_4_), custom_call_target="tpu_custom_call" | custom-call | flops 402653184 | bytes 3145728 | tf_op jit(solution)/shard_map/pallas_call | solution.py:193
  18.7 7.6 %collective-permute-start.1 = (bf16[8,128,256]{2,1,0:T(8,128)(2,1)S(1)}, bf16[8,128,256]{2,1,0:T(8,128)(2,1)S(1)}, u32[]{:S(2)}, u32[]{:S(2)}) collective-permute-start(bf16[8,128,256]{2,1,0:T(8,128)(2,1)S(1)} %get-tuple-element.16), channel_id=1, source_target_pairs={{0,248},{8,0},{16,8},{24,16},{32,24},{40,32},{48,40},{56,48},{64,5... | collective-permute-start | bytes 1572872 | tf_op jit(solution)/shard_map/ppermute | solution.py:153
  26.3 0.0 collective-permute-done.2.refs_4_
  26.3 3.6 %shard_map.70 = (bf16[8,128,256]{2,1,0:T(8,128)(2,1)S(1)}, f32[9,128,256]{2,1,0:T(8,128)S(1)}) custom-call(s32[1,3]{1,0:T(1,128)S(1)} %bitcast.14, s32[3,32]{1,0:T(4,128)S(1)} %copy-done.4, bf16[8,128,256]{2,1,0:T(8,128)(2,1)S(1)} %bitcast.9, bf16[3,32,128,128]{3,2,1,0:T(8,128)(2,1)S(1)} %copy-done, bf16[8,128,256]{2,1,0:T(8,128)(2,1)S(1)} %collective-permute-done.2.refs_4_, ...), custom_call_target="tpu_custom_call" | custom-call | flops 402653184 | bytes 3145728 | tf_op jit(solution)/shard_map/pallas_call | solution.py:193
  29.9 4.1 %collective-permute-start.4 = (bf16[8,128,256]{2,1,0:T(8,128)(2,1)S(1)}, bf16[8,128,256]{2,1,0:T(8,128)(2,1)S(1)}, u32[]{:S(2)}, u32[]{:S(2)}) collective-permute-start(bf16[8,128,256]{2,1,0:T(8,128)(2,1)S(1)} %get-tuple-element.21), channel_id=1, source_target_pairs={{0,248},{8,0},{16,8},{24,16},{32,24},{40,32},{48,40},{56,48},{64,5... | collective-permute-start | bytes 1572872 | tf_op jit(solution)/shard_map/ppermute | solution.py:153
  34.0 0.0 collective-permute-done.1.refs_4_
  34.0 0.0 copy-start.2
  34.0 3.7 %shard_map.71 = (bf16[8,128,256]{2,1,0:T(8,128)(2,1)}, f32[9,128,256]{2,1,0:T(8,128)S(1)}) custom-call(s32[1,3]{1,0:T(1,128)S(1)} %bitcast.15, s32[3,32]{1,0:T(4,128)S(1)} %copy-done.4, bf16[8,128,256]{2,1,0:T(8,128)(2,1)S(1)} %bitcast.10, bf16[3,32,128,128]{3,2,1,0:T(8,128)(2,1)S(1)} %copy-done, bf16[8,128,256]{2,1,0:T(8,128)(2,1)S(1)} %collective-permute-done.1.refs_4_, ...), custom_call_target="tpu_custom_call" | custom-call | flops 402653184 | bytes 3145728 | tf_op jit(solution)/shard_map/pallas_call | solution.py:193
  37.7 0.0 collective-permute-start.3
  37.7 0.9 %collective-permute-done.4.refs_4_ = bf16[8,128,256]{2,1,0:T(8,128)(2,1)S(1)} collective-permute-done((bf16[8,128,256]{2,1,0:T(8,128)(2,1)S(1)}, bf16[8,128,256]{2,1,0:T(8,128)(2,1)S(1)}, u32[]{:S(2)}, u32[]{:S(2)}) %collective-permute-start.4) | collective-permute-done | bytes 524320 | tf_op jit(solution)/shard_map/ppermute | solution.py:153
  38.6 0.0 copy-done.2
  38.6 3.7 %shard_map.72 = (bf16[8,128,256]{2,1,0:T(8,128)(2,1)}, bf16[8,128,256]{2,1,0:T(8,128)(2,1)S(1)}) custom-call(s32[1,3]{1,0:T(1,128)S(1)} %bitcast.16, s32[3,32]{1,0:T(4,128)S(1)} %copy-done.4, bf16[8,128,256]{2,1,0:T(8,128)(2,1)S(1)} %bitcast.11, bf16[3,32,128,128]{3,2,1,0:T(8,128)(2,1)S(1)} %copy-done, ...), custom_call_target="tpu_custom_call" | custom-call | flops 402653184 | bytes 3145728 | tf_op jit(solution)/shard_map/pallas_call | solution.py:193
  42.3 0.0 copy-start.3
  42.3 0.0 collective-permute-start.5
  42.3 0.8 %copy-done.3 = bf16[8,128,256]{2,1,0:T(8,128)(2,1)} copy-done((bf16[8,128,256]{2,1,0:T(8,128)(2,1)}, bf16[8,128,256]{2,1,0:T(8,128)(2,1)S(1)}, u32[]{:S(2)}) %copy-start.3) | copy-done | bytes 524312
  43.2 3.5 %all-to-all-start = ((bf16[8,128,256]{2,1,0:T(8,128)(2,1)}), bf16[8,128,256]{2,1,0:T(8,128)(2,1)S(1)}, u32[]{:S(2)}, u32[]{:S(2)}) async-start(bf16[8,128,256]{2,1,0:T(8,128)(2,1)} %copy-done.3), calls=%async_computation | async-start | bytes 1048576 | tf_op jit(solution)/shard_map/all_to_all | solution.py:210
  46.7 11.0 %collective-permute-done.3.refs_0_ = bf16[8,128,256]{2,1,0:T(8,128)(2,1)} collective-permute-done((bf16[8,128,256]{2,1,0:T(8,128)(2,1)}, bf16[8,128,256]{2,1,0:T(8,128)(2,1)}, u32[]{:S(2)}, u32[]{:S(2)}) %collective-permute-start.3) | collective-permute-done | bytes 524320 | tf_op jit(solution)/shard_map/ppermute | solution.py:153
  57.6 11.1 %collective-permute-done.5.refs_1_ = bf16[8,128,256]{2,1,0:T(8,128)(2,1)S(1)} collective-permute-done((bf16[8,128,256]{2,1,0:T(8,128)(2,1)}, bf16[8,128,256]{2,1,0:T(8,128)(2,1)S(1)}, u32[]{:S(2)}, u32[]{:S(2)}) %collective-permute-start.5) | collective-permute-done | bytes 524320 | tf_op jit(solution)/shard_map/ppermute | solution.py:153
  68.8 2.0 %shard_map.73 = bf16[16,128,256]{2,1,0:T(8,128)(2,1)} custom-call(bf16[8,128,256]{2,1,0:T(8,128)(2,1)} %collective-permute-done.3.refs_0_, bf16[8,128,256]{2,1,0:T(8,128)(2,1)S(1)} %collective-permute-done.5.refs_1_), custom_call_target="tpu_custom_call" | custom-call | bytes 8388608 | tf_op jit(solution)/shard_map/pallas_call | solution.py:211
  70.8 4.6 %all-to-all-done = bf16[8,128,256]{2,1,0:T(8,128)(2,1)S(1)} async-done(((bf16[8,128,256]{2,1,0:T(8,128)(2,1)}), bf16[8,128,256]{2,1,0:T(8,128)(2,1)S(1)}, u32[]{:S(2)}, u32[]{:S(2)}) %all-to-all-start) | async-done | bytes 524320 | tf_op jit(solution)/shard_map/all_to_all | solution.py:210
  75.4 0.7 convert_reduce_fusion
Async XLA Ops:
  0.6 15.2 %copy-start = (bf16[3,32,128,128]{3,2,1,0:T(8,128)(2,1)S(1)}, bf16[3,32,128,128]{3,2,1,0:T(8,128)(2,1)}, u32[]{:S(2)}) copy-start(bf16[3,32,128,128]{3,2,1,0:T(8,128)(2,1)} %refs_3_.7) | copy-start | bytes 9437188
  0.6 15.2 %copy-start.1 = (bf16[1024,256]{1,0:T(8,128)(2,1)S(1)}, bf16[1024,256]{1,0:T(8,128)(2,1)}, u32[]{:S(2)}) copy-start(bf16[1024,256]{1,0:T(8,128)(2,1)} %param.5) | copy-start | bytes 1572868
  0.7 15.2 %copy-start.4 = (s32[3,32]{1,0:T(4,128)S(1)}, s32[3,32]{1,0:T(4,128)}, u32[]{:S(2)}) copy-start(s32[3,32]{1,0:T(4,128)} %refs_1_.7) | copy-start | bytes 1156
  0.7 15.2 %copy-start.5 = (s32[3,1]{0,1:T(1,128)S(1)}, s32[3,1]{0,1:T(1,128)}, u32[]{:S(2)}) copy-start(s32[3,1]{0,1:T(1,128)} %param.9) | copy-start | bytes 40
  5.6 10.2 %collective-permute-start = (bf16[8,128,256]{2,1,0:T(8,128)(2,1)}, bf16[8,128,256]{2,1,0:T(8,128)(2,1)S(1)}, u32[]{:S(2)}, u32[]{:S(2)}) collective-permute-start(bf16[8,128,256]{2,1,0:T(8,128)(2,1)} %get-tuple-element.15), channel_id=1, source_target_pairs={{0,248},{8,0},{16,8},{24,16},{32,24},{40,32},{48,40},{56,48},{64,5... | collective-permute-start | bytes 1572872 | tf_op jit(solution)/shard_map/ppermute | solution.py:153
  9.6 16.7 %collective-permute-start.2 = (bf16[8,128,256]{2,1,0:T(8,128)(2,1)}, bf16[8,128,256]{2,1,0:T(8,128)(2,1)S(1)}, u32[]{:S(2)}, u32[]{:S(2)}) collective-permute-start(bf16[8,128,256]{2,1,0:T(8,128)(2,1)} %get-tuple-element.17), channel_id=1, source_target_pairs={{0,248},{8,0},{16,8},{24,16},{32,24},{40,32},{48,40},{56,48},{64,5... | collective-permute-start | bytes 1572872 | tf_op jit(solution)/shard_map/ppermute | solution.py:153
  18.7 15.3 %collective-permute-start.1 = (bf16[8,128,256]{2,1,0:T(8,128)(2,1)S(1)}, bf16[8,128,256]{2,1,0:T(8,128)(2,1)S(1)}, u32[]{:S(2)}, u32[]{:S(2)}) collective-permute-start(bf16[8,128,256]{2,1,0:T(8,128)(2,1)S(1)} %get-tuple-element.16), channel_id=1, source_target_pairs={{0,248},{8,0},{16,8},{24,16},{32,24},{40,32},{48,40},{56,48},{64,5... | collective-permute-start | bytes 1572872 | tf_op jit(solution)/shard_map/ppermute | solution.py:153
  29.9 8.7 %collective-permute-start.4 = (bf16[8,128,256]{2,1,0:T(8,128)(2,1)S(1)}, bf16[8,128,256]{2,1,0:T(8,128)(2,1)S(1)}, u32[]{:S(2)}, u32[]{:S(2)}) collective-permute-start(bf16[8,128,256]{2,1,0:T(8,128)(2,1)S(1)} %get-tuple-element.21), channel_id=1, source_target_pairs={{0,248},{8,0},{16,8},{24,16},{32,24},{40,32},{48,40},{56,48},{64,5... | collective-permute-start | bytes 1572872 | tf_op jit(solution)/shard_map/ppermute | solution.py:153
  34.0 4.6 %copy-start.2 = (f32[8,128,256]{2,1,0:T(8,128)S(1)}, f32[8,128,256]{2,1,0:T(8,128)}, u32[]{:S(2)}) copy-start(f32[8,128,256]{2,1,0:T(8,128)} %get-tuple-element.23.refs_6_) | copy-start | bytes 3145732
  37.7 19.9 %collective-permute-start.3 = (bf16[8,128,256]{2,1,0:T(8,128)(2,1)}, bf16[8,128,256]{2,1,0:T(8,128)(2,1)}, u32[]{:S(2)}, u32[]{:S(2)}) collective-permute-start(bf16[8,128,256]{2,1,0:T(8,128)(2,1)} %get-tuple-element.20), channel_id=1, source_target_pairs={{0,16},{8,24},{16,32},{24,40},{32,48},{40,56},{48,64},{56,72},{64,... | collective-permute-start | bytes 1572872 | tf_op jit(solution)/shard_map/ppermute | solution.py:153
  42.3 0.8 %copy-start.3 = (bf16[8,128,256]{2,1,0:T(8,128)(2,1)}, bf16[8,128,256]{2,1,0:T(8,128)(2,1)S(1)}, u32[]{:S(2)}) copy-start(bf16[8,128,256]{2,1,0:T(8,128)(2,1)S(1)} %get-tuple-element.25) | copy-start | bytes 1572868
  42.3 26.4 %collective-permute-start.5 = (bf16[8,128,256]{2,1,0:T(8,128)(2,1)}, bf16[8,128,256]{2,1,0:T(8,128)(2,1)S(1)}, u32[]{:S(2)}, u32[]{:S(2)}) collective-permute-start(bf16[8,128,256]{2,1,0:T(8,128)(2,1)} %get-tuple-element.24), channel_id=1, source_target_pairs={{0,16},{8,24},{16,32},{24,40},{32,48},{40,56},{48,64},{56,72},{64,... | collective-permute-start | bytes 1572872 | tf_op jit(solution)/shard_map/ppermute | solution.py:153
  43.2 32.3 %all-to-all-start = ((bf16[8,128,256]{2,1,0:T(8,128)(2,1)}), bf16[8,128,256]{2,1,0:T(8,128)(2,1)S(1)}, u32[]{:S(2)}, u32[]{:S(2)}) async-start(bf16[8,128,256]{2,1,0:T(8,128)(2,1)} %copy-done.3), calls=%async_computation | async-start | bytes 1048576 | tf_op jit(solution)/shard_map/all_to_all | solution.py:210

commit v5 on v4

--- a/solution.py
+++ b/solution.py
@@ -111,21 +111,17 @@
     for c in range(own_tiles):
         new_ref[c] = stepped(peak_ref[c], peak_grad[c], scaling)
     if closing:
+        near = out_ref.shape[0]
         for r in range(row_tiles):
-            out_ref[r] = ((early[r] + grad_ref[r]) * (gradient_scale * scaling)).astype(out_ref.dtype)
-
-
-def place_kernel(*refs):
-    pieces, (out_ref, sems) = refs[:parts], refs[parts:]
-    own_tiles = pieces[0].shape[0]
-    copies = [
-        pltpu.make_async_copy(pieces[p], out_ref.at[pl.ds(p * own_tiles, own_tiles)], sems.at[p])
-        for p in range(parts)
-    ]
-    for copy in copies:
-        copy.start()
-    for copy in copies:
-        copy.wait()
+            out_ref[r % near, r // near] = ((early[r] + grad_ref[r]) * (gradient_scale * scaling)).astype(out_ref.dtype)
+
+
+def place_kernel(part, piece_ref, *refs):
+    out_ref, sem = refs[-2:]
+    own_tiles = piece_ref.shape[0]
+    copy = pltpu.make_async_copy(piece_ref, out_ref.at[pl.ds(part * own_tiles, own_tiles)], sem)
+    copy.start()
+    copy.wait()
 
 
 def cost(flops, read):
@@ -142,6 +138,8 @@
     chroms = lax.axis_size("chrom")
     cells = lax.axis_size("cell")
     share_rows = cell_dev // chroms
+    assert share_rows == tile_size
+    near = chroms // 2
     scaling = 1.0 / math.sqrt(rank_width)
     flops = 6 * slots * tile_size * tile_size * rank_width
     cell_blocks = cell_factors.reshape(row_tiles, tile_size, rank_width)
@@ -188,7 +186,7 @@
         ]
         second = grad_out
         if closing:
-            second = jax.ShapeDtypeStruct(cell_blocks.shape, jnp.bfloat16)
+            second = jax.ShapeDtypeStruct((near, chroms // near, share_rows, rank_width), jnp.bfloat16)
             scratch.insert(0, pltpu.VMEM(grad_out.shape, jnp.float32))
         return pl.pallas_call(
             functools.partial(part_kernel, scaling, stratum, part, peak_tiles, closing, given is None),
@@ -207,19 +205,35 @@
             closing = stratum == last and part == parts - 1
             piece, grad = part_call(stratum, part, pieces[part], grad, closing)
             pieces[part] = moved(piece, last if stratum == last else -1)
-    shares = lax.all_to_all(grad.reshape(cell_dev, rank_width), "chrom", 0, 0, tiled=True)
-    peak_out = pl.pallas_call(
-        place_kernel,
-        grid=(1,),
-        out_shape=jax.ShapeDtypeStruct(peak_block.shape, jnp.bfloat16),
-        in_specs=[vmem] * parts,
-        out_specs=far,
-        scratch_shapes=[pltpu.SemaphoreType.DMA((parts,))],
-        compiler_params=pltpu.CompilerParams(vmem_limit_bytes=16 * mebi),
-        cost_estimate=cost(0, 8 * mebi),
-    )(*pieces)
+
+    def put(part, peak_out):
+        args = [pieces[part]] + ([] if peak_out is None else [peak_out])
+        return pl.pallas_call(
+            functools.partial(place_kernel, part),
+            grid=(1,),
+            out_shape=jax.ShapeDtypeStruct(peak_block.shape, jnp.bfloat16),
+            in_specs=[vmem, far][: len(args)],
+            out_specs=far,
+            scratch_shapes=[pltpu.SemaphoreType.DMA],
+            input_output_aliases={} if peak_out is None else {1: 0},
+            compiler_params=pltpu.CompilerParams(vmem_limit_bytes=16 * mebi),
+            cost_estimate=cost(0, 8 * mebi),
+        )(*args)
+
+    rings = [list(range(r * near, (r + 1) * near)) for r in range(chroms // near)]
+    shares = lax.all_to_all(grad, "chrom", 0, 0, axis_index_groups=rings, tiled=True)
+    peak_out = None
+    for part in range(parts - 1):
+        peak_out = put(part, peak_out)
     peak_out, shares = lax.optimization_barrier((peak_out, shares))
-    summed = jnp.sum(shares.reshape(chroms, share_rows, rank_width).astype(jnp.float32), axis=0)
+    shares = jnp.sum(shares.astype(jnp.float32), axis=0)
+    side = lax.axis_index("chrom") // near
+    kept = lax.dynamic_index_in_dim(shares, side, 0, keepdims=False)
+    sent = lax.dynamic_index_in_dim(shares, 1 - side, 0, keepdims=False).astype(jnp.bfloat16)
+    got = lax.ppermute(sent, "chrom", [(j, (j + near) % chroms) for j in range(chroms)])
+    peak_out = put(parts - 1, peak_out)
+    peak_out, got = lax.optimization_barrier((peak_out, got))
+    summed = kept + got.astype(jnp.float32)
     return (peak_out.reshape(block_rows, rank_width), summed)
 
 

time: 77.1 us -> 72.1 us (0.935); the launches traced: 76.2 us -> 72.8 us
  waiting for transfers between devices: 27.8 us -> 23.1 us
  starting transfers between devices: 25.2 us -> 29.1 us
  Pallas kernels: 20.9 us -> 17.4 us
  local copies, waits for them, and re-layouts: 0.84 us -> 1.64 us
    pallas_call x4, Pallas kernels: 13.9 us -> 7.76 us  [part_call(): pl.pallas_call(functools.partial(part_kernel, scaling, stratum, part, pea...]
    all_to_all x1, waiting for transfers between devices: 4.64 us -> 0.01 us  [per_device(): lax.all_to_all(grad, 'chrom', 0, 0, axis_index_groups=rings, tiled=True)]
    ppermute x6, starting transfers between devices: 21.7 us -> 25.5 us  [moved(): lax.ppermute(piece, 'cell', [(i, (i + by) % cells) for i in range(cells)])]
    pallas_call x1, Pallas kernels: 4.95 us -> 6.98 us  [per_device(): pl.pallas_call(functools.partial(first_kernel, scaling), grid=(1,), out_s...]
    unnamed x12 -> x14, local copies, waits for them, and re-layouts: 0.84 us -> 1.63 us
    pallas_call x1 -> x2, Pallas kernels: 2.02 us -> 2.64 us  [put(): pl.pallas_call(functools.partial(place_kernel, part), grid=(1,), out_shap...]
  transfers between devices with their start and end apart: 7 -> 8, of which waited for: 5 -> 2; matrix products, arithmetic and copies ran while one was open for 0% -> 0% of each run, Pallas kernels for 21% -> 14%
where the time goes in v5:
time: 72.1 us; the launch traced here: 72.8 us
  starting transfers between devices  29.1 us (40%)
  waiting for transfers between devices  23.1 us (32%)
  Pallas kernels  17.4 us (24%)
  local copies, waits for them, and re-layouts  1.64 us (2%)
  between operations  0.79 us (1%)
  other arithmetic  0.75 us (1%)
    ppermute x6, starting transfers between devices, moved(): lax.ppermute(piece, 'cell', [(i, (i + by) % cells) for i in range(cells)])  25.5 us
    ppermute x6, waiting for transfers between devices, moved(): lax.ppermute(piece, 'cell', [(i, (i + by) % cells) for i in range(cells)])  23.1 us
    pallas_call x4, Pallas kernels, part_call(): pl.pallas_call(functools.partial(part_kernel, scaling, stratum, part, pea...  7.76 us
    pallas_call x1, Pallas kernels, per_device(): pl.pallas_call(functools.partial(first_kernel, scaling), grid=(1,), out_s...  6.98 us
    all_to_all x1, starting transfers between devices, per_device(): lax.all_to_all(grad, 'chrom', 0, 0, axis_index_groups=rings, tiled=True)  3.47 us
    pallas_call x2, Pallas kernels, put(): pl.pallas_call(functools.partial(place_kernel, part), grid=(1,), out_shap...  2.64 us
    unnamed x14, local copies, waits for them, and re-layouts  1.63 us
  transfers between devices with their start and end apart: 8, of which 2 were waited for; matrix products, arithmetic and copies ran while one was open for 0% of the time, Pallas kernels for 14%

profile of v5, /device:TPU:1, one launch (start us, length us, event | category | flops | bytes accessed | tf_op | source)
XLA Modules:
  0.0 72.8 jit_solution(7118432990910049444)
XLA Ops:
  0.6 0.0 copy-start
  0.6 0.0 copy-start.1
  0.7 0.0 copy-start.4
  0.7 0.0 copy-start.5
  0.7 7.0 %shard_map.68 = (bf16[8,128,256]{2,1,0:T(8,128)(2,1)}, bf16[8,128,256]{2,1,0:T(8,128)(2,1)}, f32[8,128,256]{2,1,0:T(8,128)}) custom-call(s32[1,3]{1,0:T(1,128)} %bitcast.13, s32[3,32]{1,0:T(4,128)} %refs_1_.7, bf16[8,128,256]{2,1,0:T(8,128)(2,1)} %bitcast.8, bf16[16,128,256]{2,1,0:T(8,128)(2,1)} %bitcast.19, bf16[3,32,128,128]{3,2,1,0:T(8,128)(2,1)} %refs_3_.7), custom_call_target="tpu_custom_call" | custom-call | flops 805306368 | bytes 4194304 | tf_op jit(solution)/shard_map/pallas_call | solution.py:156
  7.7 2.0 %collective-permute-start.1 = (bf16[8,128,256]{2,1,0:T(8,128)(2,1)}, bf16[8,128,256]{2,1,0:T(8,128)(2,1)S(1)}, u32[]{:S(2)}, u32[]{:S(2)}) collective-permute-start(bf16[8,128,256]{2,1,0:T(8,128)(2,1)} %get-tuple-element.18), channel_id=1, source_target_pairs={{0,248},{8,0},{16,8},{24,16},{32,24},{40,32},{48,40},{56,48},{64,5... | collective-permute-start | bytes 1572872 | tf_op jit(solution)/shard_map/ppermute | solution.py:151
  9.6 7.3 %collective-permute-start = (bf16[8,128,256]{2,1,0:T(8,128)(2,1)}, bf16[8,128,256]{2,1,0:T(8,128)(2,1)S(1)}, u32[]{:S(2)}, u32[]{:S(2)}) collective-permute-start(bf16[8,128,256]{2,1,0:T(8,128)(2,1)} %get-tuple-element.17), channel_id=1, source_target_pairs={{0,248},{8,0},{16,8},{24,16},{32,24},{40,32},{48,40},{56,48},{64,5... | collective-permute-start | bytes 1572872 | tf_op jit(solution)/shard_map/ppermute | solution.py:151
  17.0 0.0 collective-permute-done.1.refs_4_
  17.0 0.0 copy-done
  17.0 0.0 copy-done.1
  17.0 0.0 copy-done.4
  17.0 0.0 copy-done.5
  17.0 1.7 %shard_map.69 = (bf16[8,128,256]{2,1,0:T(8,128)(2,1)S(1)}, f32[9,128,256]{2,1,0:T(8,128)S(1)}) custom-call(s32[1,3]{1,0:T(1,128)S(1)} %bitcast.14, s32[3,32]{1,0:T(4,128)S(1)} %copy-done.4, bf16[8,128,256]{2,1,0:T(8,128)(2,1)S(1)} %bitcast.9, bf16[3,32,128,128]{3,2,1,0:T(8,128)(2,1)S(1)} %copy-done, bf16[8,128,256]{2,1,0:T(8,128)(2,1)S(1)} %collective-permute-done.1.refs_4_), custom_call_target="tpu_custom_call" | custom-call | flops 402653184 | bytes 3145728 | tf_op jit(solution)/shard_map/pallas_call | solution.py:191
  18.7 8.9 %collective-permute-start.3 = (bf16[8,128,256]{2,1,0:T(8,128)(2,1)S(1)}, bf16[8,128,256]{2,1,0:T(8,128)(2,1)S(1)}, u32[]{:S(2)}, u32[]{:S(2)}) collective-permute-start(bf16[8,128,256]{2,1,0:T(8,128)(2,1)S(1)} %get-tuple-element.21), channel_id=1, source_target_pairs={{0,248},{8,0},{16,8},{24,16},{32,24},{40,32},{48,40},{56,48},{64,5... | collective-permute-start | bytes 1572872 | tf_op jit(solution)/shard_map/ppermute | solution.py:151
  27.6 0.0 collective-permute-done.refs_4_
  27.6 1.7 %shard_map.70 = (bf16[8,128,256]{2,1,0:T(8,128)(2,1)S(1)}, f32[9,128,256]{2,1,0:T(8,128)S(1)}) custom-call(s32[1,3]{1,0:T(1,128)S(1)} %bitcast.15, s32[3,32]{1,0:T(4,128)S(1)} %copy-done.4, bf16[8,128,256]{2,1,0:T(8,128)(2,1)S(1)} %bitcast.10, bf16[3,32,128,128]{3,2,1,0:T(8,128)(2,1)S(1)} %copy-done, bf16[8,128,256]{2,1,0:T(8,128)(2,1)S(1)} %collective-permute-done.refs_4_, ...), custom_call_target="tpu_custom_call" | custom-call | flops 402653184 | bytes 3145728 | tf_op jit(solution)/shard_map/pallas_call | solution.py:191
  29.3 6.6 %collective-permute-start.2 = (bf16[8,128,256]{2,1,0:T(8,128)(2,1)S(1)}, bf16[8,128,256]{2,1,0:T(8,128)(2,1)S(1)}, u32[]{:S(2)}, u32[]{:S(2)}) collective-permute-start(bf16[8,128,256]{2,1,0:T(8,128)(2,1)S(1)} %get-tuple-element.20), channel_id=1, source_target_pairs={{0,248},{8,0},{16,8},{24,16},{32,24},{40,32},{48,40},{56,48},{64,5... | collective-permute-start | bytes 1572872 | tf_op jit(solution)/shard_map/ppermute | solution.py:151
  36.0 0.0 collective-permute-done.3.refs_4_
  36.0 0.0 copy-start.2
  36.0 2.5 %shard_map.71 = (bf16[8,128,256]{2,1,0:T(8,128)(2,1)}, f32[9,128,256]{2,1,0:T(8,128)S(1)}) custom-call(s32[1,3]{1,0:T(1,128)S(1)} %bitcast.16, s32[3,32]{1,0:T(4,128)S(1)} %copy-done.4, bf16[8,128,256]{2,1,0:T(8,128)(2,1)S(1)} %bitcast.11, bf16[3,32,128,128]{3,2,1,0:T(8,128)(2,1)S(1)} %copy-done, bf16[8,128,256]{2,1,0:T(8,128)(2,1)S(1)} %collective-permute-done.3.refs_4_, ...), custom_call_target="tpu_custom_call" | custom-call | flops 402653184 | bytes 3145728 | tf_op jit(solution)/shard_map/pallas_call | solution.py:191
  38.5 0.0 collective-permute-start.5
  38.5 0.0 collective-permute-done.2.refs_4_
  38.5 0.0 copy-done.2
  38.5 1.8 %shard_map.72 = (bf16[8,128,256]{2,1,0:T(8,128)(2,1)S(1)}, bf16[4,2,128,256]{3,2,1,0:T(8,128)(2,1)S(1)}) custom-call(s32[1,3]{1,0:T(1,128)S(1)} %bitcast.17, s32[3,32]{1,0:T(4,128)S(1)} %copy-done.4, bf16[8,128,256]{2,1,0:T(8,128)(2,1)S(1)} %bitcast.12, bf16[3,32,128,128]{3,2,1,0:T(8,128)(2,1)S(1)} %copy-done, ...), custom_call_target="tpu_custom_call" | custom-call | flops 402653184 | bytes 3145728 | tf_op jit(solution)/shard_map/pallas_call | solution.py:191
  40.3 0.0 copy-start.3
  40.3 0.8 %copy-done.3 = bf16[4,2,128,256]{3,2,1,0:T(8,128)(2,1)} copy-done((bf16[4,2,128,256]{3,2,1,0:T(8,128)(2,1)}, bf16[4,2,128,256]{3,2,1,0:T(8,128)(2,1)S(1)}, u32[]{:S(2)}) %copy-start.3) | copy-done | bytes 524312
  41.1 0.0 copy-start.6
  41.1 0.8 %copy-done.6 = bf16[8,128,256]{2,1,0:T(8,128)(2,1)} copy-done((bf16[8,128,256]{2,1,0:T(8,128)(2,1)}, bf16[8,128,256]{2,1,0:T(8,128)(2,1)S(1)}, u32[]{:S(2)}) %copy-start.6) | copy-done | bytes 524312
  41.9 3.5 %all-to-all-start = ((bf16[4,2,128,256]{3,2,1,0:T(8,128)(2,1)}), bf16[4,2,128,256]{3,2,1,0:T(8,128)(2,1)S(1)}, u32[]{:S(2)}, u32[]{:S(2)}) async-start(bf16[4,2,128,256]{3,2,1,0:T(8,128)(2,1)} %copy-done.3), calls=%async_computation | async-start | bytes 1048576 | tf_op jit(solution)/shard_map/all_to_all | solution.py:224
  45.4 0.7 collective-permute-start.4
  46.1 13.7 %collective-permute-done.5.piece_ref = bf16[8,128,256]{2,1,0:T(8,128)(2,1)} collective-permute-done((bf16[8,128,256]{2,1,0:T(8,128)(2,1)}, bf16[8,128,256]{2,1,0:T(8,128)(2,1)}, u32[]{:S(2)}, u32[]{:S(2)}) %collective-permute-start.5) | collective-permute-done | bytes 524320 | tf_op jit(solution)/shard_map/ppermute | solution.py:151
  59.8 1.8 %shard_map.73.refs_0_ = bf16[16,128,256]{2,1,0:T(8,128)(2,1)} custom-call(bf16[8,128,256]{2,1,0:T(8,128)(2,1)} %collective-permute-done.5.piece_ref), custom_call_target="tpu_custom_call" | custom-call | bytes 8388608 | tf_op jit(solution)/shard_map/pallas_call | solution.py:211
  61.7 0.0 all-to-all-done
  61.7 0.1 convert_reduce_fusion
  61.8 0.1 collective-permute-start.6
  61.9 9.4 %collective-permute-done.4.piece_ref = bf16[8,128,256]{2,1,0:T(8,128)(2,1)S(1)} collective-permute-done((bf16[8,128,256]{2,1,0:T(8,128)(2,1)}, bf16[8,128,256]{2,1,0:T(8,128)(2,1)S(1)}, u32[]{:S(2)}, u32[]{:S(2)}) %collective-permute-start.4) | collective-permute-done | bytes 524320 | tf_op jit(solution)/shard_map/ppermute | solution.py:151
  71.3 0.8 %shard_map.74 = bf16[16,128,256]{2,1,0:T(8,128)(2,1)} custom-call(bf16[8,128,256]{2,1,0:T(8,128)(2,1)S(1)} %collective-permute-done.4.piece_ref, bf16[16,128,256]{2,1,0:T(8,128)(2,1)} %shard_map.73.refs_0_), custom_call_target="tpu_custom_call", output_to_operand_aliasing={{}: (1, {})} | custom-call | bytes 8388608 | tf_op jit(solution)/shard_map/pallas_call | solution.py:211
  72.1 0.0 collective-permute-done.6
  72.1 0.7 bitcast_add_fusion
  (1 shorter events, 0.0 us)
Async XLA Ops:
  0.6 16.4 %copy-start = (bf16[3,32,128,128]{3,2,1,0:T(8,128)(2,1)S(1)}, bf16[3,32,128,128]{3,2,1,0:T(8,128)(2,1)}, u32[]{:S(2)}) copy-start(bf16[3,32,128,128]{3,2,1,0:T(8,128)(2,1)} %refs_3_.7) | copy-start | bytes 9437188
  0.6 16.3 %copy-start.1 = (bf16[1024,256]{1,0:T(8,128)(2,1)S(1)}, bf16[1024,256]{1,0:T(8,128)(2,1)}, u32[]{:S(2)}) copy-start(bf16[1024,256]{1,0:T(8,128)(2,1)} %param.5) | copy-start | bytes 1572868
  0.7 16.3 %copy-start.4 = (s32[3,32]{1,0:T(4,128)S(1)}, s32[3,32]{1,0:T(4,128)}, u32[]{:S(2)}) copy-start(s32[3,32]{1,0:T(4,128)} %refs_1_.7) | copy-start | bytes 1156
  0.7 16.3 %copy-start.5 = (s32[3,1]{0,1:T(1,128)S(1)}, s32[3,1]{0,1:T(1,128)}, u32[]{:S(2)}) copy-start(s32[3,1]{0,1:T(1,128)} %param.9) | copy-start | bytes 40
  7.7 9.3 %collective-permute-start.1 = (bf16[8,128,256]{2,1,0:T(8,128)(2,1)}, bf16[8,128,256]{2,1,0:T(8,128)(2,1)S(1)}, u32[]{:S(2)}, u32[]{:S(2)}) collective-permute-start(bf16[8,128,256]{2,1,0:T(8,128)(2,1)} %get-tuple-element.18), channel_id=1, source_target_pairs={{0,248},{8,0},{16,8},{24,16},{32,24},{40,32},{48,40},{56,48},{64,5... | collective-permute-start | bytes 1572872 | tf_op jit(solution)/shard_map/ppermute | solution.py:151
  9.6 18.0 %collective-permute-start = (bf16[8,128,256]{2,1,0:T(8,128)(2,1)}, bf16[8,128,256]{2,1,0:T(8,128)(2,1)S(1)}, u32[]{:S(2)}, u32[]{:S(2)}) collective-permute-start(bf16[8,128,256]{2,1,0:T(8,128)(2,1)} %get-tuple-element.17), channel_id=1, source_target_pairs={{0,248},{8,0},{16,8},{24,16},{32,24},{40,32},{48,40},{56,48},{64,5... | collective-permute-start | bytes 1572872 | tf_op jit(solution)/shard_map/ppermute | solution.py:151
  18.7 17.2 %collective-permute-start.3 = (bf16[8,128,256]{2,1,0:T(8,128)(2,1)S(1)}, bf16[8,128,256]{2,1,0:T(8,128)(2,1)S(1)}, u32[]{:S(2)}, u32[]{:S(2)}) collective-permute-start(bf16[8,128,256]{2,1,0:T(8,128)(2,1)S(1)} %get-tuple-element.21), channel_id=1, source_target_pairs={{0,248},{8,0},{16,8},{24,16},{32,24},{40,32},{48,40},{56,48},{64,5... | collective-permute-start | bytes 1572872 | tf_op jit(solution)/shard_map/ppermute | solution.py:151
  29.3 9.2 %collective-permute-start.2 = (bf16[8,128,256]{2,1,0:T(8,128)(2,1)S(1)}, bf16[8,128,256]{2,1,0:T(8,128)(2,1)S(1)}, u32[]{:S(2)}, u32[]{:S(2)}) collective-permute-start(bf16[8,128,256]{2,1,0:T(8,128)(2,1)S(1)} %get-tuple-element.20), channel_id=1, source_target_pairs={{0,248},{8,0},{16,8},{24,16},{32,24},{40,32},{48,40},{56,48},{64,5... | collective-permute-start | bytes 1572872 | tf_op jit(solution)/shard_map/ppermute | solution.py:151
  36.0 2.5 %copy-start.2 = (f32[8,128,256]{2,1,0:T(8,128)S(1)}, f32[8,128,256]{2,1,0:T(8,128)}, u32[]{:S(2)}) copy-start(f32[8,128,256]{2,1,0:T(8,128)} %get-tuple-element.24.refs_6_) | copy-start | bytes 3145732
  38.5 21.3 %collective-permute-start.5 = (bf16[8,128,256]{2,1,0:T(8,128)(2,1)}, bf16[8,128,256]{2,1,0:T(8,128)(2,1)}, u32[]{:S(2)}, u32[]{:S(2)}) collective-permute-start(bf16[8,128,256]{2,1,0:T(8,128)(2,1)} %get-tuple-element.26), channel_id=1, source_target_pairs={{0,16},{8,24},{16,32},{24,40},{32,48},{40,56},{48,64},{56,72},{64,... | collective-permute-start | bytes 1572872 | tf_op jit(solution)/shard_map/ppermute | solution.py:151
  40.3 0.8 %copy-start.3 = (bf16[4,2,128,256]{3,2,1,0:T(8,128)(2,1)}, bf16[4,2,128,256]{3,2,1,0:T(8,128)(2,1)S(1)}, u32[]{:S(2)}) copy-start(bf16[4,2,128,256]{3,2,1,0:T(8,128)(2,1)S(1)} %get-tuple-element.27) | copy-start | bytes 1572868
  41.1 0.8 %copy-start.6 = (bf16[8,128,256]{2,1,0:T(8,128)(2,1)}, bf16[8,128,256]{2,1,0:T(8,128)(2,1)S(1)}, u32[]{:S(2)}) copy-start(bf16[8,128,256]{2,1,0:T(8,128)(2,1)S(1)} %get-tuple-element.25) | copy-start | bytes 1572868
  41.9 19.8 %all-to-all-start = ((bf16[4,2,128,256]{3,2,1,0:T(8,128)(2,1)}), bf16[4,2,128,256]{3,2,1,0:T(8,128)(2,1)S(1)}, u32[]{:S(2)}, u32[]{:S(2)}) async-start(bf16[4,2,128,256]{3,2,1,0:T(8,128)(2,1)} %copy-done.3), calls=%async_computation | async-start | bytes 1048576 | tf_op jit(solution)/shard_map/all_to_all | solution.py:224
  45.4 25.9 %collective-permute-start.4 = (bf16[8,128,256]{2,1,0:T(8,128)(2,1)}, bf16[8,128,256]{2,1,0:T(8,128)(2,1)S(1)}, u32[]{:S(2)}, u32[]{:S(2)}) collective-permute-start(bf16[8,128,256]{2,1,0:T(8,128)(2,1)} %copy-done.6), channel_id=1, source_target_pairs={{0,16},{8,24},{16,32},{24,40},{32,48},{40,56},{48,64},{56,72},{64,... | collective-permute-start | bytes 1572872 | tf_op jit(solution)/shard_map/ppermute | solution.py:151
  61.8 10.3 %collective-permute-start.6 = (bf16[128,256]{1,0:T(8,128)(2,1)S(1)}, bf16[128,256]{1,0:T(8,128)(2,1)S(1)}, u32[]{:S(2)}, u32[]{:S(2)}) collective-permute-start(bf16[128,256]{1,0:T(8,128)(2,1)S(1)} %fusion), channel_id=1, source_target_pairs={{0,4},{1,5},{2,6},{3,7},{4,0},{5,1},{6,2},{7,3},{8,12},{9,13},{10,... | collective-permute-start | bytes 196616 | tf_op jit(solution)/shard_map/ppermute | solution.py:233

commit v6 on v5

--- a/solution.py
+++ b/solution.py
@@ -25,8 +25,8 @@
 
 
 def walk(groups, slot_of, cell_ref, peak_ref, values_at, peak_grad, grad_ref, scaling):
-    def group(g, carry):
-        found = [slot_of(g * group_size + k) for k in range(group_size)]
+    def tiles(start, count):
+        found = [slot_of(start + k) for k in range(count)]
         resids = []
         for t, row, col, _, _ in found:
             predicted = contract(cell_ref[row], peak_ref[col], (1, 1))
@@ -37,9 +37,18 @@
         terms = [contract(r, peak_ref[f[2]], (1, 0)) for r, f in zip(resids, found)]
         for term, f in zip(terms, found):
             grad_ref[f[3]] += term
+
+    pairs = groups // 2
+
+    def pair(g, carry):
+        tiles(g * 2 * group_size, 2 * group_size)
         return carry
 
-    lax.fori_loop(0, groups, group, 0)
+    lax.fori_loop(0, pairs, pair, 0)
+
+    @pl.when(groups > 2 * pairs)
+    def _():
+        tiles(pairs * 2 * group_size, group_size)
 
 
 def stepped(peak, grad, scaling):
@@ -231,9 +240,9 @@
     kept = lax.dynamic_index_in_dim(shares, side, 0, keepdims=False)
     sent = lax.dynamic_index_in_dim(shares, 1 - side, 0, keepdims=False).astype(jnp.bfloat16)
     got = lax.ppermute(sent, "chrom", [(j, (j + near) % chroms) for j in range(chroms)])
+    summed = kept + got.astype(jnp.float32)
+    summed, pieces[-1] = lax.optimization_barrier((summed, pieces[-1]))
     peak_out = put(parts - 1, peak_out)
-    peak_out, got = lax.optimization_barrier((peak_out, got))
-    summed = kept + got.astype(jnp.float32)
     return (peak_out.reshape(block_rows, rank_width), summed)
 
 

time: 72.1 us -> 71.9 us (level)
  waiting for transfers between devices: 23.1 us -> 24.5 us
  Pallas kernels: 17.4 us -> 16.4 us
  starting transfers between devices: 29.1 us -> 28.2 us
    ppermute x1, waiting for transfers between devices: 0.01 us -> 5.71 us  [per_device(): lax.ppermute(sent, 'chrom', [(j, (j + near) % chroms) for j in range(chro...]
    ppermute x6, waiting for transfers between devices: 23.1 us -> 18.8 us  [moved(): lax.ppermute(piece, 'cell', [(i, (i + by) % cells) for i in range(cells)])]
    pallas_call x1, Pallas kernels: 6.98 us -> 4.97 us  [per_device(): pl.pallas_call(functools.partial(first_kernel, scaling), grid=(1,), out_s...]
    ppermute x6, starting transfers between devices: 25.5 us -> 23.7 us  [moved(): lax.ppermute(piece, 'cell', [(i, (i + by) % cells) for i in range(cells)])]
    pallas_call x4, Pallas kernels: 7.76 us -> 8.74 us  [part_call(): pl.pallas_call(functools.partial(part_kernel, scaling, stratum, part, pea...]
    all_to_all x1, starting transfers between devices: 3.47 us -> 4.31 us  [per_device(): lax.all_to_all(grad, 'chrom', 0, 0, axis_index_groups=rings, tiled=True)]
  transfers between devices with their start and end apart: 8 -> 8, of which waited for: 2 -> 4; matrix products, arithmetic and copies ran while one was open for 0% -> 1% of each run, Pallas kernels for 14% -> 15%
where the time goes in v6:
time: 71.9 us; the launch traced here: 72.3 us
  starting transfers between devices  28.2 us (39%)
  waiting for transfers between devices  24.5 us (34%)
  Pallas kernels  16.4 us (23%)
  local copies, waits for them, and re-layouts  1.64 us (2%)
  between operations  0.93 us (1%)
  other arithmetic  0.74 us (1%)
    ppermute x6, starting transfers between devices, moved(): lax.ppermute(piece, 'cell', [(i, (i + by) % cells) for i in range(cells)])  23.7 us
    ppermute x6, waiting for transfers between devices, moved(): lax.ppermute(piece, 'cell', [(i, (i + by) % cells) for i in range(cells)])  18.8 us
    pallas_call x4, Pallas kernels, part_call(): pl.pallas_call(functools.partial(part_kernel, scaling, stratum, part, pea...  8.74 us
    ppermute x1, waiting for transfers between devices, per_device(): lax.ppermute(sent, 'chrom', [(j, (j + near) % chroms) for j in range(chro...  5.71 us
    pallas_call x1, Pallas kernels, per_device(): pl.pallas_call(functools.partial(first_kernel, scaling), grid=(1,), out_s...  4.97 us
    all_to_all x1, starting transfers between devices, per_device(): lax.all_to_all(grad, 'chrom', 0, 0, axis_index_groups=rings, tiled=True)  4.31 us
    pallas_call x2, Pallas kernels, put(): pl.pallas_call(functools.partial(place_kernel, part), grid=(1,), out_shap...  2.64 us
    unnamed x14, local copies, waits for them, and re-layouts  1.63 us
  transfers between devices with their start and end apart: 8, of which 4 were waited for; matrix products, arithmetic and copies ran while one was open for 1% of the time, Pallas kernels for 15%

profile of v6, /device:TPU:1, one launch (start us, length us, event | category | flops | bytes accessed | tf_op | source)
XLA Modules:
  0.0 72.3 jit_solution(13812432598283252429)
XLA Ops:
  0.6 0.0 copy-start
  0.6 0.0 copy-start.1
  0.7 0.0 copy-start.4
  0.7 0.0 copy-start.5
  0.7 5.0 %shard_map.68 = (bf16[8,128,256]{2,1,0:T(8,128)(2,1)}, bf16[8,128,256]{2,1,0:T(8,128)(2,1)}, f32[8,128,256]{2,1,0:T(8,128)}) custom-call(s32[1,3]{1,0:T(1,128)} %bitcast.13, s32[3,32]{1,0:T(4,128)} %refs_1_.7, bf16[8,128,256]{2,1,0:T(8,128)(2,1)} %bitcast.8, bf16[16,128,256]{2,1,0:T(8,128)(2,1)} %bitcast.19, bf16[3,32,128,128]{3,2,1,0:T(8,128)(2,1)} %refs_3_.7), custom_call_target="tpu_custom_call" | custom-call | flops 805306368 | bytes 4194304 | tf_op jit(solution)/shard_map/pallas_call | solution.py:165
  5.6 3.7 %collective-permute-start = (bf16[8,128,256]{2,1,0:T(8,128)(2,1)}, bf16[8,128,256]{2,1,0:T(8,128)(2,1)S(1)}, u32[]{:S(2)}, u32[]{:S(2)}) collective-permute-start(bf16[8,128,256]{2,1,0:T(8,128)(2,1)} %get-tuple-element.17), channel_id=1, source_target_pairs={{0,248},{8,0},{16,8},{24,16},{32,24},{40,32},{48,40},{56,48},{64,5... | collective-permute-start | bytes 1572872 | tf_op jit(solution)/shard_map/ppermute | solution.py:160
  9.3 7.0 %collective-permute-start.2 = (bf16[8,128,256]{2,1,0:T(8,128)(2,1)}, bf16[8,128,256]{2,1,0:T(8,128)(2,1)S(1)}, u32[]{:S(2)}, u32[]{:S(2)}) collective-permute-start(bf16[8,128,256]{2,1,0:T(8,128)(2,1)} %get-tuple-element.19), channel_id=1, source_target_pairs={{0,248},{8,0},{16,8},{24,16},{32,24},{40,32},{48,40},{56,48},{64,5... | collective-permute-start | bytes 1572872 | tf_op jit(solution)/shard_map/ppermute | solution.py:160
  16.3 0.8 %collective-permute-done.refs_4_ = bf16[8,128,256]{2,1,0:T(8,128)(2,1)S(1)} collective-permute-done((bf16[8,128,256]{2,1,0:T(8,128)(2,1)}, bf16[8,128,256]{2,1,0:T(8,128)(2,1)S(1)}, u32[]{:S(2)}, u32[]{:S(2)}) %collective-permute-start) | collective-permute-done | bytes 524320 | tf_op jit(solution)/shard_map/ppermute | solution.py:160
  17.2 0.0 copy-done
  17.2 0.0 copy-done.1
  17.2 0.0 copy-done.4
  17.2 0.0 copy-done.5
  17.2 2.2 %shard_map.69 = (bf16[8,128,256]{2,1,0:T(8,128)(2,1)S(1)}, f32[9,128,256]{2,1,0:T(8,128)S(1)}) custom-call(s32[1,3]{1,0:T(1,128)S(1)} %bitcast.14, s32[3,32]{1,0:T(4,128)S(1)} %copy-done.4, bf16[8,128,256]{2,1,0:T(8,128)(2,1)S(1)} %bitcast.9, bf16[3,32,128,128]{3,2,1,0:T(8,128)(2,1)S(1)} %copy-done, bf16[8,128,256]{2,1,0:T(8,128)(2,1)S(1)} %collective-permute-done.refs_4_), custom_call_target="tpu_custom_call" | custom-call | flops 402653184 | bytes 3145728 | tf_op jit(solution)/shard_map/pallas_call | solution.py:200
  19.4 5.9 %collective-permute-start.1 = (bf16[8,128,256]{2,1,0:T(8,128)(2,1)S(1)}, bf16[8,128,256]{2,1,0:T(8,128)(2,1)S(1)}, u32[]{:S(2)}, u32[]{:S(2)}) collective-permute-start(bf16[8,128,256]{2,1,0:T(8,128)(2,1)S(1)} %get-tuple-element.18), channel_id=1, source_target_pairs={{0,248},{8,0},{16,8},{24,16},{32,24},{40,32},{48,40},{56,48},{64,5... | collective-permute-start | bytes 1572872 | tf_op jit(solution)/shard_map/ppermute | solution.py:160
  25.3 0.0 collective-permute-done.2.refs_4_
  25.3 1.9 %shard_map.70 = (bf16[8,128,256]{2,1,0:T(8,128)(2,1)S(1)}, f32[9,128,256]{2,1,0:T(8,128)S(1)}) custom-call(s32[1,3]{1,0:T(1,128)S(1)} %bitcast.15, s32[3,32]{1,0:T(4,128)S(1)} %copy-done.4, bf16[8,128,256]{2,1,0:T(8,128)(2,1)S(1)} %bitcast.10, bf16[3,32,128,128]{3,2,1,0:T(8,128)(2,1)S(1)} %copy-done, ...), custom_call_target="tpu_custom_call" | custom-call | flops 402653184 | bytes 3145728 | tf_op jit(solution)/shard_map/pallas_call | solution.py:200
  27.2 7.2 %collective-permute-start.4 = (bf16[8,128,256]{2,1,0:T(8,128)(2,1)S(1)}, bf16[8,128,256]{2,1,0:T(8,128)(2,1)S(1)}, u32[]{:S(2)}, u32[]{:S(2)}) collective-permute-start(bf16[8,128,256]{2,1,0:T(8,128)(2,1)S(1)} %get-tuple-element.23), channel_id=1, source_target_pairs={{0,248},{8,0},{16,8},{24,16},{32,24},{40,32},{48,40},{56,48},{64,5... | collective-permute-start | bytes 1572872 | tf_op jit(solution)/shard_map/ppermute | solution.py:160
  34.4 0.0 collective-permute-done.1.refs_4_
  34.4 0.0 copy-start.2
  34.4 2.7 %shard_map.71 = (bf16[8,128,256]{2,1,0:T(8,128)(2,1)}, f32[9,128,256]{2,1,0:T(8,128)S(1)}) custom-call(s32[1,3]{1,0:T(1,128)S(1)} %bitcast.16, s32[3,32]{1,0:T(4,128)S(1)} %copy-done.4, bf16[8,128,256]{2,1,0:T(8,128)(2,1)S(1)} %bitcast.11, bf16[3,32,128,128]{3,2,1,0:T(8,128)(2,1)S(1)} %copy-done, bf16[8,128,256]{2,1,0:T(8,128)(2,1)S(1)} %collective-permute-done.1.refs_4_, ...), custom_call_target="tpu_custom_call" | custom-call | flops 402653184 | bytes 3145728 | tf_op jit(solution)/shard_map/pallas_call | solution.py:200
  37.0 0.0 collective-permute-start.3
  37.0 0.0 collective-permute-done.4.refs_4_
  37.1 0.0 copy-done.2
  37.1 2.0 %shard_map.73 = (bf16[8,128,256]{2,1,0:T(8,128)(2,1)S(1)}, bf16[4,2,128,256]{3,2,1,0:T(8,128)(2,1)S(1)}) custom-call(s32[1,3]{1,0:T(1,128)S(1)} %bitcast.17, s32[3,32]{1,0:T(4,128)S(1)} %copy-done.4, bf16[8,128,256]{2,1,0:T(8,128)(2,1)S(1)} %bitcast.12, bf16[3,32,128,128]{3,2,1,0:T(8,128)(2,1)S(1)} %copy-done, ...), custom_call_target="tpu_custom_call" | custom-call | flops 402653184 | bytes 3145728 | tf_op jit(solution)/shard_map/pallas_call | solution.py:200
  39.0 0.0 copy-start.3
  39.0 0.8 %copy-done.3 = bf16[4,2,128,256]{3,2,1,0:T(8,128)(2,1)} copy-done((bf16[4,2,128,256]{3,2,1,0:T(8,128)(2,1)}, bf16[4,2,128,256]{3,2,1,0:T(8,128)(2,1)S(1)}, u32[]{:S(2)}) %copy-start.3) | copy-done | bytes 524312
  39.9 0.0 copy-start.6
  39.9 0.8 %copy-done.6 = bf16[8,128,256]{2,1,0:T(8,128)(2,1)} copy-done((bf16[8,128,256]{2,1,0:T(8,128)(2,1)}, bf16[8,128,256]{2,1,0:T(8,128)(2,1)S(1)}, u32[]{:S(2)}) %copy-start.6) | copy-done | bytes 524312
  40.7 4.3 %all-to-all-start = ((bf16[4,2,128,256]{3,2,1,0:T(8,128)(2,1)}), bf16[4,2,128,256]{3,2,1,0:T(8,128)(2,1)S(1)}, u32[]{:S(2)}, u32[]{:S(2)}) async-start(bf16[4,2,128,256]{3,2,1,0:T(8,128)(2,1)} %copy-done.3), calls=%async_computation | async-start | bytes 1048576 | tf_op jit(solution)/shard_map/all_to_all | solution.py:233
  45.0 0.0 collective-permute-start.6
  45.0 15.6 %collective-permute-done.3.piece_ref = bf16[8,128,256]{2,1,0:T(8,128)(2,1)} collective-permute-done((bf16[8,128,256]{2,1,0:T(8,128)(2,1)}, bf16[8,128,256]{2,1,0:T(8,128)(2,1)}, u32[]{:S(2)}, u32[]{:S(2)}) %collective-permute-start.3) | collective-permute-done | bytes 524320 | tf_op jit(solution)/shard_map/ppermute | solution.py:160
  60.6 1.8 %shard_map.72.refs_0_ = bf16[16,128,256]{2,1,0:T(8,128)(2,1)} custom-call(bf16[8,128,256]{2,1,0:T(8,128)(2,1)} %collective-permute-done.3.piece_ref), custom_call_target="tpu_custom_call" | custom-call | bytes 8388608 | tf_op jit(solution)/shard_map/pallas_call | solution.py:220
  62.4 0.0 all-to-all-done
  62.4 0.1 convert_reduce_fusion
  62.5 0.1 collective-permute-start.5
  62.6 5.7 %collective-permute-done.5 = bf16[128,256]{1,0:T(8,128)(2,1)S(1)} collective-permute-done((bf16[128,256]{1,0:T(8,128)(2,1)S(1)}, bf16[128,256]{1,0:T(8,128)(2,1)S(1)}, u32[]{:S(2)}, u32[]{:S(2)}) %collective-permute-start.5) | collective-permute-done | bytes 65568 | tf_op jit(solution)/shard_map/ppermute | solution.py:242
  68.4 0.7 bitcast_add_fusion
  69.0 2.3 %collective-permute-done.6.piece_ref = bf16[8,128,256]{2,1,0:T(8,128)(2,1)S(1)} collective-permute-done((bf16[8,128,256]{2,1,0:T(8,128)(2,1)}, bf16[8,128,256]{2,1,0:T(8,128)(2,1)S(1)}, u32[]{:S(2)}, u32[]{:S(2)}) %collective-permute-start.6) | collective-permute-done | bytes 524320 | tf_op jit(solution)/shard_map/ppermute | solution.py:160
  71.4 0.8 %shard_map.74 = bf16[16,128,256]{2,1,0:T(8,128)(2,1)} custom-call(bf16[8,128,256]{2,1,0:T(8,128)(2,1)S(1)} %collective-permute-done.6.piece_ref, bf16[16,128,256]{2,1,0:T(8,128)(2,1)} %shard_map.72.refs_0_), custom_call_target="tpu_custom_call", output_to_operand_aliasing={{}: (1, {})} | custom-call | bytes 8388608 | tf_op jit(solution)/shard_map/pallas_call | solution.py:220
  (1 shorter events, 0.0 us)
Async XLA Ops:
  0.6 16.5 %copy-start = (bf16[3,32,128,128]{3,2,1,0:T(8,128)(2,1)S(1)}, bf16[3,32,128,128]{3,2,1,0:T(8,128)(2,1)}, u32[]{:S(2)}) copy-start(bf16[3,32,128,128]{3,2,1,0:T(8,128)(2,1)} %refs_3_.7) | copy-start | bytes 9437188
  0.6 16.5 %copy-start.1 = (bf16[1024,256]{1,0:T(8,128)(2,1)S(1)}, bf16[1024,256]{1,0:T(8,128)(2,1)}, u32[]{:S(2)}) copy-start(bf16[1024,256]{1,0:T(8,128)(2,1)} %param.5) | copy-start | bytes 1572868
  0.7 16.5 %copy-start.4 = (s32[3,32]{1,0:T(4,128)S(1)}, s32[3,32]{1,0:T(4,128)}, u32[]{:S(2)}) copy-start(s32[3,32]{1,0:T(4,128)} %refs_1_.7) | copy-start | bytes 1156
  0.7 16.5 %copy-start.5 = (s32[3,1]{0,1:T(1,128)S(1)}, s32[3,1]{0,1:T(1,128)}, u32[]{:S(2)}) copy-start(s32[3,1]{0,1:T(1,128)} %param.9) | copy-start | bytes 40
  5.6 11.5 %collective-permute-start = (bf16[8,128,256]{2,1,0:T(8,128)(2,1)}, bf16[8,128,256]{2,1,0:T(8,128)(2,1)S(1)}, u32[]{:S(2)}, u32[]{:S(2)}) collective-permute-start(bf16[8,128,256]{2,1,0:T(8,128)(2,1)} %get-tuple-element.17), channel_id=1, source_target_pairs={{0,248},{8,0},{16,8},{24,16},{32,24},{40,32},{48,40},{56,48},{64,5... | collective-permute-start | bytes 1572872 | tf_op jit(solution)/shard_map/ppermute | solution.py:160
  9.3 16.0 %collective-permute-start.2 = (bf16[8,128,256]{2,1,0:T(8,128)(2,1)}, bf16[8,128,256]{2,1,0:T(8,128)(2,1)S(1)}, u32[]{:S(2)}, u32[]{:S(2)}) collective-permute-start(bf16[8,128,256]{2,1,0:T(8,128)(2,1)} %get-tuple-element.19), channel_id=1, source_target_pairs={{0,248},{8,0},{16,8},{24,16},{32,24},{40,32},{48,40},{56,48},{64,5... | collective-permute-start | bytes 1572872 | tf_op jit(solution)/shard_map/ppermute | solution.py:160
  19.4 14.9 %collective-permute-start.1 = (bf16[8,128,256]{2,1,0:T(8,128)(2,1)S(1)}, bf16[8,128,256]{2,1,0:T(8,128)(2,1)S(1)}, u32[]{:S(2)}, u32[]{:S(2)}) collective-permute-start(bf16[8,128,256]{2,1,0:T(8,128)(2,1)S(1)} %get-tuple-element.18), channel_id=1, source_target_pairs={{0,248},{8,0},{16,8},{24,16},{32,24},{40,32},{48,40},{56,48},{64,5... | collective-permute-start | bytes 1572872 | tf_op jit(solution)/shard_map/ppermute | solution.py:160
  27.2 9.9 %collective-permute-start.4 = (bf16[8,128,256]{2,1,0:T(8,128)(2,1)S(1)}, bf16[8,128,256]{2,1,0:T(8,128)(2,1)S(1)}, u32[]{:S(2)}, u32[]{:S(2)}) collective-permute-start(bf16[8,128,256]{2,1,0:T(8,128)(2,1)S(1)} %get-tuple-element.23), channel_id=1, source_target_pairs={{0,248},{8,0},{16,8},{24,16},{32,24},{40,32},{48,40},{56,48},{64,5... | collective-permute-start | bytes 1572872 | tf_op jit(solution)/shard_map/ppermute | solution.py:160
  34.4 2.7 %copy-start.2 = (f32[8,128,256]{2,1,0:T(8,128)S(1)}, f32[8,128,256]{2,1,0:T(8,128)}, u32[]{:S(2)}) copy-start(f32[8,128,256]{2,1,0:T(8,128)} %get-tuple-element.25.refs_6_) | copy-start | bytes 3145732
  37.0 23.5 %collective-permute-start.3 = (bf16[8,128,256]{2,1,0:T(8,128)(2,1)}, bf16[8,128,256]{2,1,0:T(8,128)(2,1)}, u32[]{:S(2)}, u32[]{:S(2)}) collective-permute-start(bf16[8,128,256]{2,1,0:T(8,128)(2,1)} %get-tuple-element.22), channel_id=1, source_target_pairs={{0,16},{8,24},{16,32},{24,40},{32,48},{40,56},{48,64},{56,72},{64,... | collective-permute-start | bytes 1572872 | tf_op jit(solution)/shard_map/ppermute | solution.py:160
  39.0 0.8 %copy-start.3 = (bf16[4,2,128,256]{3,2,1,0:T(8,128)(2,1)}, bf16[4,2,128,256]{3,2,1,0:T(8,128)(2,1)S(1)}, u32[]{:S(2)}) copy-start(bf16[4,2,128,256]{3,2,1,0:T(8,128)(2,1)S(1)} %get-tuple-element.26) | copy-start | bytes 1572868
  39.9 0.8 %copy-start.6 = (bf16[8,128,256]{2,1,0:T(8,128)(2,1)}, bf16[8,128,256]{2,1,0:T(8,128)(2,1)S(1)}, u32[]{:S(2)}) copy-start(bf16[8,128,256]{2,1,0:T(8,128)(2,1)S(1)} %get-tuple-element.28) | copy-start | bytes 1572868
  40.7 21.8 %all-to-all-start = ((bf16[4,2,128,256]{3,2,1,0:T(8,128)(2,1)}), bf16[4,2,128,256]{3,2,1,0:T(8,128)(2,1)S(1)}, u32[]{:S(2)}, u32[]{:S(2)}) async-start(bf16[4,2,128,256]{3,2,1,0:T(8,128)(2,1)} %copy-done.3), calls=%async_computation | async-start | bytes 1048576 | tf_op jit(solution)/shard_map/all_to_all | solution.py:233
  45.0 26.4 %collective-permute-start.6 = (bf16[8,128,256]{2,1,0:T(8,128)(2,1)}, bf16[8,128,256]{2,1,0:T(8,128)(2,1)S(1)}, u32[]{:S(2)}, u32[]{:S(2)}) collective-permute-start(bf16[8,128,256]{2,1,0:T(8,128)(2,1)} %copy-done.6), channel_id=1, source_target_pairs={{0,16},{8,24},{16,32},{24,40},{32,48},{40,56},{48,64},{56,72},{64,... | collective-permute-start | bytes 1572872 | tf_op jit(solution)/shard_map/ppermute | solution.py:160
  62.5 5.8 %collective-permute-start.5 = (bf16[128,256]{1,0:T(8,128)(2,1)S(1)}, bf16[128,256]{1,0:T(8,128)(2,1)S(1)}, u32[]{:S(2)}, u32[]{:S(2)}) collective-permute-start(bf16[128,256]{1,0:T(8,128)(2,1)S(1)} %fusion), channel_id=1, source_target_pairs={{0,4},{1,5},{2,6},{3,7},{4,0},{5,1},{6,2},{7,3},{8,12},{9,13},{10,... | collective-permute-start | bytes 196616 | tf_op jit(solution)/shard_map/ppermute | solution.py:242

commit v7 on v6

--- a/solution.py
+++ b/solution.py
@@ -31,12 +31,14 @@
         for t, row, col, _, _ in found:
             predicted = contract(cell_ref[row], peak_ref[col], (1, 1))
             resids.append((predicted * scaling - values_at(t).astype(jnp.float32)).astype(jnp.bfloat16))
-        terms = [contract(r, cell_ref[f[1]], (0, 0)) for r, f in zip(resids, found)]
-        for term, f in zip(terms, found):
-            peak_grad[f[4]] += term
-        terms = [contract(r, peak_ref[f[2]], (1, 0)) for r, f in zip(resids, found)]
-        for term, f in zip(terms, found):
-            grad_ref[f[3]] += term
+        if peak_grad is not None:
+            terms = [contract(r, cell_ref[f[1]], (0, 0)) for r, f in zip(resids, found)]
+            for term, f in zip(terms, found):
+                peak_grad[f[4]] += term
+        if grad_ref is not None:
+            terms = [contract(r, peak_ref[f[2]], (1, 0)) for r, f in zip(resids, found)]
+            for term, f in zip(terms, found):
+                grad_ref[f[3]] += term
 
     pairs = groups // 2
 
@@ -56,7 +58,7 @@
 
 
 def first_kernel(scaling, counts, index, cell_in, peak_in, values_in, *refs):
-    news, (grad_ref, cell_ref, peak_ref, values_ref, peak_grad, sems) = refs[:parts], refs[parts:]
+    news, (cell_ref, peak_ref, values_ref, peak_grad, sems) = refs[:parts], refs[parts:]
     peak_tiles = peak_ref.shape[0]
     loads = [
         pltpu.make_async_copy(cell_in, cell_ref, sems.at[0]),
@@ -66,7 +68,6 @@
     for copy in loads:
         copy.start()
     peak_grad[...] = jnp.zeros_like(peak_grad)
-    grad_ref[...] = jnp.zeros_like(grad_ref)
     for copy in loads:
         copy.wait()
 
@@ -76,10 +77,23 @@
         return t, row, col, row, col
 
     groups = counts[0, 0] // group_size
-    walk(groups, slot_of, cell_ref, peak_ref, lambda t: values_ref[t], peak_grad, grad_ref, scaling)
+    walk(groups, slot_of, cell_ref, peak_ref, lambda t: values_ref[t], peak_grad, None, scaling)
     own_tiles = peak_tiles // parts
     for c in range(peak_tiles):
         news[c // own_tiles][c % own_tiles] = stepped(peak_ref[c], peak_grad[c], scaling)
+
+
+def cell_kernel(scaling, counts, index, cell_ref, peak_ref, values, grad_ref):
+    peak_tiles = peak_ref.shape[0]
+    grad_ref[...] = jnp.zeros_like(grad_ref)
+
+    def slot_of(t):
+        place = index[0, t]
+        row, col = place // peak_tiles, place % peak_tiles
+        return t, row, col, row, col
+
+    groups = counts[0, 0] // group_size
+    walk(groups, slot_of, cell_ref, peak_ref, lambda t: values[0, t], None, grad_ref, scaling)
 
 
 def part_kernel(scaling, stratum, part, peak_tiles, closing, fresh, *refs):
@@ -88,7 +102,7 @@
     if not fresh:
         given, *rest = rest
     if closing:
-        early, new_ref, out_ref, grad_ref, peak_grad, places = rest
+        new_ref, out_ref, grad_ref, peak_grad, places = rest
     else:
         new_ref, grad_ref, peak_grad, places = rest
     own_tiles = peak_ref.shape[0]
@@ -122,7 +136,7 @@
     if closing:
         near = out_ref.shape[0]
         for r in range(row_tiles):
-            out_ref[r % near, r // near] = ((early[r] + grad_ref[r]) * (gradient_scale * scaling)).astype(out_ref.dtype)
+            out_ref[r % near, r // near] = (grad_ref[r] * (gradient_scale * scaling)).astype(out_ref.dtype)
 
 
 def place_kernel(part, piece_ref, *refs):
@@ -162,12 +176,12 @@
     piece_out = jax.ShapeDtypeStruct((own_tiles, tile_size, rank_width), jnp.bfloat16)
     grad_out = jax.ShapeDtypeStruct((row_tiles + 1, tile_size, rank_width), jnp.float32)
 
-    *pieces, early = pl.pallas_call(
+    pieces = pl.pallas_call(
         functools.partial(first_kernel, scaling),
         grid=(1,),
-        out_shape=(piece_out,) * parts + (jax.ShapeDtypeStruct(cell_blocks.shape, jnp.float32),),
+        out_shape=(piece_out,) * parts,
         in_specs=[smem, smem, far, far, far],
-        out_specs=(vmem,) * (parts + 1),
+        out_specs=(vmem,) * parts,
         scratch_shapes=[
             pltpu.VMEM(cell_blocks.shape, jnp.bfloat16),
             pltpu.VMEM(peak_block.shape, jnp.bfloat16),
@@ -179,6 +193,16 @@
         cost_estimate=cost(flops, 4 * mebi),
     )(counts, tile_index, cell_blocks, peak_block, tile_values)
     pieces = [moved(piece, -1) for piece in pieces]
+    first_values = pl.BlockSpec((1,) + tile_values.shape[1:], lambda i: (0, 0, 0, 0))
+    grad = pl.pallas_call(
+        functools.partial(cell_kernel, scaling),
+        grid=(1,),
+        out_shape=grad_out,
+        in_specs=[smem, smem, vmem, vmem, first_values],
+        out_specs=vmem,
+        compiler_params=pltpu.CompilerParams(vmem_limit_bytes=16 * mebi),
+        cost_estimate=cost(flops, 4 * mebi),
+    )(counts, tile_index, cell_blocks, peak_block, tile_values)
 
     def part_call(stratum, part, piece, given, closing):
         own_values = pl.BlockSpec((1,) + tile_values.shape[1:], lambda i: (stratum, 0, 0, 0))
@@ -186,8 +210,6 @@
         in_specs = [smem, smem, vmem, own_values, vmem]
         if given is not None:
             args.append(given)
-        if closing:
-            args.append(early)
         in_specs += [vmem] * (len(args) - len(in_specs))
         scratch = [
             pltpu.VMEM((own_tiles + 1, tile_size, rank_width), jnp.float32),
@@ -208,7 +230,6 @@
             cost_estimate=cost(flops // parts, 3 * mebi),
         )(*args)
 
-    grad = None
     for stratum in range(1, strata):
         for part in range(parts):
             closing = stratum == last and part == parts - 1

time: 71.9 us -> 70.7 us (0.983)
  starting transfers between devices: 28.2 us -> 23.3 us
  Pallas kernels: 16.4 us -> 19.7 us
  waiting for transfers between devices: 24.5 us -> 23.2 us
  local copies, waits for them, and re-layouts: 1.64 us -> 2.87 us
    ppermute x6, starting transfers between devices: 23.7 us -> 17.7 us  [moved(): lax.ppermute(piece, 'cell', [(i, (i + by) % cells) for i in range(cells)])]
    ppermute x6, waiting for transfers between devices: 18.8 us -> 14 us  [moved(): lax.ppermute(piece, 'cell', [(i, (i + by) % cells) for i in range(cells)])]
    ppermute x1, waiting for transfers between devices: 5.71 us -> 9.22 us  [per_device(): lax.ppermute(sent, 'chrom', [(j, (j + near) % chroms) for j in range(chro...]
    pallas_call x0 -> x1, Pallas kernels: none -> 2.12 us  [per_device(): pl.pallas_call(functools.partial(cell_kernel, scaling), grid=(1,), out_sh...]
    unnamed x14, local copies, waits for them, and re-layouts: 1.63 us -> 2.86 us
    all_to_all x1, starting transfers between devices: 4.31 us -> 5.53 us  [per_device(): lax.all_to_all(grad, 'chrom', 0, 0, axis_index_groups=rings, tiled=True)]
    pallas_call x4, Pallas kernels: 8.74 us -> 9.52 us  [part_call(): pl.pallas_call(functools.partial(part_kernel, scaling, stratum, part, pea...]
  transfers between devices with their start and end apart: 8 -> 8, of which waited for: 4 -> 2; matrix products, arithmetic and copies ran while one was open for 1% -> 1% of each run, Pallas kernels for 15% -> 19%
where the time goes in v7:
time: 70.7 us; the launch traced here: 70.8 us
  starting transfers between devices  23.3 us (33%)
  waiting for transfers between devices  23.2 us (33%)
  Pallas kernels  19.7 us (28%)
  local copies, waits for them, and re-layouts  2.87 us (4%)
  between operations  0.94 us (1%)
  other arithmetic  0.74 us (1%)
    ppermute x6, starting transfers between devices, moved(): lax.ppermute(piece, 'cell', [(i, (i + by) % cells) for i in range(cells)])  17.7 us
    ppermute x6, waiting for transfers between devices, moved(): lax.ppermute(piece, 'cell', [(i, (i + by) % cells) for i in range(cells)])  14 us
    pallas_call x4, Pallas kernels, part_call(): pl.pallas_call(functools.partial(part_kernel, scaling, stratum, part, pea...  9.52 us
    ppermute x1, waiting for transfers between devices, per_device(): lax.ppermute(sent, 'chrom', [(j, (j + near) % chroms) for j in range(chro...  9.22 us
    all_to_all x1, starting transfers between devices, per_device(): lax.all_to_all(grad, 'chrom', 0, 0, axis_index_groups=rings, tiled=True)  5.53 us
    pallas_call x1, Pallas kernels, per_device(): pl.pallas_call(functools.partial(first_kernel, scaling), grid=(1,), out_s...  5.41 us
    unnamed x14, local copies, waits for them, and re-layouts  2.86 us
    pallas_call x2, Pallas kernels, put(): pl.pallas_call(functools.partial(place_kernel, part), grid=(1,), out_shap...  2.64 us
  transfers between devices with their start and end apart: 8, of which 2 were waited for; matrix products, arithmetic and copies ran while one was open for 1% of the time, Pallas kernels for 19%

profile of v7, /device:TPU:1, one launch (start us, length us, event | category | flops | bytes accessed | tf_op | source)
XLA Modules:
  0.0 70.8 jit_solution(2120896459822808768)
XLA Ops:
  0.6 0.0 copy-start
  0.6 0.0 copy-start.1
  0.7 0.0 copy-start.4
  0.7 0.0 copy-start.5
  0.7 5.4 %shard_map.68 = (bf16[8,128,256]{2,1,0:T(8,128)(2,1)}, bf16[8,128,256]{2,1,0:T(8,128)(2,1)}) custom-call(s32[1,3]{1,0:T(1,128)} %bitcast.16, s32[3,32]{1,0:T(4,128)} %refs_1_.7, bf16[8,128,256]{2,1,0:T(8,128)(2,1)} %bitcast.8, bf16[16,128,256]{2,1,0:T(8,128)(2,1)} %bitcast.14, bf16[3,32,128,128]{3,2,1,0:T(8,128)(2,1)} %refs_3_.7), custom_call_target="tpu_custom_call" | custom-call | flops 805306368 | bytes 4194304 | tf_op jit(solution)/shard_map/pallas_call | solution.py:179
  6.1 3.3 %collective-permute-start = (bf16[8,128,256]{2,1,0:T(8,128)(2,1)}, bf16[8,128,256]{2,1,0:T(8,128)(2,1)S(1)}, u32[]{:S(2)}, u32[]{:S(2)}) collective-permute-start(bf16[8,128,256]{2,1,0:T(8,128)(2,1)} %get-tuple-element.16), channel_id=1, source_target_pairs={{0,248},{8,0},{16,8},{24,16},{32,24},{40,32},{48,40},{56,48},{64,5... | collective-permute-start | bytes 1572872 | tf_op jit(solution)/shard_map/ppermute | solution.py:174
  9.4 5.3 %collective-permute-start.2 = (bf16[8,128,256]{2,1,0:T(8,128)(2,1)}, bf16[8,128,256]{2,1,0:T(8,128)(2,1)S(1)}, u32[]{:S(2)}, u32[]{:S(2)}) collective-permute-start(bf16[8,128,256]{2,1,0:T(8,128)(2,1)} %get-tuple-element.18), channel_id=1, source_target_pairs={{0,248},{8,0},{16,8},{24,16},{32,24},{40,32},{48,40},{56,48},{64,5... | collective-permute-start | bytes 1572872 | tf_op jit(solution)/shard_map/ppermute | solution.py:174
  14.7 0.0 copy-done
  14.7 0.0 copy-done.1
  14.7 0.0 copy-done.4
  14.7 0.0 copy-done.5
  14.7 0.0 copy-start.2
  14.7 1.2 %copy-done.2 = bf16[2048,256]{1,0:T(8,128)(2,1)S(1)} copy-done((bf16[2048,256]{1,0:T(8,128)(2,1)S(1)}, bf16[2048,256]{1,0:T(8,128)(2,1)}, u32[]{:S(2)}) %copy-start.2) | copy-done | bytes 1048600
  15.9 2.1 %shard_map.69.refs_5_ = f32[9,128,256]{2,1,0:T(8,128)S(1)} custom-call(s32[1,3]{1,0:T(1,128)S(1)} %bitcast.17, s32[3,32]{1,0:T(4,128)S(1)} %copy-done.4, bf16[8,128,256]{2,1,0:T(8,128)(2,1)S(1)} %bitcast.9, bf16[16,128,256]{2,1,0:T(8,128)(2,1)S(1)} %bitcast.15, bf16[3,32,128,128]{3,2,1,0:T(8,128)(2,1)S(1)} %copy-done), custom_call_target="tpu_custom_call" | custom-call | flops 805306368 | bytes 4194304 | tf_op jit(solution)/shard_map/pallas_call | solution.py:197
  18.1 0.0 collective-permute-done.refs_4_
  18.1 2.5 %shard_map.70 = (bf16[8,128,256]{2,1,0:T(8,128)(2,1)S(1)}, f32[9,128,256]{2,1,0:T(8,128)S(1)}) custom-call(s32[1,3]{1,0:T(1,128)S(1)} %bitcast.18, s32[3,32]{1,0:T(4,128)S(1)} %copy-done.4, bf16[8,128,256]{2,1,0:T(8,128)(2,1)S(1)} %bitcast.10, bf16[3,32,128,128]{3,2,1,0:T(8,128)(2,1)S(1)} %copy-done, bf16[8,128,256]{2,1,0:T(8,128)(2,1)S(1)} %collective-permute-done.refs_4_, ...), custom_call_target="tpu_custom_call" | custom-call | flops 402653184 | bytes 3145728 | tf_op jit(solution)/shard_map/pallas_call | solution.py:222
  20.6 2.9 %collective-permute-start.1 = (bf16[8,128,256]{2,1,0:T(8,128)(2,1)S(1)}, bf16[8,128,256]{2,1,0:T(8,128)(2,1)S(1)}, u32[]{:S(2)}, u32[]{:S(2)}) collective-permute-start(bf16[8,128,256]{2,1,0:T(8,128)(2,1)S(1)} %get-tuple-element.17), channel_id=1, source_target_pairs={{0,248},{8,0},{16,8},{24,16},{32,24},{40,32},{48,40},{56,48},{64,5... | collective-permute-start | bytes 1572872 | tf_op jit(solution)/shard_map/ppermute | solution.py:174
  23.5 0.0 collective-permute-done.2.refs_4_
  23.5 2.5 %shard_map.71 = (bf16[8,128,256]{2,1,0:T(8,128)(2,1)S(1)}, f32[9,128,256]{2,1,0:T(8,128)S(1)}) custom-call(s32[1,3]{1,0:T(1,128)S(1)} %bitcast.19, s32[3,32]{1,0:T(4,128)S(1)} %copy-done.4, bf16[8,128,256]{2,1,0:T(8,128)(2,1)S(1)} %bitcast.11, bf16[3,32,128,128]{3,2,1,0:T(8,128)(2,1)S(1)} %copy-done, ...), custom_call_target="tpu_custom_call" | custom-call | flops 402653184 | bytes 3145728 | tf_op jit(solution)/shard_map/pallas_call | solution.py:222
  26.0 6.2 %collective-permute-start.4 = (bf16[8,128,256]{2,1,0:T(8,128)(2,1)S(1)}, bf16[8,128,256]{2,1,0:T(8,128)(2,1)S(1)}, u32[]{:S(2)}, u32[]{:S(2)}) collective-permute-start(bf16[8,128,256]{2,1,0:T(8,128)(2,1)S(1)} %get-tuple-element.22), channel_id=1, source_target_pairs={{0,248},{8,0},{16,8},{24,16},{32,24},{40,32},{48,40},{56,48},{64,5... | collective-permute-start | bytes 1572872 | tf_op jit(solution)/shard_map/ppermute | solution.py:174
  32.2 0.0 collective-permute-done.1.refs_4_
  32.2 2.7 %shard_map.72 = (bf16[8,128,256]{2,1,0:T(8,128)(2,1)}, f32[9,128,256]{2,1,0:T(8,128)S(1)}) custom-call(s32[1,3]{1,0:T(1,128)S(1)} %bitcast.20, s32[3,32]{1,0:T(4,128)S(1)} %copy-done.4, bf16[8,128,256]{2,1,0:T(8,128)(2,1)S(1)} %bitcast.12, bf16[3,32,128,128]{3,2,1,0:T(8,128)(2,1)S(1)} %copy-done, bf16[8,128,256]{2,1,0:T(8,128)(2,1)S(1)} %collective-permute-done.1.refs_4_, ...), custom_call_target="tpu_custom_call" | custom-call | flops 402653184 | bytes 3145728 | tf_op jit(solution)/shard_map/pallas_call | solution.py:222
  34.9 0.0 collective-permute-start.3
  34.9 0.0 collective-permute-done.4.refs_4_
  34.9 1.8 %shard_map.74 = (bf16[8,128,256]{2,1,0:T(8,128)(2,1)S(1)}, bf16[4,2,128,256]{3,2,1,0:T(8,128)(2,1)S(1)}) custom-call(s32[1,3]{1,0:T(1,128)S(1)} %bitcast.21, s32[3,32]{1,0:T(4,128)S(1)} %copy-done.4, bf16[8,128,256]{2,1,0:T(8,128)(2,1)S(1)} %bitcast.13, bf16[3,32,128,128]{3,2,1,0:T(8,128)(2,1)S(1)} %copy-done, ...), custom_call_target="tpu_custom_call" | custom-call | flops 402653184 | bytes 3145728 | tf_op jit(solution)/shard_map/pallas_call | solution.py:222
  36.7 0.0 copy-start.3
  36.7 0.8 %copy-done.3 = bf16[4,2,128,256]{3,2,1,0:T(8,128)(2,1)} copy-done((bf16[4,2,128,256]{3,2,1,0:T(8,128)(2,1)}, bf16[4,2,128,256]{3,2,1,0:T(8,128)(2,1)S(1)}, u32[]{:S(2)}) %copy-start.3) | copy-done | bytes 524312
  37.5 0.0 copy-start.6
  37.5 0.8 %copy-done.6 = bf16[8,128,256]{2,1,0:T(8,128)(2,1)} copy-done((bf16[8,128,256]{2,1,0:T(8,128)(2,1)}, bf16[8,128,256]{2,1,0:T(8,128)(2,1)S(1)}, u32[]{:S(2)}) %copy-start.6) | copy-done | bytes 524312
  38.3 5.5 %all-to-all-start = ((bf16[4,2,128,256]{3,2,1,0:T(8,128)(2,1)}), bf16[4,2,128,256]{3,2,1,0:T(8,128)(2,1)S(1)}, u32[]{:S(2)}, u32[]{:S(2)}) async-start(bf16[4,2,128,256]{3,2,1,0:T(8,128)(2,1)} %copy-done.3), calls=%async_computation | async-start | bytes 1048576 | tf_op jit(solution)/shard_map/all_to_all | solution.py:254
  43.9 0.0 collective-permute-start.6
  43.9 14.0 %collective-permute-done.3.piece_ref = bf16[8,128,256]{2,1,0:T(8,128)(2,1)} collective-permute-done((bf16[8,128,256]{2,1,0:T(8,128)(2,1)}, bf16[8,128,256]{2,1,0:T(8,128)(2,1)}, u32[]{:S(2)}, u32[]{:S(2)}) %collective-permute-start.3) | collective-permute-done | bytes 524320 | tf_op jit(solution)/shard_map/ppermute | solution.py:174
  57.8 1.8 %shard_map.73.refs_0_ = bf16[16,128,256]{2,1,0:T(8,128)(2,1)} custom-call(bf16[8,128,256]{2,1,0:T(8,128)(2,1)} %collective-permute-done.3.piece_ref), custom_call_target="tpu_custom_call" | custom-call | bytes 8388608 | tf_op jit(solution)/shard_map/pallas_call | solution.py:241
  59.7 0.0 all-to-all-done
  59.7 0.1 convert_reduce_fusion
  59.8 0.1 collective-permute-start.5
  59.9 9.2 %collective-permute-done.5 = bf16[128,256]{1,0:T(8,128)(2,1)S(1)} collective-permute-done((bf16[128,256]{1,0:T(8,128)(2,1)S(1)}, bf16[128,256]{1,0:T(8,128)(2,1)S(1)}, u32[]{:S(2)}, u32[]{:S(2)}) %collective-permute-start.5) | collective-permute-done | bytes 65568 | tf_op jit(solution)/shard_map/ppermute | solution.py:263
  69.1 0.7 bitcast_add_fusion
  69.8 0.0 collective-permute-done.6.piece_ref
  69.8 0.8 %shard_map.75 = bf16[16,128,256]{2,1,0:T(8,128)(2,1)} custom-call(bf16[8,128,256]{2,1,0:T(8,128)(2,1)S(1)} %collective-permute-done.6.piece_ref, bf16[16,128,256]{2,1,0:T(8,128)(2,1)} %shard_map.73.refs_0_), custom_call_target="tpu_custom_call", output_to_operand_aliasing={{}: (1, {})} | custom-call | bytes 8388608 | tf_op jit(solution)/shard_map/pallas_call | solution.py:241
  (1 shorter events, 0.0 us)
Async XLA Ops:
  0.6 14.1 %copy-start = (bf16[3,32,128,128]{3,2,1,0:T(8,128)(2,1)S(1)}, bf16[3,32,128,128]{3,2,1,0:T(8,128)(2,1)}, u32[]{:S(2)}) copy-start(bf16[3,32,128,128]{3,2,1,0:T(8,128)(2,1)} %refs_3_.7) | copy-start | bytes 9437188
  0.6 14.1 %copy-start.1 = (bf16[1024,256]{1,0:T(8,128)(2,1)S(1)}, bf16[1024,256]{1,0:T(8,128)(2,1)}, u32[]{:S(2)}) copy-start(bf16[1024,256]{1,0:T(8,128)(2,1)} %param.5) | copy-start | bytes 1572868
  0.7 14.1 %copy-start.4 = (s32[3,32]{1,0:T(4,128)S(1)}, s32[3,32]{1,0:T(4,128)}, u32[]{:S(2)}) copy-start(s32[3,32]{1,0:T(4,128)} %refs_1_.7) | copy-start | bytes 1156
  0.7 14.0 %copy-start.5 = (s32[3,1]{0,1:T(1,128)S(1)}, s32[3,1]{0,1:T(1,128)}, u32[]{:S(2)}) copy-start(s32[3,1]{0,1:T(1,128)} %param.9) | copy-start | bytes 40
  6.1 12.0 %collective-permute-start = (bf16[8,128,256]{2,1,0:T(8,128)(2,1)}, bf16[8,128,256]{2,1,0:T(8,128)(2,1)S(1)}, u32[]{:S(2)}, u32[]{:S(2)}) collective-permute-start(bf16[8,128,256]{2,1,0:T(8,128)(2,1)} %get-tuple-element.16), channel_id=1, source_target_pairs={{0,248},{8,0},{16,8},{24,16},{32,24},{40,32},{48,40},{56,48},{64,5... | collective-permute-start | bytes 1572872 | tf_op jit(solution)/shard_map/ppermute | solution.py:174
  9.4 14.1 %collective-permute-start.2 = (bf16[8,128,256]{2,1,0:T(8,128)(2,1)}, bf16[8,128,256]{2,1,0:T(8,128)(2,1)S(1)}, u32[]{:S(2)}, u32[]{:S(2)}) collective-permute-start(bf16[8,128,256]{2,1,0:T(8,128)(2,1)} %get-tuple-element.18), channel_id=1, source_target_pairs={{0,248},{8,0},{16,8},{24,16},{32,24},{40,32},{48,40},{56,48},{64,5... | collective-permute-start | bytes 1572872 | tf_op jit(solution)/shard_map/ppermute | solution.py:174
  14.7 1.2 %copy-start.2 = (bf16[2048,256]{1,0:T(8,128)(2,1)S(1)}, bf16[2048,256]{1,0:T(8,128)(2,1)}, u32[]{:S(2)}) copy-start(bf16[2048,256]{1,0:T(8,128)(2,1)} %param.6) | copy-start | bytes 3145732
  20.6 11.6 %collective-permute-start.1 = (bf16[8,128,256]{2,1,0:T(8,128)(2,1)S(1)}, bf16[8,128,256]{2,1,0:T(8,128)(2,1)S(1)}, u32[]{:S(2)}, u32[]{:S(2)}) collective-permute-start(bf16[8,128,256]{2,1,0:T(8,128)(2,1)S(1)} %get-tuple-element.17), channel_id=1, source_target_pairs={{0,248},{8,0},{16,8},{24,16},{32,24},{40,32},{48,40},{56,48},{64,5... | collective-permute-start | bytes 1572872 | tf_op jit(solution)/shard_map/ppermute | solution.py:174
  26.0 8.9 %collective-permute-start.4 = (bf16[8,128,256]{2,1,0:T(8,128)(2,1)S(1)}, bf16[8,128,256]{2,1,0:T(8,128)(2,1)S(1)}, u32[]{:S(2)}, u32[]{:S(2)}) collective-permute-start(bf16[8,128,256]{2,1,0:T(8,128)(2,1)S(1)} %get-tuple-element.22), channel_id=1, source_target_pairs={{0,248},{8,0},{16,8},{24,16},{32,24},{40,32},{48,40},{56,48},{64,5... | collective-permute-start | bytes 1572872 | tf_op jit(solution)/shard_map/ppermute | solution.py:174
  34.9 22.9 %collective-permute-start.3 = (bf16[8,128,256]{2,1,0:T(8,128)(2,1)}, bf16[8,128,256]{2,1,0:T(8,128)(2,1)}, u32[]{:S(2)}, u32[]{:S(2)}) collective-permute-start(bf16[8,128,256]{2,1,0:T(8,128)(2,1)} %get-tuple-element.21), channel_id=1, source_target_pairs={{0,16},{8,24},{16,32},{24,40},{32,48},{40,56},{48,64},{56,72},{64,... | collective-permute-start | bytes 1572872 | tf_op jit(solution)/shard_map/ppermute | solution.py:174
  36.7 0.8 %copy-start.3 = (bf16[4,2,128,256]{3,2,1,0:T(8,128)(2,1)}, bf16[4,2,128,256]{3,2,1,0:T(8,128)(2,1)S(1)}, u32[]{:S(2)}) copy-start(bf16[4,2,128,256]{3,2,1,0:T(8,128)(2,1)S(1)} %get-tuple-element.24) | copy-start | bytes 1572868
  37.5 0.8 %copy-start.6 = (bf16[8,128,256]{2,1,0:T(8,128)(2,1)}, bf16[8,128,256]{2,1,0:T(8,128)(2,1)S(1)}, u32[]{:S(2)}) copy-start(bf16[8,128,256]{2,1,0:T(8,128)(2,1)S(1)} %get-tuple-element.26) | copy-start | bytes 1572868
  38.3 21.3 %all-to-all-start = ((bf16[4,2,128,256]{3,2,1,0:T(8,128)(2,1)}), bf16[4,2,128,256]{3,2,1,0:T(8,128)(2,1)S(1)}, u32[]{:S(2)}, u32[]{:S(2)}) async-start(bf16[4,2,128,256]{3,2,1,0:T(8,128)(2,1)} %copy-done.3), calls=%async_computation | async-start | bytes 1048576 | tf_op jit(solution)/shard_map/all_to_all | solution.py:254
  43.9 25.9 %collective-permute-start.6 = (bf16[8,128,256]{2,1,0:T(8,128)(2,1)}, bf16[8,128,256]{2,1,0:T(8,128)(2,1)S(1)}, u32[]{:S(2)}, u32[]{:S(2)}) collective-permute-start(bf16[8,128,256]{2,1,0:T(8,128)(2,1)} %copy-done.6), channel_id=1, source_target_pairs={{0,16},{8,24},{16,32},{24,40},{32,48},{40,56},{48,64},{56,72},{64,... | collective-permute-start | bytes 1572872 | tf_op jit(solution)/shard_map/ppermute | solution.py:174
  59.8 9.3 %collective-permute-start.5 = (bf16[128,256]{1,0:T(8,128)(2,1)S(1)}, bf16[128,256]{1,0:T(8,128)(2,1)S(1)}, u32[]{:S(2)}, u32[]{:S(2)}) collective-permute-start(bf16[128,256]{1,0:T(8,128)(2,1)S(1)} %fusion), channel_id=1, source_target_pairs={{0,4},{1,5},{2,6},{3,7},{4,0},{5,1},{6,2},{7,3},{8,12},{9,13},{10,... | collective-permute-start | bytes 196616 | tf_op jit(solution)/shard_map/ppermute | solution.py:263

commit v8 on v7

--- a/solution.py
+++ b/solution.py
@@ -102,7 +102,7 @@
     if not fresh:
         given, *rest = rest
     if closing:
-        new_ref, out_ref, grad_ref, peak_grad, places = rest
+        new_ref, *out_refs, grad_ref, peak_grad, places = rest
     else:
         new_ref, grad_ref, peak_grad, places = rest
     own_tiles = peak_ref.shape[0]
@@ -134,9 +134,13 @@
     for c in range(own_tiles):
         new_ref[c] = stepped(peak_ref[c], peak_grad[c], scaling)
     if closing:
-        near = out_ref.shape[0]
-        for r in range(row_tiles):
-            out_ref[r % near, r // near] = (grad_ref[r] * (gradient_scale * scaling)).astype(out_ref.dtype)
+        near = len(out_refs)
+        spot = lax.axis_index("chrom") % near
+        for ahead in range(near):
+            for side in range(row_tiles // near):
+                row = (spot + ahead) % near + side * near
+                total = grad_ref[row] * (gradient_scale * scaling)
+                out_refs[ahead][side] = total.astype(out_refs[ahead].dtype)
 
 
 def place_kernel(part, piece_ref, *refs):
@@ -215,16 +219,16 @@
             pltpu.VMEM((own_tiles + 1, tile_size, rank_width), jnp.float32),
             pltpu.SMEM((slots + group_size,), jnp.int32),
         ]
-        second = grad_out
+        others = (grad_out,)
         if closing:
-            second = jax.ShapeDtypeStruct((near, chroms // near, share_rows, rank_width), jnp.bfloat16)
+            others = (jax.ShapeDtypeStruct((chroms // near, share_rows, rank_width), jnp.bfloat16),) * near
             scratch.insert(0, pltpu.VMEM(grad_out.shape, jnp.float32))
         return pl.pallas_call(
             functools.partial(part_kernel, scaling, stratum, part, peak_tiles, closing, given is None),
             grid=(1,),
-            out_shape=(piece_out, second),
+            out_shape=(piece_out,) + others,
             in_specs=in_specs,
-            out_specs=(vmem, vmem),
+            out_specs=(vmem,) * (1 + len(others)),
             scratch_shapes=scratch,
             compiler_params=pltpu.CompilerParams(vmem_limit_bytes=16 * mebi),
             cost_estimate=cost(flops // parts, 3 * mebi),
@@ -233,7 +237,8 @@
     for stratum in range(1, strata):
         for part in range(parts):
             closing = stratum == last and part == parts - 1
-            piece, grad = part_call(stratum, part, pieces[part], grad, closing)
+            piece, *grads = part_call(stratum, part, pieces[part], grad, closing)
+            grad = grads[0]
             pieces[part] = moved(piece, last if stratum == last else -1)
 
     def put(part, peak_out):
@@ -250,13 +255,16 @@
             cost_estimate=cost(0, 8 * mebi),
         )(*args)
 
-    rings = [list(range(r * near, (r + 1) * near)) for r in range(chroms // near)]
-    shares = lax.all_to_all(grad, "chrom", 0, 0, axis_index_groups=rings, tiled=True)
+    around = [j // near * near for j in range(chroms)]
+    shares = grads[:1] + [
+        lax.ppermute(grads[d], "chrom", [(j, around[j] + (j + d) % near) for j in range(chroms)])
+        for d in range(1, near)
+    ]
     peak_out = None
     for part in range(parts - 1):
         peak_out = put(part, peak_out)
     peak_out, shares = lax.optimization_barrier((peak_out, shares))
-    shares = jnp.sum(shares.astype(jnp.float32), axis=0)
+    shares = sum(share.astype(jnp.float32) for share in shares)
     side = lax.axis_index("chrom") // near
     kept = lax.dynamic_index_in_dim(shares, side, 0, keepdims=False)
     sent = lax.dynamic_index_in_dim(shares, 1 - side, 0, keepdims=False).astype(jnp.bfloat16)

time: 70.7 us -> 70.3 us (level)
  local copies, waits for them, and re-layouts: 2.87 us -> 2.04 us
    all_to_all x1 -> x0, starting transfers between devices: 5.53 us -> none  [per_device(): lax.all_to_all(grad, 'chrom', 0, 0, axis_index_groups=rings, tiled=True)]
    ppermute x0 -> x3, starting transfers between devices: none -> 3.49 us  [per_device(): lax.ppermute(grads[d], 'chrom', [(j, around[j] + (j + d) % near) for j in...]
    ppermute x6, waiting for transfers between devices: 14 us -> 15.5 us  [moved(): lax.ppermute(piece, 'cell', [(i, (i + by) % cells) for i in range(cells)])]
    pallas_call x4, Pallas kernels: 9.52 us -> 10.9 us  [part_call(): pl.pallas_call(functools.partial(part_kernel, scaling, stratum, part, pea...]
    ppermute x6, starting transfers between devices: 17.7 us -> 19 us  [moved(): lax.ppermute(piece, 'cell', [(i, (i + by) % cells) for i in range(cells)])]
    ppermute x1, starting transfers between devices: 0.09 us -> 1.22 us  [per_device(): lax.ppermute(sent, 'chrom', [(j, (j + near) % chroms) for j in range(chro...]
    ppermute x1, waiting for transfers between devices: 9.22 us -> 8.12 us  [per_device(): lax.ppermute(sent, 'chrom', [(j, (j + near) % chroms) for j in range(chro...]
    pallas_call x1, Pallas kernels: 2.12 us -> 1.11 us  [per_device(): pl.pallas_call(functools.partial(cell_kernel, scaling), grid=(1,), out_sh...]
  transfers between devices with their start and end apart: 8 -> 10, of which waited for: 2 -> 3; matrix products, arithmetic and copies ran while one was open for 1% -> 1% of each run, Pallas kernels for 19% -> 20%
where the time goes in v8:
time: 70.3 us; the launch traced here: 70.1 us
  starting transfers between devices  23.7 us (34%)
  waiting for transfers between devices  23.6 us (34%)
  Pallas kernels  19.1 us (27%)
  local copies, waits for them, and re-layouts  2.04 us (3%)
  between operations  0.93 us (1%)
  other arithmetic  0.73 us (1%)
    ppermute x6, starting transfers between devices, moved(): lax.ppermute(piece, 'cell', [(i, (i + by) % cells) for i in range(cells)])  19 us
    ppermute x6, waiting for transfers between devices, moved(): lax.ppermute(piece, 'cell', [(i, (i + by) % cells) for i in range(cells)])  15.5 us
    pallas_call x4, Pallas kernels, part_call(): pl.pallas_call(functools.partial(part_kernel, scaling, stratum, part, pea...  10.9 us
    ppermute x1, waiting for transfers between devices, per_device(): lax.ppermute(sent, 'chrom', [(j, (j + near) % chroms) for j in range(chro...  8.12 us
    pallas_call x1, Pallas kernels, per_device(): pl.pallas_call(functools.partial(first_kernel, scaling), grid=(1,), out_s...  4.47 us
    ppermute x3, starting transfers between devices, per_device(): lax.ppermute(grads[d], 'chrom', [(j, around[j] + (j + d) % near) for j in...  3.49 us
    pallas_call x2, Pallas kernels, put(): pl.pallas_call(functools.partial(place_kernel, part), grid=(1,), out_shap...  2.64 us
    unnamed x12, local copies, waits for them, and re-layouts  2.03 us
  transfers between devices with their start and end apart: 10, of which 3 were waited for; matrix products, arithmetic and copies ran while one was open for 1% of the time, Pallas kernels for 20%

profile of v8, /device:TPU:1, one launch (start us, length us, event | category | flops | bytes accessed | tf_op | source)
XLA Modules:
  0.0 70.1 jit_solution(5631097216461150261)
XLA Ops:
  0.6 0.0 copy-start
  0.6 0.0 copy-start.1
  0.7 0.0 copy-start.3
  0.7 0.0 copy-start.4
  0.7 4.5 %shard_map.68 = (bf16[8,128,256]{2,1,0:T(8,128)(2,1)}, bf16[8,128,256]{2,1,0:T(8,128)(2,1)}) custom-call(s32[1,3]{1,0:T(1,128)} %bitcast.16, s32[3,32]{1,0:T(4,128)} %refs_1_.7, bf16[8,128,256]{2,1,0:T(8,128)(2,1)} %bitcast.8, bf16[16,128,256]{2,1,0:T(8,128)(2,1)} %bitcast.14, bf16[3,32,128,128]{3,2,1,0:T(8,128)(2,1)} %refs_3_.7), custom_call_target="tpu_custom_call" | custom-call | flops 805306368 | bytes 4194304 | tf_op jit(solution)/shard_map/pallas_call | solution.py:183
  5.1 3.3 %collective-permute-start = (bf16[8,128,256]{2,1,0:T(8,128)(2,1)}, bf16[8,128,256]{2,1,0:T(8,128)(2,1)S(1)}, u32[]{:S(2)}, u32[]{:S(2)}) collective-permute-start(bf16[8,128,256]{2,1,0:T(8,128)(2,1)} %get-tuple-element.22), channel_id=1, source_target_pairs={{0,248},{8,0},{16,8},{24,16},{32,24},{40,32},{48,40},{56,48},{64,5... | collective-permute-start | bytes 1572872 | tf_op jit(solution)/shard_map/ppermute | solution.py:178
  8.5 7.0 %collective-permute-start.2 = (bf16[8,128,256]{2,1,0:T(8,128)(2,1)}, bf16[8,128,256]{2,1,0:T(8,128)(2,1)S(1)}, u32[]{:S(2)}, u32[]{:S(2)}) collective-permute-start(bf16[8,128,256]{2,1,0:T(8,128)(2,1)} %get-tuple-element.24), channel_id=1, source_target_pairs={{0,248},{8,0},{16,8},{24,16},{32,24},{40,32},{48,40},{56,48},{64,5... | collective-permute-start | bytes 1572872 | tf_op jit(solution)/shard_map/ppermute | solution.py:178
  15.4 0.0 copy-done
  15.4 0.0 copy-done.1
  15.4 0.0 copy-done.3
  15.4 0.0 copy-done.4
  15.4 0.0 copy-start.2
  15.4 1.2 %copy-done.2 = bf16[2048,256]{1,0:T(8,128)(2,1)S(1)} copy-done((bf16[2048,256]{1,0:T(8,128)(2,1)S(1)}, bf16[2048,256]{1,0:T(8,128)(2,1)}, u32[]{:S(2)}) %copy-start.2) | copy-done | bytes 1048600
  16.6 1.1 %shard_map.69.refs_5_ = f32[9,128,256]{2,1,0:T(8,128)S(1)} custom-call(s32[1,3]{1,0:T(1,128)S(1)} %bitcast.17, s32[3,32]{1,0:T(4,128)S(1)} %copy-done.3, bf16[8,128,256]{2,1,0:T(8,128)(2,1)S(1)} %bitcast.9, bf16[16,128,256]{2,1,0:T(8,128)(2,1)S(1)} %bitcast.15, bf16[3,32,128,128]{3,2,1,0:T(8,128)(2,1)S(1)} %copy-done), custom_call_target="tpu_custom_call" | custom-call | flops 805306368 | bytes 4194304 | tf_op jit(solution)/shard_map/pallas_call | solution.py:201
  17.8 0.0 collective-permute-done.refs_4_
  17.8 2.6 %shard_map.70 = (bf16[8,128,256]{2,1,0:T(8,128)(2,1)S(1)}, f32[9,128,256]{2,1,0:T(8,128)S(1)}) custom-call(s32[1,3]{1,0:T(1,128)S(1)} %bitcast.18, s32[3,32]{1,0:T(4,128)S(1)} %copy-done.3, bf16[8,128,256]{2,1,0:T(8,128)(2,1)S(1)} %bitcast.10, bf16[3,32,128,128]{3,2,1,0:T(8,128)(2,1)S(1)} %copy-done, bf16[8,128,256]{2,1,0:T(8,128)(2,1)S(1)} %collective-permute-done.refs_4_, ...), custom_call_target="tpu_custom_call" | custom-call | flops 402653184 | bytes 3145728 | tf_op jit(solution)/shard_map/pallas_call | solution.py:226
  20.4 5.4 %collective-permute-start.1 = (bf16[8,128,256]{2,1,0:T(8,128)(2,1)S(1)}, bf16[8,128,256]{2,1,0:T(8,128)(2,1)S(1)}, u32[]{:S(2)}, u32[]{:S(2)}) collective-permute-start(bf16[8,128,256]{2,1,0:T(8,128)(2,1)S(1)} %get-tuple-element.23), channel_id=1, source_target_pairs={{0,248},{8,0},{16,8},{24,16},{32,24},{40,32},{48,40},{56,48},{64,5... | collective-permute-start | bytes 1572872 | tf_op jit(solution)/shard_map/ppermute | solution.py:178
  25.8 0.0 collective-permute-done.2.refs_4_
  25.8 3.3 %shard_map.71 = (bf16[8,128,256]{2,1,0:T(8,128)(2,1)S(1)}, f32[9,128,256]{2,1,0:T(8,128)S(1)}) custom-call(s32[1,3]{1,0:T(1,128)S(1)} %bitcast.19, s32[3,32]{1,0:T(4,128)S(1)} %copy-done.3, bf16[8,128,256]{2,1,0:T(8,128)(2,1)S(1)} %bitcast.11, bf16[3,32,128,128]{3,2,1,0:T(8,128)(2,1)S(1)} %copy-done, ...), custom_call_target="tpu_custom_call" | custom-call | flops 402653184 | bytes 3145728 | tf_op jit(solution)/shard_map/pallas_call | solution.py:226
  29.1 3.3 %collective-permute-start.4 = (bf16[8,128,256]{2,1,0:T(8,128)(2,1)S(1)}, bf16[8,128,256]{2,1,0:T(8,128)(2,1)S(1)}, u32[]{:S(2)}, u32[]{:S(2)}) collective-permute-start(bf16[8,128,256]{2,1,0:T(8,128)(2,1)S(1)} %get-tuple-element.28), channel_id=1, source_target_pairs={{0,248},{8,0},{16,8},{24,16},{32,24},{40,32},{48,40},{56,48},{64,5... | collective-permute-start | bytes 1572872 | tf_op jit(solution)/shard_map/ppermute | solution.py:178
  32.4 0.0 collective-permute-done.1.refs_4_
  32.4 2.7 %shard_map.72 = (bf16[8,128,256]{2,1,0:T(8,128)(2,1)}, f32[9,128,256]{2,1,0:T(8,128)S(1)}) custom-call(s32[1,3]{1,0:T(1,128)S(1)} %bitcast.20, s32[3,32]{1,0:T(4,128)S(1)} %copy-done.3, bf16[8,128,256]{2,1,0:T(8,128)(2,1)S(1)} %bitcast.12, bf16[3,32,128,128]{3,2,1,0:T(8,128)(2,1)S(1)} %copy-done, bf16[8,128,256]{2,1,0:T(8,128)(2,1)S(1)} %collective-permute-done.1.refs_4_, ...), custom_call_target="tpu_custom_call" | custom-call | flops 402653184 | bytes 3145728 | tf_op jit(solution)/shard_map/pallas_call | solution.py:226
  35.1 0.0 collective-permute-start.3
  35.1 2.7 %collective-permute-done.4.refs_4_ = bf16[8,128,256]{2,1,0:T(8,128)(2,1)S(1)} collective-permute-done((bf16[8,128,256]{2,1,0:T(8,128)(2,1)S(1)}, bf16[8,128,256]{2,1,0:T(8,128)(2,1)S(1)}, u32[]{:S(2)}, u32[]{:S(2)}) %collective-permute-start.4) | collective-permute-done | bytes 524320 | tf_op jit(solution)/shard_map/ppermute | solution.py:178
  37.8 2.3 %shard_map.74 = (bf16[8,128,256]{2,1,0:T(8,128)(2,1)S(1)}, bf16[2,128,256]{2,1,0:T(8,128)(2,1)S(1)}, bf16[2,128,256]{2,1,0:T(8,128)(2,1)}, bf16[2,128,256]{2,1,0:T(8,128)(2,1)S(1)}, bf16[2,128,256]{2,1,0:T(8,128)(2,1)S(1)}) custom-call(s32[1,3]{1,0:T(1,128)S(1)} %bitcast.21, s32[3,32]{1,0:T(4,128)S(1)} %copy-done.3, bf16[8,128,256]{2,1,0:T(8,128)(2,1)S(1)} %bitcast.13, ...), custom_call_target="tpu_custom_call" | custom-call | flops 402653184 | bytes 3145728 | tf_op jit(solution)/shard_map/pallas_call | solution.py:226
  40.1 0.0 copy-start.5
  40.1 0.8 %copy-done.5 = bf16[8,128,256]{2,1,0:T(8,128)(2,1)} copy-done((bf16[8,128,256]{2,1,0:T(8,128)(2,1)}, bf16[8,128,256]{2,1,0:T(8,128)(2,1)S(1)}, u32[]{:S(2)}) %copy-start.5) | copy-done | bytes 524312
  40.9 1.1 %collective-permute-start.5 = (bf16[2,128,256]{2,1,0:T(8,128)(2,1)}, bf16[2,128,256]{2,1,0:T(8,128)(2,1)S(1)}, u32[]{:S(2)}, u32[]{:S(2)}) collective-permute-start(bf16[2,128,256]{2,1,0:T(8,128)(2,1)} %get-tuple-element.31), channel_id=1, source_target_pairs={{0,1},{1,2},{2,3},{3,0},{4,5},{5,6},{6,7},{7,4},{8,9},{9,10},{10,1... | collective-permute-start | bytes 393224 | tf_op jit(solution)/shard_map/ppermute | solution.py:260
  41.9 1.4 %collective-permute-start.6 = (bf16[2,128,256]{2,1,0:T(8,128)(2,1)S(1)}, bf16[2,128,256]{2,1,0:T(8,128)(2,1)S(1)}, u32[]{:S(2)}, u32[]{:S(2)}) collective-permute-start(bf16[2,128,256]{2,1,0:T(8,128)(2,1)S(1)} %get-tuple-element.32), channel_id=1, source_target_pairs={{0,2},{1,3},{2,0},{3,1},{4,6},{5,7},{6,4},{7,5},{8,10},{9,11},{10,... | collective-permute-start | bytes 393224 | tf_op jit(solution)/shard_map/ppermute | solution.py:260
  43.4 1.0 %collective-permute-start.7 = (bf16[2,128,256]{2,1,0:T(8,128)(2,1)S(1)}, bf16[2,128,256]{2,1,0:T(8,128)(2,1)S(1)}, u32[]{:S(2)}, u32[]{:S(2)}) collective-permute-start(bf16[2,128,256]{2,1,0:T(8,128)(2,1)S(1)} %get-tuple-element.33), channel_id=1, source_target_pairs={{0,3},{1,0},{2,1},{3,2},{4,7},{5,4},{6,5},{7,6},{8,11},{9,8},{10,9... | collective-permute-start | bytes 393224 | tf_op jit(solution)/shard_map/ppermute | solution.py:260
  44.3 0.0 collective-permute-start.9
  44.4 12.8 %collective-permute-done.3.piece_ref = bf16[8,128,256]{2,1,0:T(8,128)(2,1)} collective-permute-done((bf16[8,128,256]{2,1,0:T(8,128)(2,1)}, bf16[8,128,256]{2,1,0:T(8,128)(2,1)}, u32[]{:S(2)}, u32[]{:S(2)}) %collective-permute-start.3) | collective-permute-done | bytes 524320 | tf_op jit(solution)/shard_map/ppermute | solution.py:178
  57.2 1.8 %shard_map.73.refs_0_ = bf16[16,128,256]{2,1,0:T(8,128)(2,1)} custom-call(bf16[8,128,256]{2,1,0:T(8,128)(2,1)} %collective-permute-done.3.piece_ref), custom_call_target="tpu_custom_call" | custom-call | bytes 8388608 | tf_op jit(solution)/shard_map/pallas_call | solution.py:246
  59.0 0.0 collective-permute-done.5
  59.0 0.0 collective-permute-done.6
  59.0 0.0 collective-permute-done.7
  59.1 0.1 convert_add_fusion
  59.2 1.2 %collective-permute-start.8 = (bf16[128,256]{1,0:T(8,128)(2,1)S(1)}, bf16[128,256]{1,0:T(8,128)(2,1)S(1)}, u32[]{:S(2)}, u32[]{:S(2)}) collective-permute-start(bf16[128,256]{1,0:T(8,128)(2,1)S(1)} %fusion), channel_id=1, source_target_pairs={{0,4},{1,5},{2,6},{3,7},{4,0},{5,1},{6,2},{7,3},{8,12},{9,13},{10,... | collective-permute-start | bytes 196616 | tf_op jit(solution)/shard_map/ppermute | solution.py:271
  60.4 8.1 %collective-permute-done.8 = bf16[128,256]{1,0:T(8,128)(2,1)S(1)} collective-permute-done((bf16[128,256]{1,0:T(8,128)(2,1)S(1)}, bf16[128,256]{1,0:T(8,128)(2,1)S(1)}, u32[]{:S(2)}, u32[]{:S(2)}) %collective-permute-start.8) | collective-permute-done | bytes 65568 | tf_op jit(solution)/shard_map/ppermute | solution.py:271
  68.5 0.7 bitcast_add_fusion
  69.2 0.0 collective-permute-done.9.piece_ref
  69.2 0.8 %shard_map.75 = bf16[16,128,256]{2,1,0:T(8,128)(2,1)} custom-call(bf16[8,128,256]{2,1,0:T(8,128)(2,1)S(1)} %collective-permute-done.9.piece_ref, bf16[16,128,256]{2,1,0:T(8,128)(2,1)} %shard_map.73.refs_0_), custom_call_target="tpu_custom_call", output_to_operand_aliasing={{}: (1, {})} | custom-call | bytes 8388608 | tf_op jit(solution)/shard_map/pallas_call | solution.py:246
  (1 shorter events, 0.0 us)
Async XLA Ops:
  0.6 14.8 %copy-start = (bf16[3,32,128,128]{3,2,1,0:T(8,128)(2,1)S(1)}, bf16[3,32,128,128]{3,2,1,0:T(8,128)(2,1)}, u32[]{:S(2)}) copy-start(bf16[3,32,128,128]{3,2,1,0:T(8,128)(2,1)} %refs_3_.7) | copy-start | bytes 9437188
  0.6 14.8 %copy-start.1 = (bf16[1024,256]{1,0:T(8,128)(2,1)S(1)}, bf16[1024,256]{1,0:T(8,128)(2,1)}, u32[]{:S(2)}) copy-start(bf16[1024,256]{1,0:T(8,128)(2,1)} %param.5) | copy-start | bytes 1572868
  0.7 14.8 %copy-start.3 = (s32[3,32]{1,0:T(4,128)S(1)}, s32[3,32]{1,0:T(4,128)}, u32[]{:S(2)}) copy-start(s32[3,32]{1,0:T(4,128)} %refs_1_.7) | copy-start | bytes 1156
  0.7 14.8 %copy-start.4 = (s32[3,1]{0,1:T(1,128)S(1)}, s32[3,1]{0,1:T(1,128)}, u32[]{:S(2)}) copy-start(s32[3,1]{0,1:T(1,128)} %param.9) | copy-start | bytes 40
  5.1 12.6 %collective-permute-start = (bf16[8,128,256]{2,1,0:T(8,128)(2,1)}, bf16[8,128,256]{2,1,0:T(8,128)(2,1)S(1)}, u32[]{:S(2)}, u32[]{:S(2)}) collective-permute-start(bf16[8,128,256]{2,1,0:T(8,128)(2,1)} %get-tuple-element.22), channel_id=1, source_target_pairs={{0,248},{8,0},{16,8},{24,16},{32,24},{40,32},{48,40},{56,48},{64,5... | collective-permute-start | bytes 1572872 | tf_op jit(solution)/shard_map/ppermute | solution.py:178
  8.5 17.3 %collective-permute-start.2 = (bf16[8,128,256]{2,1,0:T(8,128)(2,1)}, bf16[8,128,256]{2,1,0:T(8,128)(2,1)S(1)}, u32[]{:S(2)}, u32[]{:S(2)}) collective-permute-start(bf16[8,128,256]{2,1,0:T(8,128)(2,1)} %get-tuple-element.24), channel_id=1, source_target_pairs={{0,248},{8,0},{16,8},{24,16},{32,24},{40,32},{48,40},{56,48},{64,5... | collective-permute-start | bytes 1572872 | tf_op jit(solution)/shard_map/ppermute | solution.py:178
  15.4 1.2 %copy-start.2 = (bf16[2048,256]{1,0:T(8,128)(2,1)S(1)}, bf16[2048,256]{1,0:T(8,128)(2,1)}, u32[]{:S(2)}) copy-start(bf16[2048,256]{1,0:T(8,128)(2,1)} %param.6) | copy-start | bytes 3145732
  20.4 12.0 %collective-permute-start.1 = (bf16[8,128,256]{2,1,0:T(8,128)(2,1)S(1)}, bf16[8,128,256]{2,1,0:T(8,128)(2,1)S(1)}, u32[]{:S(2)}, u32[]{:S(2)}) collective-permute-start(bf16[8,128,256]{2,1,0:T(8,128)(2,1)S(1)} %get-tuple-element.23), channel_id=1, source_target_pairs={{0,248},{8,0},{16,8},{24,16},{32,24},{40,32},{48,40},{56,48},{64,5... | collective-permute-start | bytes 1572872 | tf_op jit(solution)/shard_map/ppermute | solution.py:178
  29.1 8.7 %collective-permute-start.4 = (bf16[8,128,256]{2,1,0:T(8,128)(2,1)S(1)}, bf16[8,128,256]{2,1,0:T(8,128)(2,1)S(1)}, u32[]{:S(2)}, u32[]{:S(2)}) collective-permute-start(bf16[8,128,256]{2,1,0:T(8,128)(2,1)S(1)} %get-tuple-element.28), channel_id=1, source_target_pairs={{0,248},{8,0},{16,8},{24,16},{32,24},{40,32},{48,40},{56,48},{64,5... | collective-permute-start | bytes 1572872 | tf_op jit(solution)/shard_map/ppermute | solution.py:178
  35.1 22.1 %collective-permute-start.3 = (bf16[8,128,256]{2,1,0:T(8,128)(2,1)}, bf16[8,128,256]{2,1,0:T(8,128)(2,1)}, u32[]{:S(2)}, u32[]{:S(2)}) collective-permute-start(bf16[8,128,256]{2,1,0:T(8,128)(2,1)} %get-tuple-element.27), channel_id=1, source_target_pairs={{0,16},{8,24},{16,32},{24,40},{32,48},{40,56},{48,64},{56,72},{64,... | collective-permute-start | bytes 1572872 | tf_op jit(solution)/shard_map/ppermute | solution.py:178
  40.1 0.8 %copy-start.5 = (bf16[8,128,256]{2,1,0:T(8,128)(2,1)}, bf16[8,128,256]{2,1,0:T(8,128)(2,1)S(1)}, u32[]{:S(2)}) copy-start(bf16[8,128,256]{2,1,0:T(8,128)(2,1)S(1)} %get-tuple-element.38) | copy-start | bytes 1572868
  40.9 18.2 %collective-permute-start.5 = (bf16[2,128,256]{2,1,0:T(8,128)(2,1)}, bf16[2,128,256]{2,1,0:T(8,128)(2,1)S(1)}, u32[]{:S(2)}, u32[]{:S(2)}) collective-permute-start(bf16[2,128,256]{2,1,0:T(8,128)(2,1)} %get-tuple-element.31), channel_id=1, source_target_pairs={{0,1},{1,2},{2,3},{3,0},{4,5},{5,6},{6,7},{7,4},{8,9},{9,10},{10,1... | collective-permute-start | bytes 393224 | tf_op jit(solution)/shard_map/ppermute | solution.py:260
  41.9 17.1 %collective-permute-start.6 = (bf16[2,128,256]{2,1,0:T(8,128)(2,1)S(1)}, bf16[2,128,256]{2,1,0:T(8,128)(2,1)S(1)}, u32[]{:S(2)}, u32[]{:S(2)}) collective-permute-start(bf16[2,128,256]{2,1,0:T(8,128)(2,1)S(1)} %get-tuple-element.32), channel_id=1, source_target_pairs={{0,2},{1,3},{2,0},{3,1},{4,6},{5,7},{6,4},{7,5},{8,10},{9,11},{10,... | collective-permute-start | bytes 393224 | tf_op jit(solution)/shard_map/ppermute | solution.py:260
  43.4 15.7 %collective-permute-start.7 = (bf16[2,128,256]{2,1,0:T(8,128)(2,1)S(1)}, bf16[2,128,256]{2,1,0:T(8,128)(2,1)S(1)}, u32[]{:S(2)}, u32[]{:S(2)}) collective-permute-start(bf16[2,128,256]{2,1,0:T(8,128)(2,1)S(1)} %get-tuple-element.33), channel_id=1, source_target_pairs={{0,3},{1,0},{2,1},{3,2},{4,7},{5,4},{6,5},{7,6},{8,11},{9,8},{10,9... | collective-permute-start | bytes 393224 | tf_op jit(solution)/shard_map/ppermute | solution.py:260
  44.3 24.8 %collective-permute-start.9 = (bf16[8,128,256]{2,1,0:T(8,128)(2,1)}, bf16[8,128,256]{2,1,0:T(8,128)(2,1)S(1)}, u32[]{:S(2)}, u32[]{:S(2)}) collective-permute-start(bf16[8,128,256]{2,1,0:T(8,128)(2,1)} %copy-done.5), channel_id=1, source_target_pairs={{0,16},{8,24},{16,32},{24,40},{32,48},{40,56},{48,64},{56,72},{64,... | collective-permute-start | bytes 1572872 | tf_op jit(solution)/shard_map/ppermute | solution.py:178
  59.2 9.3 %collective-permute-start.8 = (bf16[128,256]{1,0:T(8,128)(2,1)S(1)}, bf16[128,256]{1,0:T(8,128)(2,1)S(1)}, u32[]{:S(2)}, u32[]{:S(2)}) collective-permute-start(bf16[128,256]{1,0:T(8,128)(2,1)S(1)} %fusion), channel_id=1, source_target_pairs={{0,4},{1,5},{2,6},{3,7},{4,0},{5,1},{6,2},{7,3},{8,12},{9,13},{10,... | collective-permute-start | bytes 196616 | tf_op jit(solution)/shard_map/ppermute | solution.py:271

commit v9 on v8

--- a/solution.py
+++ b/solution.py
@@ -57,52 +57,56 @@
     return (peak.astype(jnp.float32) - learning_rate * (grad * scaling)).astype(jnp.bfloat16)
 
 
-def first_kernel(scaling, counts, index, cell_in, peak_in, values_in, *refs):
-    news, (cell_ref, peak_ref, values_ref, peak_grad, sems) = refs[:parts], refs[parts:]
+def first_kernel(scaling, parity, counts, index, cell_in, peak_in, values_in, *refs):
+    news, (grad_ref, cell_ref, peak_ref, values_ref, peak_grad, sems) = refs[-6 - parts : -6], refs[-6:]
     peak_tiles = peak_ref.shape[0]
-    loads = [
-        pltpu.make_async_copy(cell_in, cell_ref, sems.at[0]),
-        pltpu.make_async_copy(peak_in, peak_ref, sems.at[1]),
-        pltpu.make_async_copy(values_in.at[0], values_ref, sems.at[2]),
-    ]
-    for copy in loads:
-        copy.start()
-    peak_grad[...] = jnp.zeros_like(peak_grad)
-    for copy in loads:
-        copy.wait()
-
-    def slot_of(t):
-        place = index[0, t]
-        row, col = place // peak_tiles, place % peak_tiles
-        return t, row, col, row, col
-
-    groups = counts[0, 0] // group_size
-    walk(groups, slot_of, cell_ref, peak_ref, lambda t: values_ref[t], peak_grad, None, scaling)
-    own_tiles = peak_tiles // parts
-    for c in range(peak_tiles):
-        news[c // own_tiles][c % own_tiles] = stepped(peak_ref[c], peak_grad[c], scaling)
-
-
-def cell_kernel(scaling, counts, index, cell_ref, peak_ref, values, grad_ref):
-    peak_tiles = peak_ref.shape[0]
-    grad_ref[...] = jnp.zeros_like(grad_ref)
-
-    def slot_of(t):
-        place = index[0, t]
-        row, col = place // peak_tiles, place % peak_tiles
-        return t, row, col, row, col
-
-    groups = counts[0, 0] // group_size
-    walk(groups, slot_of, cell_ref, peak_ref, lambda t: values[0, t], None, grad_ref, scaling)
-
-
-def part_kernel(scaling, stratum, part, peak_tiles, closing, fresh, *refs):
+
+    @pl.when(lax.axis_index("cell") % 2 == parity)
+    def _():
+        loads = [
+            pltpu.make_async_copy(cell_in, cell_ref, sems.at[0]),
+            pltpu.make_async_copy(peak_in, peak_ref, sems.at[1]),
+            pltpu.make_async_copy(values_in.at[0], values_ref, sems.at[2]),
+        ]
+        for copy in loads:
+            copy.start()
+        peak_grad[...] = jnp.zeros_like(peak_grad)
+        grad_ref[...] = jnp.zeros_like(grad_ref)
+        for copy in loads:
+            copy.wait()
+
+        def slot_of(t):
+            place = index[0, t]
+            row, col = place // peak_tiles, place % peak_tiles
+            return t, row, col, row, col
+
+        groups = counts[0, 0] // group_size
+        walk(groups, slot_of, cell_ref, peak_ref, lambda t: values_ref[t], peak_grad, grad_ref, scaling)
+        own_tiles = peak_tiles // parts
+        for c in range(peak_tiles):
+            news[c // own_tiles][c % own_tiles] = stepped(peak_ref[c], peak_grad[c], scaling)
+
+
+def part_kernel(scaling, stratum, part, peak_tiles, closing, paired, fresh, *refs):
     counts, index, cell_ref, values, peak_ref, *rest = refs
-    given = None
+    if paired:
+        far_ref, _, *rest, chosen = rest
+        odd = lax.axis_index("cell") % 2
+
+        @pl.when(odd == 0)
+        def _():
+            chosen[...] = peak_ref[...]
+
+        @pl.when(odd == 1)
+        def _():
+            chosen[...] = far_ref[...]
+
+        peak_ref = chosen
     if not fresh:
         given, *rest = rest
     if closing:
-        new_ref, *out_refs, grad_ref, peak_grad, places = rest
+        *earlier, new_ref, out0, out1, out2, out3, grad_ref, peak_grad, places = rest
+        out_refs = (out0, out1, out2, out3)
     else:
         new_ref, grad_ref, peak_grad, places = rest
     own_tiles = peak_ref.shape[0]
@@ -136,11 +140,19 @@
     if closing:
         near = len(out_refs)
         spot = lax.axis_index("chrom") % near
-        for ahead in range(near):
-            for side in range(row_tiles // near):
-                row = (spot + ahead) % near + side * near
-                total = grad_ref[row] * (gradient_scale * scaling)
-                out_refs[ahead][side] = total.astype(out_refs[ahead].dtype)
+        for parity, early in enumerate(earlier):
+
+            @pl.when(lax.axis_index("cell") % 2 == parity)
+            def _():
+                for ahead in range(near):
+                    for side in range(row_tiles // near):
+                        row = (spot + ahead) % near + side * near
+                        total = (early[row] + grad_ref[row]) * (gradient_scale * scaling)
+                        out_refs[ahead][side] = total.astype(out_refs[ahead].dtype)
+
+
+def token_kernel(piece_ref, token_ref):
+    token_ref[...] = jnp.zeros_like(token_ref)
 
 
 def place_kernel(part, piece_ref, *refs):
@@ -180,51 +192,65 @@
     piece_out = jax.ShapeDtypeStruct((own_tiles, tile_size, rank_width), jnp.bfloat16)
     grad_out = jax.ShapeDtypeStruct((row_tiles + 1, tile_size, rank_width), jnp.float32)
 
-    pieces = pl.pallas_call(
-        functools.partial(first_kernel, scaling),
-        grid=(1,),
-        out_shape=(piece_out,) * parts,
-        in_specs=[smem, smem, far, far, far],
-        out_specs=(vmem,) * parts,
-        scratch_shapes=[
-            pltpu.VMEM(cell_blocks.shape, jnp.bfloat16),
-            pltpu.VMEM(peak_block.shape, jnp.bfloat16),
-            pltpu.VMEM(tile_values.shape[1:], jnp.bfloat16),
-            pltpu.VMEM(peak_block.shape, jnp.float32),
-            pltpu.SemaphoreType.DMA((3,)),
-        ],
-        compiler_params=pltpu.CompilerParams(vmem_limit_bytes=60 * mebi),
-        cost_estimate=cost(flops, 4 * mebi),
-    )(counts, tile_index, cell_blocks, peak_block, tile_values)
-    pieces = [moved(piece, -1) for piece in pieces]
-    first_values = pl.BlockSpec((1,) + tile_values.shape[1:], lambda i: (0, 0, 0, 0))
-    grad = pl.pallas_call(
-        functools.partial(cell_kernel, scaling),
-        grid=(1,),
-        out_shape=grad_out,
-        in_specs=[smem, smem, vmem, vmem, first_values],
-        out_specs=vmem,
-        compiler_params=pltpu.CompilerParams(vmem_limit_bytes=16 * mebi),
-        cost_estimate=cost(flops, 4 * mebi),
-    )(counts, tile_index, cell_blocks, peak_block, tile_values)
-
+    early_out = jax.ShapeDtypeStruct(cell_blocks.shape, jnp.float32)
+
+    def first_call(parity, before):
+        return pl.pallas_call(
+            functools.partial(first_kernel, scaling, parity),
+            grid=(1,),
+            out_shape=(piece_out,) * parts + (early_out,),
+            in_specs=[smem, smem, far, far, far] + [far] * len(before),
+            out_specs=(vmem,) * (parts + 1),
+            scratch_shapes=[
+                pltpu.VMEM(cell_blocks.shape, jnp.bfloat16),
+                pltpu.VMEM(peak_block.shape, jnp.bfloat16),
+                pltpu.VMEM(tile_values.shape[1:], jnp.bfloat16),
+                pltpu.VMEM(peak_block.shape, jnp.float32),
+                pltpu.SemaphoreType.DMA((3,)),
+            ],
+            compiler_params=pltpu.CompilerParams(vmem_limit_bytes=60 * mebi),
+            cost_estimate=cost(flops, 4 * mebi),
+        )(counts, tile_index, cell_blocks, peak_block, tile_values, *before)
+
+    *firsts, early_even = first_call(0, [])
+    over = [moved(piece, -1) for piece in firsts]
+    *seconds, early_odd = first_call(1, firsts[:1])
+    swapped = [lax.ppermute(piece, "cell", [(i, i ^ 1) for i in range(cells)]) for piece in seconds]
+    pieces = []
+    for near_piece, far_piece in zip(swapped, over):
+        token = pl.pallas_call(
+            token_kernel,
+            grid=(1,),
+            out_shape=jax.ShapeDtypeStruct((8, lanes), jnp.int32),
+            in_specs=[far],
+            out_specs=vmem,
+            compiler_params=pltpu.CompilerParams(vmem_limit_bytes=16 * mebi),
+            cost_estimate=cost(0, 32 * mebi),
+        )(far_piece)
+        pieces.append((near_piece, far_piece, token))
+    grad = None
     def part_call(stratum, part, piece, given, closing):
         own_values = pl.BlockSpec((1,) + tile_values.shape[1:], lambda i: (stratum, 0, 0, 0))
-        args = [counts, tile_index, cell_blocks, tile_values, piece]
-        in_specs = [smem, smem, vmem, own_values, vmem]
+        paired = isinstance(piece, tuple)
+        args = [counts, tile_index, cell_blocks, tile_values, *(piece if paired else (piece,))]
         if given is not None:
             args.append(given)
+        if closing:
+            args += [early_even, early_odd]
+        in_specs = [smem, smem, vmem, own_values]
         in_specs += [vmem] * (len(args) - len(in_specs))
         scratch = [
             pltpu.VMEM((own_tiles + 1, tile_size, rank_width), jnp.float32),
             pltpu.SMEM((slots + group_size,), jnp.int32),
         ]
+        if paired:
+            scratch.append(pltpu.VMEM(piece_out.shape, jnp.bfloat16))
         others = (grad_out,)
         if closing:
             others = (jax.ShapeDtypeStruct((chroms // near, share_rows, rank_width), jnp.bfloat16),) * near
             scratch.insert(0, pltpu.VMEM(grad_out.shape, jnp.float32))
         return pl.pallas_call(
-            functools.partial(part_kernel, scaling, stratum, part, peak_tiles, closing, given is None),
+            functools.partial(part_kernel, scaling, stratum, part, peak_tiles, closing, paired, given is None),
             grid=(1,),
             out_shape=(piece_out,) + others,
             in_specs=in_specs,

time: 70.3 us -> 71.1 us (1.011); the launches traced: 70.1 us -> 69.9 us
  Pallas kernels: 19.1 us -> 22.6 us
  waiting for transfers between devices: 23.6 us -> 21.9 us
  local copies, waits for them, and re-layouts: 2.04 us -> 0.85 us
  starting transfers between devices: 23.7 us -> 22.8 us
    ppermute x6, starting transfers between devices: 19 us -> 10.8 us  [moved(): lax.ppermute(piece, 'cell', [(i, (i + by) % cells) for i in range(cells)])]
    ppermute x6, waiting for transfers between devices: 15.5 us -> 9.21 us  [moved(): lax.ppermute(piece, 'cell', [(i, (i + by) % cells) for i in range(cells)])]
    ppermute x0 -> x2, starting transfers between devices: none -> 5.01 us  [per_device(): lax.ppermute(piece, 'cell', [(i, i ^ 1) for i in range(cells)])]
    ppermute x1, waiting for transfers between devices: 8.12 us -> 12.7 us  [per_device(): lax.ppermute(sent, 'chrom', [(j, (j + near) % chroms) for j in range(chro...]
    ppermute x3, starting transfers between devices: 3.49 us -> 6.82 us  [per_device(): lax.ppermute(grads[d], 'chrom', [(j, around[j] + (j + d) % near) for j in...]
    pallas_call x2 -> x4, Pallas kernels: 5.58 us -> 8.37 us  [the longest x2 8.37 us: first_call(): pl.pallas_call(functools.partial(first_kernel, scaling, parity), grid=(1,...]
    unnamed x12 -> x14, local copies, waits for them, and re-layouts: 2.03 us -> 0.84 us
    ppermute x1, starting transfers between devices: 1.22 us -> 0.21 us  [per_device(): lax.ppermute(sent, 'chrom', [(j, (j + near) % chroms) for j in range(chro...]
  transfers between devices with their start and end apart: 10 -> 12, of which waited for: 3 -> 5; matrix products, arithmetic and copies ran while one was open for 1% -> 1% of each run, Pallas kernels for 20% -> 28%
where the time goes in v9:
time: 71.1 us; the launch traced here: 69.9 us
  starting transfers between devices  22.8 us (32%)
  Pallas kernels  22.6 us (32%)
  waiting for transfers between devices  21.9 us (31%)
  between operations  0.95 us (1%)
  local copies, waits for them, and re-layouts  0.85 us (1%)
  other arithmetic  0.73 us (1%)
    ppermute x1, waiting for transfers between devices, per_device(): lax.ppermute(sent, 'chrom', [(j, (j + near) % chroms) for j in range(chro...  12.7 us
    pallas_call x4, Pallas kernels, part_call(): pl.pallas_call(functools.partial(part_kernel, scaling, stratum, part, pea...  11.5 us
    ppermute x6, starting transfers between devices, moved(): lax.ppermute(piece, 'cell', [(i, (i + by) % cells) for i in range(cells)])  10.8 us
    ppermute x6, waiting for transfers between devices, moved(): lax.ppermute(piece, 'cell', [(i, (i + by) % cells) for i in range(cells)])  9.21 us
    pallas_call x2, Pallas kernels, first_call(): pl.pallas_call(functools.partial(first_kernel, scaling, parity), grid=(1,...  8.37 us
    ppermute x3, starting transfers between devices, per_device(): lax.ppermute(grads[d], 'chrom', [(j, around[j] + (j + d) % near) for j in...  6.82 us
    ppermute x2, starting transfers between devices, per_device(): lax.ppermute(piece, 'cell', [(i, i ^ 1) for i in range(cells)])  5.01 us
    pallas_call x2, Pallas kernels, put(): pl.pallas_call(functools.partial(place_kernel, part), grid=(1,), out_shap...  2.64 us
  transfers between devices with their start and end apart: 12, of which 5 were waited for; matrix products, arithmetic and copies ran while one was open for 1% of the time, Pallas kernels for 28%

profile of v9, /device:TPU:1, one launch (start us, length us, event | category | flops | bytes accessed | tf_op | source)
XLA Modules:
  0.0 69.9 jit_solution(87061170372255047)
XLA Ops:
  0.6 2.1 %shard_map.68 = (bf16[8,128,256]{2,1,0:T(8,128)(2,1)}, bf16[8,128,256]{2,1,0:T(8,128)(2,1)}, f32[8,128,256]{2,1,0:T(8,128)}) custom-call(s32[1,3]{1,0:T(1,128)} %bitcast.14, s32[3,32]{1,0:T(4,128)} %refs_1_.7, bf16[8,128,256]{2,1,0:T(8,128)(2,1)} %bitcast.8, bf16[16,128,256]{2,1,0:T(8,128)(2,1)} %bitcast.20, bf16[3,32,128,128]{3,2,1,0:T(8,128)(2,1)} %refs_3_.7), custom_call_target="tpu_custom_call" | custom-call | flops 805306368 | bytes 4194304 | tf_op jit(solution)/shard_map/pallas_call | solution.py:198
  2.7 0.0 copy-start.1
  2.7 0.0 copy-start.4
  2.7 0.0 copy-start.5
  2.7 6.3 %collective-permute-start.1 = (bf16[8,128,256]{2,1,0:T(8,128)(2,1)}, bf16[8,128,256]{2,1,0:T(8,128)(2,1)}, u32[]{:S(2)}, u32[]{:S(2)}) collective-permute-start(bf16[8,128,256]{2,1,0:T(8,128)(2,1)} %get-tuple-element.26.refs_0_), channel_id=1, source_target_pairs={{0,248},{8,0},{16,8},{24,16},{32,24},{40,32},{48,40},{56,48},{64,5... | collective-permute-start | bytes 1572872 | tf_op jit(solution)/shard_map/ppermute | solution.py:190
  9.1 0.0 copy-start
  9.1 6.3 %shard_map.69 = (bf16[8,128,256]{2,1,0:T(8,128)(2,1)}, bf16[8,128,256]{2,1,0:T(8,128)(2,1)}, f32[8,128,256]{2,1,0:T(8,128)}) custom-call(s32[1,3]{1,0:T(1,128)} %bitcast.15, s32[3,32]{1,0:T(4,128)} %refs_1_.7, bf16[8,128,256]{2,1,0:T(8,128)(2,1)} %bitcast.9, bf16[16,128,256]{2,1,0:T(8,128)(2,1)} %bitcast.21, bf16[3,32,128,128]{3,2,1,0:T(8,128)(2,1)} %refs_3_.7, ...), custom_call_target="tpu_custom_call" | custom-call | flops 805306368 | bytes 4194304 | tf_op jit(solution)/shard_map/pallas_call | solution.py:198
  15.4 0.1 collective-permute-start
  15.5 0.5 collective-permute-start.4
  16.0 4.9 %collective-permute-start.3 = (bf16[8,128,256]{2,1,0:T(8,128)(2,1)}, bf16[8,128,256]{2,1,0:T(8,128)(2,1)S(1)}, u32[]{:S(2)}, u32[]{:S(2)}) collective-permute-start(bf16[8,128,256]{2,1,0:T(8,128)(2,1)} %get-tuple-element.29), channel_id=1, source_target_pairs={{0,8},{8,0},{16,24},{24,16},{32,40},{40,32},{48,56},{56,48},{64,72... | collective-permute-start | bytes 1572872 | tf_op jit(solution)/shard_map/ppermute | solution.py:218
  20.9 0.0 collective-permute-done.1.piece_ref.refs_5_
  20.9 0.0 collective-permute-done.refs_4_
  20.9 0.0 copy-done.1
  20.9 0.0 copy-done.4
  20.9 0.0 copy-done.5
  20.9 0.0 copy-done
  21.0 3.1 %shard_map.71 = (bf16[8,128,256]{2,1,0:T(8,128)(2,1)S(1)}, f32[9,128,256]{2,1,0:T(8,128)S(1)}) custom-call(s32[1,3]{1,0:T(1,128)S(1)} %bitcast.16, s32[3,32]{1,0:T(4,128)S(1)} %copy-done.4, bf16[8,128,256]{2,1,0:T(8,128)(2,1)S(1)} %bitcast.10, bf16[3,32,128,128]{3,2,1,0:T(8,128)(2,1)S(1)} %copy-done, bf16[8,128,256]{2,1,0:T(8,128)(2,1)S(1)} %collective-permute-done.refs_4_, ...), custom_call_target="tpu_custom_call" | custom-call | flops 402653184 | bytes 3145728 | tf_op jit(solution)/shard_map/pallas_call | solution.py:252
  24.0 0.1 collective-permute-start.2
  24.1 0.3 collective-permute-done.4.piece_ref.refs_5_
  24.4 0.0 collective-permute-done.3.refs_4_
  24.4 2.8 %shard_map.73 = (bf16[8,128,256]{2,1,0:T(8,128)(2,1)S(1)}, f32[9,128,256]{2,1,0:T(8,128)S(1)}) custom-call(s32[1,3]{1,0:T(1,128)S(1)} %bitcast.17, s32[3,32]{1,0:T(4,128)S(1)} %copy-done.4, bf16[8,128,256]{2,1,0:T(8,128)(2,1)S(1)} %bitcast.11, bf16[3,32,128,128]{3,2,1,0:T(8,128)(2,1)S(1)} %copy-done, ...), custom_call_target="tpu_custom_call" | custom-call | flops 402653184 | bytes 3145728 | tf_op jit(solution)/shard_map/pallas_call | solution.py:252
  27.2 3.9 %collective-permute-start.6 = (bf16[8,128,256]{2,1,0:T(8,128)(2,1)S(1)}, bf16[8,128,256]{2,1,0:T(8,128)(2,1)S(1)}, u32[]{:S(2)}, u32[]{:S(2)}) collective-permute-start(bf16[8,128,256]{2,1,0:T(8,128)(2,1)S(1)} %get-tuple-element.34), channel_id=1, source_target_pairs={{0,248},{8,0},{16,8},{24,16},{32,24},{40,32},{48,40},{56,48},{64,5... | collective-permute-start | bytes 1572872 | tf_op jit(solution)/shard_map/ppermute | solution.py:190
  31.0 1.7 %collective-permute-done.2.refs_4_ = bf16[8,128,256]{2,1,0:T(8,128)(2,1)S(1)} collective-permute-done((bf16[8,128,256]{2,1,0:T(8,128)(2,1)S(1)}, bf16[8,128,256]{2,1,0:T(8,128)(2,1)S(1)}, u32[]{:S(2)}, u32[]{:S(2)}) %collective-permute-start.2) | collective-permute-done | bytes 524320 | tf_op jit(solution)/shard_map/ppermute | solution.py:190
  32.7 0.0 copy-start.2
  32.7 0.0 copy-start.3
  32.7 3.0 %shard_map.74 = (bf16[8,128,256]{2,1,0:T(8,128)(2,1)}, f32[9,128,256]{2,1,0:T(8,128)S(1)}) custom-call(s32[1,3]{1,0:T(1,128)S(1)} %bitcast.18, s32[3,32]{1,0:T(4,128)S(1)} %copy-done.4, bf16[8,128,256]{2,1,0:T(8,128)(2,1)S(1)} %bitcast.12, bf16[3,32,128,128]{3,2,1,0:T(8,128)(2,1)S(1)} %copy-done, bf16[8,128,256]{2,1,0:T(8,128)(2,1)S(1)} %collective-permute-done.2.refs_4_, ...), custom_call_target="tpu_custom_call" | custom-call | flops 402653184 | bytes 3145728 | tf_op jit(solution)/shard_map/pallas_call | solution.py:252
  35.8 0.0 collective-permute-start.5
  35.8 2.6 %collective-permute-done.6.refs_4_ = bf16[8,128,256]{2,1,0:T(8,128)(2,1)S(1)} collective-permute-done((bf16[8,128,256]{2,1,0:T(8,128)(2,1)S(1)}, bf16[8,128,256]{2,1,0:T(8,128)(2,1)S(1)}, u32[]{:S(2)}, u32[]{:S(2)}) %collective-permute-start.6) | collective-permute-done | bytes 524320 | tf_op jit(solution)/shard_map/ppermute | solution.py:190
  38.3 0.0 copy-done.2
  38.3 0.0 copy-done.3
  38.3 2.7 %shard_map.76 = (bf16[8,128,256]{2,1,0:T(8,128)(2,1)S(1)}, bf16[2,128,256]{2,1,0:T(8,128)(2,1)S(1)}, bf16[2,128,256]{2,1,0:T(8,128)(2,1)}, bf16[2,128,256]{2,1,0:T(8,128)(2,1)S(1)}, bf16[2,128,256]{2,1,0:T(8,128)(2,1)S(1)}) custom-call(s32[1,3]{1,0:T(1,128)S(1)} %bitcast.19, s32[3,32]{1,0:T(4,128)S(1)} %copy-done.4, bf16[8,128,256]{2,1,0:T(8,128)(2,1)S(1)} %bitcast.13, ...), custom_call_target="tpu_custom_call" | custom-call | flops 402653184 | bytes 3145728 | tf_op jit(solution)/shard_map/pallas_call | solution.py:252
  41.0 0.0 copy-start.6
  41.0 0.8 %copy-done.6 = bf16[8,128,256]{2,1,0:T(8,128)(2,1)} copy-done((bf16[8,128,256]{2,1,0:T(8,128)(2,1)}, bf16[8,128,256]{2,1,0:T(8,128)(2,1)S(1)}, u32[]{:S(2)}) %copy-start.6) | copy-done | bytes 524312
  41.8 3.0 %collective-permute-start.7 = (bf16[2,128,256]{2,1,0:T(8,128)(2,1)}, bf16[2,128,256]{2,1,0:T(8,128)(2,1)S(1)}, u32[]{:S(2)}, u32[]{:S(2)}) collective-permute-start(bf16[2,128,256]{2,1,0:T(8,128)(2,1)} %get-tuple-element.39), channel_id=1, source_target_pairs={{0,1},{1,2},{2,3},{3,0},{4,5},{5,6},{6,7},{7,4},{8,9},{9,10},{10,1... | collective-permute-start | bytes 393224 | tf_op jit(solution)/shard_map/ppermute | solution.py:286
  44.8 3.9 %collective-permute-start.8 = (bf16[2,128,256]{2,1,0:T(8,128)(2,1)S(1)}, bf16[2,128,256]{2,1,0:T(8,128)(2,1)S(1)}, u32[]{:S(2)}, u32[]{:S(2)}) collective-permute-start(bf16[2,128,256]{2,1,0:T(8,128)(2,1)S(1)} %get-tuple-element.40), channel_id=1, source_target_pairs={{0,2},{1,3},{2,0},{3,1},{4,6},{5,7},{6,4},{7,5},{8,10},{9,11},{10,... | collective-permute-start | bytes 393224 | tf_op jit(solution)/shard_map/ppermute | solution.py:286
  48.6 0.0 collective-permute-start.9
  48.6 0.0 collective-permute-start.11
  48.6 4.7 %collective-permute-done.5.piece_ref = bf16[8,128,256]{2,1,0:T(8,128)(2,1)} collective-permute-done((bf16[8,128,256]{2,1,0:T(8,128)(2,1)}, bf16[8,128,256]{2,1,0:T(8,128)(2,1)}, u32[]{:S(2)}, u32[]{:S(2)}) %collective-permute-start.5) | collective-permute-done | bytes 524320 | tf_op jit(solution)/shard_map/ppermute | solution.py:190
  53.3 1.8 %shard_map.75.refs_0_ = bf16[16,128,256]{2,1,0:T(8,128)(2,1)} custom-call(bf16[8,128,256]{2,1,0:T(8,128)(2,1)} %collective-permute-done.5.piece_ref), custom_call_target="tpu_custom_call" | custom-call | bytes 8388608 | tf_op jit(solution)/shard_map/pallas_call | solution.py:272
  55.2 0.0 collective-permute-done.7
  55.2 0.0 collective-permute-done.8
  55.2 0.0 collective-permute-done.9
  55.2 0.1 convert_add_fusion
  55.3 0.2 collective-permute-start.10
  55.5 12.7 %collective-permute-done.10 = bf16[128,256]{1,0:T(8,128)(2,1)S(1)} collective-permute-done((bf16[128,256]{1,0:T(8,128)(2,1)S(1)}, bf16[128,256]{1,0:T(8,128)(2,1)S(1)}, u32[]{:S(2)}, u32[]{:S(2)}) %collective-permute-start.10) | collective-permute-done | bytes 65568 | tf_op jit(solution)/shard_map/ppermute | solution.py:297
  68.2 0.7 bitcast_add_fusion
  68.9 0.0 collective-permute-done.11.piece_ref
  68.9 0.8 %shard_map.77 = bf16[16,128,256]{2,1,0:T(8,128)(2,1)} custom-call(bf16[8,128,256]{2,1,0:T(8,128)(2,1)S(1)} %collective-permute-done.11.piece_ref, bf16[16,128,256]{2,1,0:T(8,128)(2,1)} %shard_map.75.refs_0_), custom_call_target="tpu_custom_call", output_to_operand_aliasing={{}: (1, {})} | custom-call | bytes 8388608 | tf_op jit(solution)/shard_map/pallas_call | solution.py:272
  (3 shorter events, 0.0 us)
Async XLA Ops:
  2.7 18.2 %copy-start.1 = (bf16[1024,256]{1,0:T(8,128)(2,1)S(1)}, bf16[1024,256]{1,0:T(8,128)(2,1)}, u32[]{:S(2)}) copy-start(bf16[1024,256]{1,0:T(8,128)(2,1)} %param.5) | copy-start | bytes 1572868
  2.7 18.2 %copy-start.4 = (s32[3,32]{1,0:T(4,128)S(1)}, s32[3,32]{1,0:T(4,128)}, u32[]{:S(2)}) copy-start(s32[3,32]{1,0:T(4,128)} %refs_1_.7) | copy-start | bytes 1156
  2.7 18.2 %copy-start.5 = (s32[3,1]{0,1:T(1,128)S(1)}, s32[3,1]{0,1:T(1,128)}, u32[]{:S(2)}) copy-start(s32[3,1]{0,1:T(1,128)} %param.9) | copy-start | bytes 40
  2.7 18.2 %collective-permute-start.1 = (bf16[8,128,256]{2,1,0:T(8,128)(2,1)}, bf16[8,128,256]{2,1,0:T(8,128)(2,1)}, u32[]{:S(2)}, u32[]{:S(2)}) collective-permute-start(bf16[8,128,256]{2,1,0:T(8,128)(2,1)} %get-tuple-element.26.refs_0_), channel_id=1, source_target_pairs={{0,248},{8,0},{16,8},{24,16},{32,24},{40,32},{48,40},{56,48},{64,5... | collective-permute-start | bytes 1572872 | tf_op jit(solution)/shard_map/ppermute | solution.py:190
  9.1 11.9 %copy-start = (bf16[3,32,128,128]{3,2,1,0:T(8,128)(2,1)S(1)}, bf16[3,32,128,128]{3,2,1,0:T(8,128)(2,1)}, u32[]{:S(2)}) copy-start(bf16[3,32,128,128]{3,2,1,0:T(8,128)(2,1)} %refs_3_.7) | copy-start | bytes 9437188
  15.4 5.5 %collective-permute-start = (bf16[8,128,256]{2,1,0:T(8,128)(2,1)}, bf16[8,128,256]{2,1,0:T(8,128)(2,1)S(1)}, u32[]{:S(2)}, u32[]{:S(2)}) collective-permute-start(bf16[8,128,256]{2,1,0:T(8,128)(2,1)} %get-tuple-element.27), channel_id=1, source_target_pairs={{0,8},{8,0},{16,24},{24,16},{32,40},{40,32},{48,56},{56,48},{64,72... | collective-permute-start | bytes 1572872 | tf_op jit(solution)/shard_map/ppermute | solution.py:218
  15.5 8.9 %collective-permute-start.4 = (bf16[8,128,256]{2,1,0:T(8,128)(2,1)}, bf16[8,128,256]{2,1,0:T(8,128)(2,1)S(1)}, u32[]{:S(2)}, u32[]{:S(2)}) collective-permute-start(bf16[8,128,256]{2,1,0:T(8,128)(2,1)} %get-tuple-element.30), channel_id=1, source_target_pairs={{0,248},{8,0},{16,8},{24,16},{32,24},{40,32},{48,40},{56,48},{64,5... | collective-permute-start | bytes 1572872 | tf_op jit(solution)/shard_map/ppermute | solution.py:190
  16.0 8.4 %collective-permute-start.3 = (bf16[8,128,256]{2,1,0:T(8,128)(2,1)}, bf16[8,128,256]{2,1,0:T(8,128)(2,1)S(1)}, u32[]{:S(2)}, u32[]{:S(2)}) collective-permute-start(bf16[8,128,256]{2,1,0:T(8,128)(2,1)} %get-tuple-element.29), channel_id=1, source_target_pairs={{0,8},{8,0},{16,24},{24,16},{32,40},{40,32},{48,56},{56,48},{64,72... | collective-permute-start | bytes 1572872 | tf_op jit(solution)/shard_map/ppermute | solution.py:218
  24.0 8.7 %collective-permute-start.2 = (bf16[8,128,256]{2,1,0:T(8,128)(2,1)S(1)}, bf16[8,128,256]{2,1,0:T(8,128)(2,1)S(1)}, u32[]{:S(2)}, u32[]{:S(2)}) collective-permute-start(bf16[8,128,256]{2,1,0:T(8,128)(2,1)S(1)} %get-tuple-element.28), channel_id=1, source_target_pairs={{0,248},{8,0},{16,8},{24,16},{32,24},{40,32},{48,40},{56,48},{64,5... | collective-permute-start | bytes 1572872 | tf_op jit(solution)/shard_map/ppermute | solution.py:190
  27.2 11.2 %collective-permute-start.6 = (bf16[8,128,256]{2,1,0:T(8,128)(2,1)S(1)}, bf16[8,128,256]{2,1,0:T(8,128)(2,1)S(1)}, u32[]{:S(2)}, u32[]{:S(2)}) collective-permute-start(bf16[8,128,256]{2,1,0:T(8,128)(2,1)S(1)} %get-tuple-element.34), channel_id=1, source_target_pairs={{0,248},{8,0},{16,8},{24,16},{32,24},{40,32},{48,40},{56,48},{64,5... | collective-permute-start | bytes 1572872 | tf_op jit(solution)/shard_map/ppermute | solution.py:190
  32.7 5.6 %copy-start.2 = (f32[8,128,256]{2,1,0:T(8,128)S(1)}, f32[8,128,256]{2,1,0:T(8,128)}, u32[]{:S(2)}) copy-start(f32[8,128,256]{2,1,0:T(8,128)} %get-tuple-element.36.refs_6_) | copy-start | bytes 3145732
  32.7 5.6 %copy-start.3 = (f32[8,128,256]{2,1,0:T(8,128)S(1)}, f32[8,128,256]{2,1,0:T(8,128)}, u32[]{:S(2)}) copy-start(f32[8,128,256]{2,1,0:T(8,128)} %get-tuple-element.37.refs_7_) | copy-start | bytes 3145732
  35.8 17.6 %collective-permute-start.5 = (bf16[8,128,256]{2,1,0:T(8,128)(2,1)}, bf16[8,128,256]{2,1,0:T(8,128)(2,1)}, u32[]{:S(2)}, u32[]{:S(2)}) collective-permute-start(bf16[8,128,256]{2,1,0:T(8,128)(2,1)} %get-tuple-element.33), channel_id=1, source_target_pairs={{0,16},{8,24},{16,32},{24,40},{32,48},{40,56},{48,64},{56,72},{64,... | collective-permute-start | bytes 1572872 | tf_op jit(solution)/shard_map/ppermute | solution.py:190
  41.0 0.8 %copy-start.6 = (bf16[8,128,256]{2,1,0:T(8,128)(2,1)}, bf16[8,128,256]{2,1,0:T(8,128)(2,1)S(1)}, u32[]{:S(2)}) copy-start(bf16[8,128,256]{2,1,0:T(8,128)(2,1)S(1)} %get-tuple-element.46) | copy-start | bytes 1572868
  41.8 13.4 %collective-permute-start.7 = (bf16[2,128,256]{2,1,0:T(8,128)(2,1)}, bf16[2,128,256]{2,1,0:T(8,128)(2,1)S(1)}, u32[]{:S(2)}, u32[]{:S(2)}) collective-permute-start(bf16[2,128,256]{2,1,0:T(8,128)(2,1)} %get-tuple-element.39), channel_id=1, source_target_pairs={{0,1},{1,2},{2,3},{3,0},{4,5},{5,6},{6,7},{7,4},{8,9},{9,10},{10,1... | collective-permute-start | bytes 393224 | tf_op jit(solution)/shard_map/ppermute | solution.py:286
  44.8 10.4 %collective-permute-start.8 = (bf16[2,128,256]{2,1,0:T(8,128)(2,1)S(1)}, bf16[2,128,256]{2,1,0:T(8,128)(2,1)S(1)}, u32[]{:S(2)}, u32[]{:S(2)}) collective-permute-start(bf16[2,128,256]{2,1,0:T(8,128)(2,1)S(1)} %get-tuple-element.40), channel_id=1, source_target_pairs={{0,2},{1,3},{2,0},{3,1},{4,6},{5,7},{6,4},{7,5},{8,10},{9,11},{10,... | collective-permute-start | bytes 393224 | tf_op jit(solution)/shard_map/ppermute | solution.py:286
  48.6 6.6 %collective-permute-start.9 = (bf16[2,128,256]{2,1,0:T(8,128)(2,1)S(1)}, bf16[2,128,256]{2,1,0:T(8,128)(2,1)S(1)}, u32[]{:S(2)}, u32[]{:S(2)}) collective-permute-start(bf16[2,128,256]{2,1,0:T(8,128)(2,1)S(1)} %get-tuple-element.41), channel_id=1, source_target_pairs={{0,3},{1,0},{2,1},{3,2},{4,7},{5,4},{6,5},{7,6},{8,11},{9,8},{10,9... | collective-permute-start | bytes 393224 | tf_op jit(solution)/shard_map/ppermute | solution.py:286
  48.6 20.3 %collective-permute-start.11 = (bf16[8,128,256]{2,1,0:T(8,128)(2,1)}, bf16[8,128,256]{2,1,0:T(8,128)(2,1)S(1)}, u32[]{:S(2)}, u32[]{:S(2)}) collective-permute-start(bf16[8,128,256]{2,1,0:T(8,128)(2,1)} %copy-done.6), channel_id=1, source_target_pairs={{0,16},{8,24},{16,32},{24,40},{32,48},{40,56},{48,64},{56,72},{64,... | collective-permute-start | bytes 1572872 | tf_op jit(solution)/shard_map/ppermute | solution.py:190
  55.3 12.9 %collective-permute-start.10 = (bf16[128,256]{1,0:T(8,128)(2,1)S(1)}, bf16[128,256]{1,0:T(8,128)(2,1)S(1)}, u32[]{:S(2)}, u32[]{:S(2)}) collective-permute-start(bf16[128,256]{1,0:T(8,128)(2,1)S(1)} %fusion), channel_id=1, source_target_pairs={{0,4},{1,5},{2,6},{3,7},{4,0},{5,1},{6,2},{7,3},{8,12},{9,13},{10,... | collective-permute-start | bytes 196616 | tf_op jit(solution)/shard_map/ppermute | solution.py:297

commit v10 on v8

--- a/solution.py
+++ b/solution.py
@@ -22,6 +22,11 @@
 
 def contract(left, right, dims):
     return lax.dot_general(left, right, ((dims[:1], dims[1:]), ((), ())), preferred_element_type=jnp.float32)
+
+
+def split(value, size):
+    assert size & (size - 1) == 0
+    return value >> (size.bit_length() - 1), value & (size - 1)
 
 
 def walk(groups, slot_of, cell_ref, peak_ref, values_at, peak_grad, grad_ref, scaling):
@@ -40,7 +45,7 @@
             for term, f in zip(terms, found):
                 grad_ref[f[3]] += term
 
-    pairs = groups // 2
+    pairs = groups >> 1
 
     def pair(g, carry):
         tiles(g * 2 * group_size, 2 * group_size)
@@ -73,10 +78,10 @@
 
     def slot_of(t):
         place = index[0, t]
-        row, col = place // peak_tiles, place % peak_tiles
+        row, col = split(place, peak_tiles)
         return t, row, col, row, col
 
-    groups = counts[0, 0] // group_size
+    groups, _ = split(counts[0, 0], group_size)
     walk(groups, slot_of, cell_ref, peak_ref, lambda t: values_ref[t], peak_grad, None, scaling)
     own_tiles = peak_tiles // parts
     for c in range(peak_tiles):
@@ -89,10 +94,10 @@
 
     def slot_of(t):
         place = index[0, t]
-        row, col = place // peak_tiles, place % peak_tiles
+        row, col = split(place, peak_tiles)
         return t, row, col, row, col
 
-    groups = counts[0, 0] // group_size
+    groups, _ = split(counts[0, 0], group_size)
     walk(groups, slot_of, cell_ref, peak_ref, lambda t: values[0, t], None, grad_ref, scaling)
 
 
@@ -109,13 +114,13 @@
     row_tiles = grad_ref.shape[0] - 1
     slots = places.shape[0] - group_size
 
-    def note(t, found):
+    found = jnp.int32(0)
+    live = counts[0, stratum]
+    for t in range(slots):
         place = index[stratum, t]
         places[found] = place * slots + t
-        mine = (place % peak_tiles) // own_tiles == part
-        return found + jnp.where(mine, 1, 0)
-
-    found = lax.fori_loop(0, counts[0, stratum], note, 0)
+        owner, _ = split(split(place, peak_tiles)[1], own_tiles)
+        found = found + jnp.where((owner == part) & (t < live), 1, 0)
     for k in range(group_size):
         places[found + k] = -1
     peak_grad[...] = jnp.zeros_like(peak_grad)
@@ -125,11 +130,12 @@
         code = places[k]
         used = code >= 0
         code = jnp.maximum(code, 0)
-        place = code // slots
-        row, col = place // peak_tiles, place % own_tiles
-        return code % slots, row, col, jnp.where(used, row, row_tiles), jnp.where(used, col, own_tiles)
-
-    groups = (found + group_size - 1) // group_size
+        place, t = split(code, slots)
+        row, col = split(place, peak_tiles)
+        col = split(col, own_tiles)[1]
+        return t, row, col, jnp.where(used, row, row_tiles), jnp.where(used, col, own_tiles)
+
+    groups, _ = split(found + group_size - 1, group_size)
     walk(groups, slot_of, cell_ref, peak_ref, lambda t: values[0, t], peak_grad, grad_ref, scaling)
     for c in range(own_tiles):
         new_ref[c] = stepped(peak_ref[c], peak_grad[c], scaling)

time: 70.3 us -> 70.1 us (level)
  starting transfers between devices: 23.7 us -> 26.7 us
  waiting for transfers between devices: 23.6 us -> 21.1 us
  Pallas kernels: 19.1 us -> 18.3 us
    pallas_call x4, Pallas kernels: 10.9 us -> 8.08 us  [part_call(): pl.pallas_call(functools.partial(part_kernel, scaling, stratum, part, pea...]
    ppermute x6, waiting for transfers between devices: 15.5 us -> 13.1 us  [moved(): lax.ppermute(piece, 'cell', [(i, (i + by) % cells) for i in range(cells)])]
    ppermute x3, starting transfers between devices: 3.49 us -> 5.59 us  [per_device(): lax.ppermute(grads[d], 'chrom', [(j, around[j] + (j + d) % near) for j in...]
    ppermute x1, starting transfers between devices: 1.22 us -> 2.37 us  [per_device(): lax.ppermute(sent, 'chrom', [(j, (j + near) % chroms) for j in range(chro...]
    pallas_call x1, Pallas kernels: 1.11 us -> 2.22 us  [per_device(): pl.pallas_call(functools.partial(cell_kernel, scaling), grid=(1,), out_sh...]
    pallas_call x1, Pallas kernels: 4.47 us -> 5.39 us  [per_device(): pl.pallas_call(functools.partial(first_kernel, scaling), grid=(1,), out_s...]
  transfers between devices with their start and end apart: 10 -> 10, of which waited for: 3 -> 2; matrix products, arithmetic and copies ran while one was open for 1% -> 1% of each run, Pallas kernels for 20% -> 17%
where the time goes in v10:
time: 70.1 us; the launch traced here: 69.8 us
  starting transfers between devices  26.7 us (38%)
  waiting for transfers between devices  21.1 us (30%)
  Pallas kernels  18.3 us (26%)
  local copies, waits for them, and re-layouts  2.04 us (3%)
  between operations  0.93 us (1%)
  other arithmetic  0.73 us (1%)
    ppermute x6, starting transfers between devices, moved(): lax.ppermute(piece, 'cell', [(i, (i + by) % cells) for i in range(cells)])  18.8 us
    ppermute x6, waiting for transfers between devices, moved(): lax.ppermute(piece, 'cell', [(i, (i + by) % cells) for i in range(cells)])  13.1 us
    pallas_call x4, Pallas kernels, part_call(): pl.pallas_call(functools.partial(part_kernel, scaling, stratum, part, pea...  8.08 us
    ppermute x1, waiting for transfers between devices, per_device(): lax.ppermute(sent, 'chrom', [(j, (j + near) % chroms) for j in range(chro...  7.92 us
    ppermute x3, starting transfers between devices, per_device(): lax.ppermute(grads[d], 'chrom', [(j, around[j] + (j + d) % near) for j in...  5.59 us
    pallas_call x1, Pallas kernels, per_device(): pl.pallas_call(functools.partial(first_kernel, scaling), grid=(1,), out_s...  5.39 us
    pallas_call x2, Pallas kernels, put(): pl.pallas_call(functools.partial(place_kernel, part), grid=(1,), out_shap...  2.64 us
    ppermute x1, starting transfers between devices, per_device(): lax.ppermute(sent, 'chrom', [(j, (j + near) % chroms) for j in range(chro...  2.37 us
  transfers between devices with their start and end apart: 10, of which 2 were waited for; matrix products, arithmetic and copies ran while one was open for 1% of the time, Pallas kernels for 17%

profile of v10, /device:TPU:1, one launch (start us, length us, event | category | flops | bytes accessed | tf_op | source)
XLA Modules:
  0.0 69.8 jit_solution(15812998205432096187)
XLA Ops:
  0.6 0.0 copy-start
  0.6 0.0 copy-start.1
  0.7 0.0 copy-start.3
  0.7 0.0 copy-start.4
  0.7 5.4 %shard_map.68 = (bf16[8,128,256]{2,1,0:T(8,128)(2,1)}, bf16[8,128,256]{2,1,0:T(8,128)(2,1)}) custom-call(s32[1,3]{1,0:T(1,128)} %bitcast.16, s32[3,32]{1,0:T(4,128)} %refs_1_.7, bf16[8,128,256]{2,1,0:T(8,128)(2,1)} %bitcast.8, bf16[16,128,256]{2,1,0:T(8,128)(2,1)} %bitcast.14, bf16[3,32,128,128]{3,2,1,0:T(8,128)(2,1)} %refs_3_.7), custom_call_target="tpu_custom_call" | custom-call | flops 805306368 | bytes 4194304 | tf_op jit(solution)/shard_map/pallas_call | solution.py:189
  6.1 2.6 %collective-permute-start = (bf16[8,128,256]{2,1,0:T(8,128)(2,1)}, bf16[8,128,256]{2,1,0:T(8,128)(2,1)S(1)}, u32[]{:S(2)}, u32[]{:S(2)}) collective-permute-start(bf16[8,128,256]{2,1,0:T(8,128)(2,1)} %get-tuple-element.22), channel_id=1, source_target_pairs={{0,248},{8,0},{16,8},{24,16},{32,24},{40,32},{48,40},{56,48},{64,5... | collective-permute-start | bytes 1572872 | tf_op jit(solution)/shard_map/ppermute | solution.py:184
  8.7 6.0 %collective-permute-start.2 = (bf16[8,128,256]{2,1,0:T(8,128)(2,1)}, bf16[8,128,256]{2,1,0:T(8,128)(2,1)S(1)}, u32[]{:S(2)}, u32[]{:S(2)}) collective-permute-start(bf16[8,128,256]{2,1,0:T(8,128)(2,1)} %get-tuple-element.24), channel_id=1, source_target_pairs={{0,248},{8,0},{16,8},{24,16},{32,24},{40,32},{48,40},{56,48},{64,5... | collective-permute-start | bytes 1572872 | tf_op jit(solution)/shard_map/ppermute | solution.py:184
  14.7 0.0 copy-done
  14.7 0.0 copy-done.1
  14.7 0.0 copy-done.3
  14.7 0.0 copy-done.4
  14.7 0.0 copy-start.2
  14.7 1.2 %copy-done.2 = bf16[2048,256]{1,0:T(8,128)(2,1)S(1)} copy-done((bf16[2048,256]{1,0:T(8,128)(2,1)S(1)}, bf16[2048,256]{1,0:T(8,128)(2,1)}, u32[]{:S(2)}) %copy-start.2) | copy-done | bytes 1048600
  15.9 2.2 %shard_map.69.refs_5_ = f32[9,128,256]{2,1,0:T(8,128)S(1)} custom-call(s32[1,3]{1,0:T(1,128)S(1)} %bitcast.17, s32[3,32]{1,0:T(4,128)S(1)} %copy-done.3, bf16[8,128,256]{2,1,0:T(8,128)(2,1)S(1)} %bitcast.9, bf16[16,128,256]{2,1,0:T(8,128)(2,1)S(1)} %bitcast.15, bf16[3,32,128,128]{3,2,1,0:T(8,128)(2,1)S(1)} %copy-done), custom_call_target="tpu_custom_call" | custom-call | flops 805306368 | bytes 4194304 | tf_op jit(solution)/shard_map/pallas_call | solution.py:207
  18.1 0.0 collective-permute-done.refs_4_
  18.2 1.6 %shard_map.70 = (bf16[8,128,256]{2,1,0:T(8,128)(2,1)S(1)}, f32[9,128,256]{2,1,0:T(8,128)S(1)}) custom-call(s32[1,3]{1,0:T(1,128)S(1)} %bitcast.18, s32[3,32]{1,0:T(4,128)S(1)} %copy-done.3, bf16[8,128,256]{2,1,0:T(8,128)(2,1)S(1)} %bitcast.10, bf16[3,32,128,128]{3,2,1,0:T(8,128)(2,1)S(1)} %copy-done, bf16[8,128,256]{2,1,0:T(8,128)(2,1)S(1)} %collective-permute-done.refs_4_, ...), custom_call_target="tpu_custom_call" | custom-call | flops 402653184 | bytes 3145728 | tf_op jit(solution)/shard_map/pallas_call | solution.py:232
  19.8 4.0 %collective-permute-start.1 = (bf16[8,128,256]{2,1,0:T(8,128)(2,1)S(1)}, bf16[8,128,256]{2,1,0:T(8,128)(2,1)S(1)}, u32[]{:S(2)}, u32[]{:S(2)}) collective-permute-start(bf16[8,128,256]{2,1,0:T(8,128)(2,1)S(1)} %get-tuple-element.23), channel_id=1, source_target_pairs={{0,248},{8,0},{16,8},{24,16},{32,24},{40,32},{48,40},{56,48},{64,5... | collective-permute-start | bytes 1572872 | tf_op jit(solution)/shard_map/ppermute | solution.py:184
  23.7 0.0 collective-permute-done.2.refs_4_
  23.7 1.6 %shard_map.71 = (bf16[8,128,256]{2,1,0:T(8,128)(2,1)S(1)}, f32[9,128,256]{2,1,0:T(8,128)S(1)}) custom-call(s32[1,3]{1,0:T(1,128)S(1)} %bitcast.19, s32[3,32]{1,0:T(4,128)S(1)} %copy-done.3, bf16[8,128,256]{2,1,0:T(8,128)(2,1)S(1)} %bitcast.11, bf16[3,32,128,128]{3,2,1,0:T(8,128)(2,1)S(1)} %copy-done, ...), custom_call_target="tpu_custom_call" | custom-call | flops 402653184 | bytes 3145728 | tf_op jit(solution)/shard_map/pallas_call | solution.py:232
  25.4 6.2 %collective-permute-start.4 = (bf16[8,128,256]{2,1,0:T(8,128)(2,1)S(1)}, bf16[8,128,256]{2,1,0:T(8,128)(2,1)S(1)}, u32[]{:S(2)}, u32[]{:S(2)}) collective-permute-start(bf16[8,128,256]{2,1,0:T(8,128)(2,1)S(1)} %get-tuple-element.28), channel_id=1, source_target_pairs={{0,248},{8,0},{16,8},{24,16},{32,24},{40,32},{48,40},{56,48},{64,5... | collective-permute-start | bytes 1572872 | tf_op jit(solution)/shard_map/ppermute | solution.py:184
  31.5 0.0 collective-permute-done.1.refs_4_
  31.5 2.8 %shard_map.72 = (bf16[8,128,256]{2,1,0:T(8,128)(2,1)}, f32[9,128,256]{2,1,0:T(8,128)S(1)}) custom-call(s32[1,3]{1,0:T(1,128)S(1)} %bitcast.20, s32[3,32]{1,0:T(4,128)S(1)} %copy-done.3, bf16[8,128,256]{2,1,0:T(8,128)(2,1)S(1)} %bitcast.12, bf16[3,32,128,128]{3,2,1,0:T(8,128)(2,1)S(1)} %copy-done, bf16[8,128,256]{2,1,0:T(8,128)(2,1)S(1)} %collective-permute-done.1.refs_4_, ...), custom_call_target="tpu_custom_call" | custom-call | flops 402653184 | bytes 3145728 | tf_op jit(solution)/shard_map/pallas_call | solution.py:232
  34.3 0.0 collective-permute-start.3
  34.3 0.0 collective-permute-done.4.refs_4_
  34.3 2.1 %shard_map.74 = (bf16[8,128,256]{2,1,0:T(8,128)(2,1)S(1)}, bf16[2,128,256]{2,1,0:T(8,128)(2,1)S(1)}, bf16[2,128,256]{2,1,0:T(8,128)(2,1)}, bf16[2,128,256]{2,1,0:T(8,128)(2,1)S(1)}, bf16[2,128,256]{2,1,0:T(8,128)(2,1)S(1)}) custom-call(s32[1,3]{1,0:T(1,128)S(1)} %bitcast.21, s32[3,32]{1,0:T(4,128)S(1)} %copy-done.3, bf16[8,128,256]{2,1,0:T(8,128)(2,1)S(1)} %bitcast.13, ...), custom_call_target="tpu_custom_call" | custom-call | flops 402653184 | bytes 3145728 | tf_op jit(solution)/shard_map/pallas_call | solution.py:232
  36.4 0.0 copy-start.5
  36.4 0.8 %copy-done.5 = bf16[8,128,256]{2,1,0:T(8,128)(2,1)} copy-done((bf16[8,128,256]{2,1,0:T(8,128)(2,1)}, bf16[8,128,256]{2,1,0:T(8,128)(2,1)S(1)}, u32[]{:S(2)}) %copy-start.5) | copy-done | bytes 524312
  37.2 1.4 %collective-permute-start.5 = (bf16[2,128,256]{2,1,0:T(8,128)(2,1)}, bf16[2,128,256]{2,1,0:T(8,128)(2,1)S(1)}, u32[]{:S(2)}, u32[]{:S(2)}) collective-permute-start(bf16[2,128,256]{2,1,0:T(8,128)(2,1)} %get-tuple-element.31), channel_id=1, source_target_pairs={{0,1},{1,2},{2,3},{3,0},{4,5},{5,6},{6,7},{7,4},{8,9},{9,10},{10,1... | collective-permute-start | bytes 393224 | tf_op jit(solution)/shard_map/ppermute | solution.py:266
  38.6 4.2 %collective-permute-start.6 = (bf16[2,128,256]{2,1,0:T(8,128)(2,1)S(1)}, bf16[2,128,256]{2,1,0:T(8,128)(2,1)S(1)}, u32[]{:S(2)}, u32[]{:S(2)}) collective-permute-start(bf16[2,128,256]{2,1,0:T(8,128)(2,1)S(1)} %get-tuple-element.32), channel_id=1, source_target_pairs={{0,2},{1,3},{2,0},{3,1},{4,6},{5,7},{6,4},{7,5},{8,10},{9,11},{10,... | collective-permute-start | bytes 393224 | tf_op jit(solution)/shard_map/ppermute | solution.py:266
  42.8 0.0 collective-permute-start.7
  42.8 0.0 collective-permute-start.9
  42.8 13.1 %collective-permute-done.3.piece_ref = bf16[8,128,256]{2,1,0:T(8,128)(2,1)} collective-permute-done((bf16[8,128,256]{2,1,0:T(8,128)(2,1)}, bf16[8,128,256]{2,1,0:T(8,128)(2,1)}, u32[]{:S(2)}, u32[]{:S(2)}) %collective-permute-start.3) | collective-permute-done | bytes 524320 | tf_op jit(solution)/shard_map/ppermute | solution.py:184
  55.9 1.8 %shard_map.73.refs_0_ = bf16[16,128,256]{2,1,0:T(8,128)(2,1)} custom-call(bf16[8,128,256]{2,1,0:T(8,128)(2,1)} %collective-permute-done.3.piece_ref), custom_call_target="tpu_custom_call" | custom-call | bytes 8388608 | tf_op jit(solution)/shard_map/pallas_call | solution.py:252
  57.8 0.0 collective-permute-done.5
  57.8 0.0 collective-permute-done.6
  57.8 0.0 collective-permute-done.7
  57.8 0.1 convert_add_fusion
  57.9 2.4 %collective-permute-start.8 = (bf16[128,256]{1,0:T(8,128)(2,1)S(1)}, bf16[128,256]{1,0:T(8,128)(2,1)S(1)}, u32[]{:S(2)}, u32[]{:S(2)}) collective-permute-start(bf16[128,256]{1,0:T(8,128)(2,1)S(1)} %fusion), channel_id=1, source_target_pairs={{0,4},{1,5},{2,6},{3,7},{4,0},{5,1},{6,2},{7,3},{8,12},{9,13},{10,... | collective-permute-start | bytes 196616 | tf_op jit(solution)/shard_map/ppermute | solution.py:277
  60.3 7.9 %collective-permute-done.8 = bf16[128,256]{1,0:T(8,128)(2,1)S(1)} collective-permute-done((bf16[128,256]{1,0:T(8,128)(2,1)S(1)}, bf16[128,256]{1,0:T(8,128)(2,1)S(1)}, u32[]{:S(2)}, u32[]{:S(2)}) %collective-permute-start.8) | collective-permute-done | bytes 65568 | tf_op jit(solution)/shard_map/ppermute | solution.py:277
  68.2 0.7 bitcast_add_fusion
  68.9 0.0 collective-permute-done.9.piece_ref
  68.9 0.8 %shard_map.75 = bf16[16,128,256]{2,1,0:T(8,128)(2,1)} custom-call(bf16[8,128,256]{2,1,0:T(8,128)(2,1)S(1)} %collective-permute-done.9.piece_ref, bf16[16,128,256]{2,1,0:T(8,128)(2,1)} %shard_map.73.refs_0_), custom_call_target="tpu_custom_call", output_to_operand_aliasing={{}: (1, {})} | custom-call | bytes 8388608 | tf_op jit(solution)/shard_map/pallas_call | solution.py:252
  (1 shorter events, 0.0 us)
Async XLA Ops:
  0.6 14.1 %copy-start = (bf16[3,32,128,128]{3,2,1,0:T(8,128)(2,1)S(1)}, bf16[3,32,128,128]{3,2,1,0:T(8,128)(2,1)}, u32[]{:S(2)}) copy-start(bf16[3,32,128,128]{3,2,1,0:T(8,128)(2,1)} %refs_3_.7) | copy-start | bytes 9437188
  0.6 14.0 %copy-start.1 = (bf16[1024,256]{1,0:T(8,128)(2,1)S(1)}, bf16[1024,256]{1,0:T(8,128)(2,1)}, u32[]{:S(2)}) copy-start(bf16[1024,256]{1,0:T(8,128)(2,1)} %param.5) | copy-start | bytes 1572868
  0.7 14.0 %copy-start.3 = (s32[3,32]{1,0:T(4,128)S(1)}, s32[3,32]{1,0:T(4,128)}, u32[]{:S(2)}) copy-start(s32[3,32]{1,0:T(4,128)} %refs_1_.7) | copy-start | bytes 1156
  0.7 14.0 %copy-start.4 = (s32[3,1]{0,1:T(1,128)S(1)}, s32[3,1]{0,1:T(1,128)}, u32[]{:S(2)}) copy-start(s32[3,1]{0,1:T(1,128)} %param.9) | copy-start | bytes 40
  6.1 12.1 %collective-permute-start = (bf16[8,128,256]{2,1,0:T(8,128)(2,1)}, bf16[8,128,256]{2,1,0:T(8,128)(2,1)S(1)}, u32[]{:S(2)}, u32[]{:S(2)}) collective-permute-start(bf16[8,128,256]{2,1,0:T(8,128)(2,1)} %get-tuple-element.22), channel_id=1, source_target_pairs={{0,248},{8,0},{16,8},{24,16},{32,24},{40,32},{48,40},{56,48},{64,5... | collective-permute-start | bytes 1572872 | tf_op jit(solution)/shard_map/ppermute | solution.py:184
  8.7 15.1 %collective-permute-start.2 = (bf16[8,128,256]{2,1,0:T(8,128)(2,1)}, bf16[8,128,256]{2,1,0:T(8,128)(2,1)S(1)}, u32[]{:S(2)}, u32[]{:S(2)}) collective-permute-start(bf16[8,128,256]{2,1,0:T(8,128)(2,1)} %get-tuple-element.24), channel_id=1, source_target_pairs={{0,248},{8,0},{16,8},{24,16},{32,24},{40,32},{48,40},{56,48},{64,5... | collective-permute-start | bytes 1572872 | tf_op jit(solution)/shard_map/ppermute | solution.py:184
  14.7 1.2 %copy-start.2 = (bf16[2048,256]{1,0:T(8,128)(2,1)S(1)}, bf16[2048,256]{1,0:T(8,128)(2,1)}, u32[]{:S(2)}) copy-start(bf16[2048,256]{1,0:T(8,128)(2,1)} %param.6) | copy-start | bytes 3145732
  19.8 11.8 %collective-permute-start.1 = (bf16[8,128,256]{2,1,0:T(8,128)(2,1)S(1)}, bf16[8,128,256]{2,1,0:T(8,128)(2,1)S(1)}, u32[]{:S(2)}, u32[]{:S(2)}) collective-permute-start(bf16[8,128,256]{2,1,0:T(8,128)(2,1)S(1)} %get-tuple-element.23), channel_id=1, source_target_pairs={{0,248},{8,0},{16,8},{24,16},{32,24},{40,32},{48,40},{56,48},{64,5... | collective-permute-start | bytes 1572872 | tf_op jit(solution)/shard_map/ppermute | solution.py:184
  25.4 9.0 %collective-permute-start.4 = (bf16[8,128,256]{2,1,0:T(8,128)(2,1)S(1)}, bf16[8,128,256]{2,1,0:T(8,128)(2,1)S(1)}, u32[]{:S(2)}, u32[]{:S(2)}) collective-permute-start(bf16[8,128,256]{2,1,0:T(8,128)(2,1)S(1)} %get-tuple-element.28), channel_id=1, source_target_pairs={{0,248},{8,0},{16,8},{24,16},{32,24},{40,32},{48,40},{56,48},{64,5... | collective-permute-start | bytes 1572872 | tf_op jit(solution)/shard_map/ppermute | solution.py:184
  34.3 21.6 %collective-permute-start.3 = (bf16[8,128,256]{2,1,0:T(8,128)(2,1)}, bf16[8,128,256]{2,1,0:T(8,128)(2,1)}, u32[]{:S(2)}, u32[]{:S(2)}) collective-permute-start(bf16[8,128,256]{2,1,0:T(8,128)(2,1)} %get-tuple-element.27), channel_id=1, source_target_pairs={{0,16},{8,24},{16,32},{24,40},{32,48},{40,56},{48,64},{56,72},{64,... | collective-permute-start | bytes 1572872 | tf_op jit(solution)/shard_map/ppermute | solution.py:184
  36.4 0.8 %copy-start.5 = (bf16[8,128,256]{2,1,0:T(8,128)(2,1)}, bf16[8,128,256]{2,1,0:T(8,128)(2,1)S(1)}, u32[]{:S(2)}) copy-start(bf16[8,128,256]{2,1,0:T(8,128)(2,1)S(1)} %get-tuple-element.38) | copy-start | bytes 1572868
  37.2 20.6 %collective-permute-start.5 = (bf16[2,128,256]{2,1,0:T(8,128)(2,1)}, bf16[2,128,256]{2,1,0:T(8,128)(2,1)S(1)}, u32[]{:S(2)}, u32[]{:S(2)}) collective-permute-start(bf16[2,128,256]{2,1,0:T(8,128)(2,1)} %get-tuple-element.31), channel_id=1, source_target_pairs={{0,1},{1,2},{2,3},{3,0},{4,5},{5,6},{6,7},{7,4},{8,9},{9,10},{10,1... | collective-permute-start | bytes 393224 | tf_op jit(solution)/shard_map/ppermute | solution.py:266
  38.6 19.2 %collective-permute-start.6 = (bf16[2,128,256]{2,1,0:T(8,128)(2,1)S(1)}, bf16[2,128,256]{2,1,0:T(8,128)(2,1)S(1)}, u32[]{:S(2)}, u32[]{:S(2)}) collective-permute-start(bf16[2,128,256]{2,1,0:T(8,128)(2,1)S(1)} %get-tuple-element.32), channel_id=1, source_target_pairs={{0,2},{1,3},{2,0},{3,1},{4,6},{5,7},{6,4},{7,5},{8,10},{9,11},{10,... | collective-permute-start | bytes 393224 | tf_op jit(solution)/shard_map/ppermute | solution.py:266
  42.8 15.0 %collective-permute-start.7 = (bf16[2,128,256]{2,1,0:T(8,128)(2,1)S(1)}, bf16[2,128,256]{2,1,0:T(8,128)(2,1)S(1)}, u32[]{:S(2)}, u32[]{:S(2)}) collective-permute-start(bf16[2,128,256]{2,1,0:T(8,128)(2,1)S(1)} %get-tuple-element.33), channel_id=1, source_target_pairs={{0,3},{1,0},{2,1},{3,2},{4,7},{5,4},{6,5},{7,6},{8,11},{9,8},{10,9... | collective-permute-start | bytes 393224 | tf_op jit(solution)/shard_map/ppermute | solution.py:266
  42.8 26.1 %collective-permute-start.9 = (bf16[8,128,256]{2,1,0:T(8,128)(2,1)}, bf16[8,128,256]{2,1,0:T(8,128)(2,1)S(1)}, u32[]{:S(2)}, u32[]{:S(2)}) collective-permute-start(bf16[8,128,256]{2,1,0:T(8,128)(2,1)} %copy-done.5), channel_id=1, source_target_pairs={{0,16},{8,24},{16,32},{24,40},{32,48},{40,56},{48,64},{56,72},{64,... | collective-permute-start | bytes 1572872 | tf_op jit(solution)/shard_map/ppermute | solution.py:184
  57.9 10.3 %collective-permute-start.8 = (bf16[128,256]{1,0:T(8,128)(2,1)S(1)}, bf16[128,256]{1,0:T(8,128)(2,1)S(1)}, u32[]{:S(2)}, u32[]{:S(2)}) collective-permute-start(bf16[128,256]{1,0:T(8,128)(2,1)S(1)} %fusion), channel_id=1, source_target_pairs={{0,4},{1,5},{2,6},{3,7},{4,0},{5,1},{6,2},{7,3},{8,12},{9,13},{10,... | collective-permute-start | bytes 196616 | tf_op jit(solution)/shard_map/ppermute | solution.py:277

commit v11 on v9

--- a/solution.py
+++ b/solution.py
@@ -22,6 +22,11 @@
 
 def contract(left, right, dims):
     return lax.dot_general(left, right, ((dims[:1], dims[1:]), ((), ())), preferred_element_type=jnp.float32)
+
+
+def split(value, size):
+    assert size & (size - 1) == 0
+    return value >> (size.bit_length() - 1), value & (size - 1)
 
 
 def walk(groups, slot_of, cell_ref, peak_ref, values_at, peak_grad, grad_ref, scaling):
@@ -40,7 +45,7 @@
             for term, f in zip(terms, found):
                 grad_ref[f[3]] += term
 
-    pairs = groups // 2
+    pairs = groups >> 1
 
     def pair(g, carry):
         tiles(g * 2 * group_size, 2 * group_size)
@@ -77,10 +82,10 @@
 
         def slot_of(t):
             place = index[0, t]
-            row, col = place // peak_tiles, place % peak_tiles
+            row, col = split(place, peak_tiles)
             return t, row, col, row, col
 
-        groups = counts[0, 0] // group_size
+        groups, _ = split(counts[0, 0], group_size)
         walk(groups, slot_of, cell_ref, peak_ref, lambda t: values_ref[t], peak_grad, grad_ref, scaling)
         own_tiles = peak_tiles // parts
         for c in range(peak_tiles):
@@ -113,13 +118,13 @@
     row_tiles = grad_ref.shape[0] - 1
     slots = places.shape[0] - group_size
 
-    def note(t, found):
+    found = jnp.int32(0)
+    live = counts[0, stratum]
+    for t in range(slots):
         place = index[stratum, t]
         places[found] = place * slots + t
-        mine = (place % peak_tiles) // own_tiles == part
-        return found + jnp.where(mine, 1, 0)
-
-    found = lax.fori_loop(0, counts[0, stratum], note, 0)
+        owner, _ = split(split(place, peak_tiles)[1], own_tiles)
+        found = found + jnp.where((owner == part) & (t < live), 1, 0)
     for k in range(group_size):
         places[found + k] = -1
     peak_grad[...] = jnp.zeros_like(peak_grad)
@@ -129,11 +134,12 @@
         code = places[k]
         used = code >= 0
         code = jnp.maximum(code, 0)
-        place = code // slots
-        row, col = place // peak_tiles, place % own_tiles
-        return code % slots, row, col, jnp.where(used, row, row_tiles), jnp.where(used, col, own_tiles)
-
-    groups = (found + group_size - 1) // group_size
+        place, t = split(code, slots)
+        row, col = split(place, peak_tiles)
+        col = split(col, own_tiles)[1]
+        return t, row, col, jnp.where(used, row, row_tiles), jnp.where(used, col, own_tiles)
+
+    groups, _ = split(found + group_size - 1, group_size)
     walk(groups, slot_of, cell_ref, peak_ref, lambda t: values[0, t], peak_grad, grad_ref, scaling)
     for c in range(own_tiles):
         new_ref[c] = stepped(peak_ref[c], peak_grad[c], scaling)

time: 71.1 us -> 71.5 us (level); the launches traced: 69.9 us -> 72 us
  waiting for transfers between devices: 21.9 us -> 27.8 us
  starting transfers between devices: 22.8 us -> 20.9 us
  Pallas kernels: 22.6 us -> 20.8 us
    ppermute x6, waiting for transfers between devices: 9.21 us -> 13.3 us  [moved(): lax.ppermute(piece, 'cell', [(i, (i + by) % cells) for i in range(cells)])]
    ppermute x3, starting transfers between devices: 6.82 us -> 4.38 us  [per_device(): lax.ppermute(grads[d], 'chrom', [(j, around[j] + (j + d) % near) for j in...]
    ppermute x1, waiting for transfers between devices: 12.7 us -> 14.5 us  [per_device(): lax.ppermute(sent, 'chrom', [(j, (j + near) % chroms) for j in range(chro...]
    pallas_call x4, Pallas kernels: 11.5 us -> 9.81 us  [part_call(): pl.pallas_call(functools.partial(part_kernel, scaling, stratum, part, pea...]
    ppermute x6, starting transfers between devices: 10.8 us -> 11.7 us  [moved(): lax.ppermute(piece, 'cell', [(i, (i + by) % cells) for i in range(cells)])]
  transfers between devices with their start and end apart: 12 -> 12, of which waited for: 5 -> 5; matrix products, arithmetic and copies ran while one was open for 1% -> 1% of each run, Pallas kernels for 28% -> 25%
where the time goes in v11:
time: 71.5 us; the launch traced here: 72 us
  waiting for transfers between devices  27.8 us (39%)
  starting transfers between devices  20.9 us (29%)
  Pallas kernels  20.8 us (29%)
  between operations  0.96 us (1%)
  local copies, waits for them, and re-layouts  0.85 us (1%)
  other arithmetic  0.73 us (1%)
    ppermute x1, waiting for transfers between devices, per_device(): lax.ppermute(sent, 'chrom', [(j, (j + near) % chroms) for j in range(chro...  14.5 us
    ppermute x6, waiting for transfers between devices, moved(): lax.ppermute(piece, 'cell', [(i, (i + by) % cells) for i in range(cells)])  13.3 us
    ppermute x6, starting transfers between devices, moved(): lax.ppermute(piece, 'cell', [(i, (i + by) % cells) for i in range(cells)])  11.7 us
    pallas_call x4, Pallas kernels, part_call(): pl.pallas_call(functools.partial(part_kernel, scaling, stratum, part, pea...  9.81 us
    pallas_call x2, Pallas kernels, first_call(): pl.pallas_call(functools.partial(first_kernel, scaling, parity), grid=(1,...  8.37 us
    ppermute x2, starting transfers between devices, per_device(): lax.ppermute(piece, 'cell', [(i, i ^ 1) for i in range(cells)])  4.65 us
    ppermute x3, starting transfers between devices, per_device(): lax.ppermute(grads[d], 'chrom', [(j, around[j] + (j + d) % near) for j in...  4.38 us
    pallas_call x2, Pallas kernels, put(): pl.pallas_call(functools.partial(place_kernel, part), grid=(1,), out_shap...  2.64 us
  transfers between devices with their start and end apart: 12, of which 5 were waited for; matrix products, arithmetic and copies ran while one was open for 1% of the time, Pallas kernels for 25%

profile of v11, /device:TPU:1, one launch (start us, length us, event | category | flops | bytes accessed | tf_op | source)
XLA Modules:
  0.0 72.0 jit_solution(10934699411021914528)
XLA Ops:
  0.6 2.1 %shard_map.68 = (bf16[8,128,256]{2,1,0:T(8,128)(2,1)}, bf16[8,128,256]{2,1,0:T(8,128)(2,1)}, f32[8,128,256]{2,1,0:T(8,128)}) custom-call(s32[1,3]{1,0:T(1,128)} %bitcast.14, s32[3,32]{1,0:T(4,128)} %refs_1_.7, bf16[8,128,256]{2,1,0:T(8,128)(2,1)} %bitcast.8, bf16[16,128,256]{2,1,0:T(8,128)(2,1)} %bitcast.20, bf16[3,32,128,128]{3,2,1,0:T(8,128)(2,1)} %refs_3_.7), custom_call_target="tpu_custom_call" | custom-call | flops 805306368 | bytes 4194304 | tf_op jit(solution)/shard_map/pallas_call | solution.py:204
  2.7 0.0 copy-start.1
  2.7 0.0 copy-start.4
  2.7 0.0 copy-start.5
  2.7 6.3 %collective-permute-start.1 = (bf16[8,128,256]{2,1,0:T(8,128)(2,1)}, bf16[8,128,256]{2,1,0:T(8,128)(2,1)}, u32[]{:S(2)}, u32[]{:S(2)}) collective-permute-start(bf16[8,128,256]{2,1,0:T(8,128)(2,1)} %get-tuple-element.26.refs_0_), channel_id=1, source_target_pairs={{0,248},{8,0},{16,8},{24,16},{32,24},{40,32},{48,40},{56,48},{64,5... | collective-permute-start | bytes 1572872 | tf_op jit(solution)/shard_map/ppermute | solution.py:196
  9.1 0.0 copy-start
  9.1 6.3 %shard_map.69 = (bf16[8,128,256]{2,1,0:T(8,128)(2,1)}, bf16[8,128,256]{2,1,0:T(8,128)(2,1)}, f32[8,128,256]{2,1,0:T(8,128)}) custom-call(s32[1,3]{1,0:T(1,128)} %bitcast.15, s32[3,32]{1,0:T(4,128)} %refs_1_.7, bf16[8,128,256]{2,1,0:T(8,128)(2,1)} %bitcast.9, bf16[16,128,256]{2,1,0:T(8,128)(2,1)} %bitcast.21, bf16[3,32,128,128]{3,2,1,0:T(8,128)(2,1)} %refs_3_.7, ...), custom_call_target="tpu_custom_call" | custom-call | flops 805306368 | bytes 4194304 | tf_op jit(solution)/shard_map/pallas_call | solution.py:204
  15.4 0.1 collective-permute-start
  15.5 0.5 collective-permute-start.4
  16.0 4.6 %collective-permute-start.3 = (bf16[8,128,256]{2,1,0:T(8,128)(2,1)}, bf16[8,128,256]{2,1,0:T(8,128)(2,1)S(1)}, u32[]{:S(2)}, u32[]{:S(2)}) collective-permute-start(bf16[8,128,256]{2,1,0:T(8,128)(2,1)} %get-tuple-element.29), channel_id=1, source_target_pairs={{0,8},{8,0},{16,24},{24,16},{32,40},{40,32},{48,56},{56,48},{64,72... | collective-permute-start | bytes 1572872 | tf_op jit(solution)/shard_map/ppermute | solution.py:224
  20.5 0.0 collective-permute-done.1.piece_ref.refs_5_
  20.5 0.0 collective-permute-done.refs_4_
  20.6 0.0 copy-done.1
  20.6 0.0 copy-done.4
  20.6 0.0 copy-done.5
  20.6 0.0 copy-done
  20.6 2.1 %shard_map.71 = (bf16[8,128,256]{2,1,0:T(8,128)(2,1)S(1)}, f32[9,128,256]{2,1,0:T(8,128)S(1)}) custom-call(s32[1,3]{1,0:T(1,128)S(1)} %bitcast.16, s32[3,32]{1,0:T(4,128)S(1)} %copy-done.4, bf16[8,128,256]{2,1,0:T(8,128)(2,1)S(1)} %bitcast.10, bf16[3,32,128,128]{3,2,1,0:T(8,128)(2,1)S(1)} %copy-done, bf16[8,128,256]{2,1,0:T(8,128)(2,1)S(1)} %collective-permute-done.refs_4_, ...), custom_call_target="tpu_custom_call" | custom-call | flops 402653184 | bytes 3145728 | tf_op jit(solution)/shard_map/pallas_call | solution.py:258
  22.7 1.1 %collective-permute-start.2 = (bf16[8,128,256]{2,1,0:T(8,128)(2,1)S(1)}, bf16[8,128,256]{2,1,0:T(8,128)(2,1)S(1)}, u32[]{:S(2)}, u32[]{:S(2)}) collective-permute-start(bf16[8,128,256]{2,1,0:T(8,128)(2,1)S(1)} %get-tuple-element.28), channel_id=1, source_target_pairs={{0,248},{8,0},{16,8},{24,16},{32,24},{40,32},{48,40},{56,48},{64,5... | collective-permute-start | bytes 1572872 | tf_op jit(solution)/shard_map/ppermute | solution.py:196
  23.8 0.6 collective-permute-done.4.piece_ref.refs_5_
  24.4 0.0 collective-permute-done.3.refs_4_
  24.4 1.6 %shard_map.73 = (bf16[8,128,256]{2,1,0:T(8,128)(2,1)S(1)}, f32[9,128,256]{2,1,0:T(8,128)S(1)}) custom-call(s32[1,3]{1,0:T(1,128)S(1)} %bitcast.17, s32[3,32]{1,0:T(4,128)S(1)} %copy-done.4, bf16[8,128,256]{2,1,0:T(8,128)(2,1)S(1)} %bitcast.11, bf16[3,32,128,128]{3,2,1,0:T(8,128)(2,1)S(1)} %copy-done, ...), custom_call_target="tpu_custom_call" | custom-call | flops 402653184 | bytes 3145728 | tf_op jit(solution)/shard_map/pallas_call | solution.py:258
  26.0 3.8 %collective-permute-start.6 = (bf16[8,128,256]{2,1,0:T(8,128)(2,1)S(1)}, bf16[8,128,256]{2,1,0:T(8,128)(2,1)S(1)}, u32[]{:S(2)}, u32[]{:S(2)}) collective-permute-start(bf16[8,128,256]{2,1,0:T(8,128)(2,1)S(1)} %get-tuple-element.34), channel_id=1, source_target_pairs={{0,248},{8,0},{16,8},{24,16},{32,24},{40,32},{48,40},{56,48},{64,5... | collective-permute-start | bytes 1572872 | tf_op jit(solution)/shard_map/ppermute | solution.py:196
  29.8 1.6 %collective-permute-done.2.refs_4_ = bf16[8,128,256]{2,1,0:T(8,128)(2,1)S(1)} collective-permute-done((bf16[8,128,256]{2,1,0:T(8,128)(2,1)S(1)}, bf16[8,128,256]{2,1,0:T(8,128)(2,1)S(1)}, u32[]{:S(2)}, u32[]{:S(2)}) %collective-permute-start.2) | collective-permute-done | bytes 524320 | tf_op jit(solution)/shard_map/ppermute | solution.py:196
  31.4 0.0 copy-start.2
  31.4 0.0 copy-start.3
  31.4 2.7 %shard_map.74 = (bf16[8,128,256]{2,1,0:T(8,128)(2,1)}, f32[9,128,256]{2,1,0:T(8,128)S(1)}) custom-call(s32[1,3]{1,0:T(1,128)S(1)} %bitcast.18, s32[3,32]{1,0:T(4,128)S(1)} %copy-done.4, bf16[8,128,256]{2,1,0:T(8,128)(2,1)S(1)} %bitcast.12, bf16[3,32,128,128]{3,2,1,0:T(8,128)(2,1)S(1)} %copy-done, bf16[8,128,256]{2,1,0:T(8,128)(2,1)S(1)} %collective-permute-done.2.refs_4_, ...), custom_call_target="tpu_custom_call" | custom-call | flops 402653184 | bytes 3145728 | tf_op jit(solution)/shard_map/pallas_call | solution.py:258
  34.1 0.0 collective-permute-start.5
  34.1 2.9 %collective-permute-done.6.refs_4_ = bf16[8,128,256]{2,1,0:T(8,128)(2,1)S(1)} collective-permute-done((bf16[8,128,256]{2,1,0:T(8,128)(2,1)S(1)}, bf16[8,128,256]{2,1,0:T(8,128)(2,1)S(1)}, u32[]{:S(2)}, u32[]{:S(2)}) %collective-permute-start.6) | collective-permute-done | bytes 524320 | tf_op jit(solution)/shard_map/ppermute | solution.py:196
  37.0 0.0 copy-done.2
  37.0 0.0 copy-done.3
  37.0 3.4 %shard_map.76 = (bf16[8,128,256]{2,1,0:T(8,128)(2,1)S(1)}, bf16[2,128,256]{2,1,0:T(8,128)(2,1)S(1)}, bf16[2,128,256]{2,1,0:T(8,128)(2,1)}, bf16[2,128,256]{2,1,0:T(8,128)(2,1)S(1)}, bf16[2,128,256]{2,1,0:T(8,128)(2,1)S(1)}) custom-call(s32[1,3]{1,0:T(1,128)S(1)} %bitcast.19, s32[3,32]{1,0:T(4,128)S(1)} %copy-done.4, bf16[8,128,256]{2,1,0:T(8,128)(2,1)S(1)} %bitcast.13, ...), custom_call_target="tpu_custom_call" | custom-call | flops 402653184 | bytes 3145728 | tf_op jit(solution)/shard_map/pallas_call | solution.py:258
  40.4 0.0 copy-start.6
  40.4 0.8 %copy-done.6 = bf16[8,128,256]{2,1,0:T(8,128)(2,1)} copy-done((bf16[8,128,256]{2,1,0:T(8,128)(2,1)}, bf16[8,128,256]{2,1,0:T(8,128)(2,1)S(1)}, u32[]{:S(2)}) %copy-start.6) | copy-done | bytes 524312
  41.2 2.0 %collective-permute-start.7 = (bf16[2,128,256]{2,1,0:T(8,128)(2,1)}, bf16[2,128,256]{2,1,0:T(8,128)(2,1)S(1)}, u32[]{:S(2)}, u32[]{:S(2)}) collective-permute-start(bf16[2,128,256]{2,1,0:T(8,128)(2,1)} %get-tuple-element.39), channel_id=1, source_target_pairs={{0,1},{1,2},{2,3},{3,0},{4,5},{5,6},{6,7},{7,4},{8,9},{9,10},{10,1... | collective-permute-start | bytes 393224 | tf_op jit(solution)/shard_map/ppermute | solution.py:292
  43.2 2.3 %collective-permute-start.8 = (bf16[2,128,256]{2,1,0:T(8,128)(2,1)S(1)}, bf16[2,128,256]{2,1,0:T(8,128)(2,1)S(1)}, u32[]{:S(2)}, u32[]{:S(2)}) collective-permute-start(bf16[2,128,256]{2,1,0:T(8,128)(2,1)S(1)} %get-tuple-element.40), channel_id=1, source_target_pairs={{0,2},{1,3},{2,0},{3,1},{4,6},{5,7},{6,4},{7,5},{8,10},{9,11},{10,... | collective-permute-start | bytes 393224 | tf_op jit(solution)/shard_map/ppermute | solution.py:292
  45.5 0.1 collective-permute-start.9
  45.6 0.0 collective-permute-start.11
  45.6 8.2 %collective-permute-done.5.piece_ref = bf16[8,128,256]{2,1,0:T(8,128)(2,1)} collective-permute-done((bf16[8,128,256]{2,1,0:T(8,128)(2,1)}, bf16[8,128,256]{2,1,0:T(8,128)(2,1)}, u32[]{:S(2)}, u32[]{:S(2)}) %collective-permute-start.5) | collective-permute-done | bytes 524320 | tf_op jit(solution)/shard_map/ppermute | solution.py:196
  53.8 1.8 %shard_map.75.refs_0_ = bf16[16,128,256]{2,1,0:T(8,128)(2,1)} custom-call(bf16[8,128,256]{2,1,0:T(8,128)(2,1)} %collective-permute-done.5.piece_ref), custom_call_target="tpu_custom_call" | custom-call | bytes 8388608 | tf_op jit(solution)/shard_map/pallas_call | solution.py:278
  55.7 0.0 collective-permute-done.7
  55.7 0.0 collective-permute-done.8
  55.7 0.0 collective-permute-done.9
  55.7 0.1 convert_add_fusion
  55.8 0.1 collective-permute-start.10
  55.9 14.5 %collective-permute-done.10 = bf16[128,256]{1,0:T(8,128)(2,1)S(1)} collective-permute-done((bf16[128,256]{1,0:T(8,128)(2,1)S(1)}, bf16[128,256]{1,0:T(8,128)(2,1)S(1)}, u32[]{:S(2)}, u32[]{:S(2)}) %collective-permute-start.10) | collective-permute-done | bytes 65568 | tf_op jit(solution)/shard_map/ppermute | solution.py:303
  70.4 0.7 bitcast_add_fusion
  71.0 0.0 collective-permute-done.11.piece_ref
  71.0 0.8 %shard_map.77 = bf16[16,128,256]{2,1,0:T(8,128)(2,1)} custom-call(bf16[8,128,256]{2,1,0:T(8,128)(2,1)S(1)} %collective-permute-done.11.piece_ref, bf16[16,128,256]{2,1,0:T(8,128)(2,1)} %shard_map.75.refs_0_), custom_call_target="tpu_custom_call", output_to_operand_aliasing={{}: (1, {})} | custom-call | bytes 8388608 | tf_op jit(solution)/shard_map/pallas_call | solution.py:278
  (3 shorter events, 0.0 us)
Async XLA Ops:
  2.7 17.9 %copy-start.1 = (bf16[1024,256]{1,0:T(8,128)(2,1)S(1)}, bf16[1024,256]{1,0:T(8,128)(2,1)}, u32[]{:S(2)}) copy-start(bf16[1024,256]{1,0:T(8,128)(2,1)} %param.5) | copy-start | bytes 1572868
  2.7 17.9 %copy-start.4 = (s32[3,32]{1,0:T(4,128)S(1)}, s32[3,32]{1,0:T(4,128)}, u32[]{:S(2)}) copy-start(s32[3,32]{1,0:T(4,128)} %refs_1_.7) | copy-start | bytes 1156
  2.7 17.8 %copy-start.5 = (s32[3,1]{0,1:T(1,128)S(1)}, s32[3,1]{0,1:T(1,128)}, u32[]{:S(2)}) copy-start(s32[3,1]{0,1:T(1,128)} %param.9) | copy-start | bytes 40
  2.7 17.8 %collective-permute-start.1 = (bf16[8,128,256]{2,1,0:T(8,128)(2,1)}, bf16[8,128,256]{2,1,0:T(8,128)(2,1)}, u32[]{:S(2)}, u32[]{:S(2)}) collective-permute-start(bf16[8,128,256]{2,1,0:T(8,128)(2,1)} %get-tuple-element.26.refs_0_), channel_id=1, source_target_pairs={{0,248},{8,0},{16,8},{24,16},{32,24},{40,32},{48,40},{56,48},{64,5... | collective-permute-start | bytes 1572872 | tf_op jit(solution)/shard_map/ppermute | solution.py:196
  9.1 11.5 %copy-start = (bf16[3,32,128,128]{3,2,1,0:T(8,128)(2,1)S(1)}, bf16[3,32,128,128]{3,2,1,0:T(8,128)(2,1)}, u32[]{:S(2)}) copy-start(bf16[3,32,128,128]{3,2,1,0:T(8,128)(2,1)} %refs_3_.7) | copy-start | bytes 9437188
  15.4 5.2 %collective-permute-start = (bf16[8,128,256]{2,1,0:T(8,128)(2,1)}, bf16[8,128,256]{2,1,0:T(8,128)(2,1)S(1)}, u32[]{:S(2)}, u32[]{:S(2)}) collective-permute-start(bf16[8,128,256]{2,1,0:T(8,128)(2,1)} %get-tuple-element.27), channel_id=1, source_target_pairs={{0,8},{8,0},{16,24},{24,16},{32,40},{40,32},{48,56},{56,48},{64,72... | collective-permute-start | bytes 1572872 | tf_op jit(solution)/shard_map/ppermute | solution.py:224
  15.5 8.9 %collective-permute-start.4 = (bf16[8,128,256]{2,1,0:T(8,128)(2,1)}, bf16[8,128,256]{2,1,0:T(8,128)(2,1)S(1)}, u32[]{:S(2)}, u32[]{:S(2)}) collective-permute-start(bf16[8,128,256]{2,1,0:T(8,128)(2,1)} %get-tuple-element.30), channel_id=1, source_target_pairs={{0,248},{8,0},{16,8},{24,16},{32,24},{40,32},{48,40},{56,48},{64,5... | collective-permute-start | bytes 1572872 | tf_op jit(solution)/shard_map/ppermute | solution.py:196
  16.0 8.4 %collective-permute-start.3 = (bf16[8,128,256]{2,1,0:T(8,128)(2,1)}, bf16[8,128,256]{2,1,0:T(8,128)(2,1)S(1)}, u32[]{:S(2)}, u32[]{:S(2)}) collective-permute-start(bf16[8,128,256]{2,1,0:T(8,128)(2,1)} %get-tuple-element.29), channel_id=1, source_target_pairs={{0,8},{8,0},{16,24},{24,16},{32,40},{40,32},{48,56},{56,48},{64,72... | collective-permute-start | bytes 1572872 | tf_op jit(solution)/shard_map/ppermute | solution.py:224
  22.7 8.7 %collective-permute-start.2 = (bf16[8,128,256]{2,1,0:T(8,128)(2,1)S(1)}, bf16[8,128,256]{2,1,0:T(8,128)(2,1)S(1)}, u32[]{:S(2)}, u32[]{:S(2)}) collective-permute-start(bf16[8,128,256]{2,1,0:T(8,128)(2,1)S(1)} %get-tuple-element.28), channel_id=1, source_target_pairs={{0,248},{8,0},{16,8},{24,16},{32,24},{40,32},{48,40},{56,48},{64,5... | collective-permute-start | bytes 1572872 | tf_op jit(solution)/shard_map/ppermute | solution.py:196
  26.0 11.0 %collective-permute-start.6 = (bf16[8,128,256]{2,1,0:T(8,128)(2,1)S(1)}, bf16[8,128,256]{2,1,0:T(8,128)(2,1)S(1)}, u32[]{:S(2)}, u32[]{:S(2)}) collective-permute-start(bf16[8,128,256]{2,1,0:T(8,128)(2,1)S(1)} %get-tuple-element.34), channel_id=1, source_target_pairs={{0,248},{8,0},{16,8},{24,16},{32,24},{40,32},{48,40},{56,48},{64,5... | collective-permute-start | bytes 1572872 | tf_op jit(solution)/shard_map/ppermute | solution.py:196
  31.4 5.6 %copy-start.2 = (f32[8,128,256]{2,1,0:T(8,128)S(1)}, f32[8,128,256]{2,1,0:T(8,128)}, u32[]{:S(2)}) copy-start(f32[8,128,256]{2,1,0:T(8,128)} %get-tuple-element.36.refs_6_) | copy-start | bytes 3145732
  31.4 5.6 %copy-start.3 = (f32[8,128,256]{2,1,0:T(8,128)S(1)}, f32[8,128,256]{2,1,0:T(8,128)}, u32[]{:S(2)}) copy-start(f32[8,128,256]{2,1,0:T(8,128)} %get-tuple-element.37.refs_7_) | copy-start | bytes 3145732
  34.1 19.7 %collective-permute-start.5 = (bf16[8,128,256]{2,1,0:T(8,128)(2,1)}, bf16[8,128,256]{2,1,0:T(8,128)(2,1)}, u32[]{:S(2)}, u32[]{:S(2)}) collective-permute-start(bf16[8,128,256]{2,1,0:T(8,128)(2,1)} %get-tuple-element.33), channel_id=1, source_target_pairs={{0,16},{8,24},{16,32},{24,40},{32,48},{40,56},{48,64},{56,72},{64,... | collective-permute-start | bytes 1572872 | tf_op jit(solution)/shard_map/ppermute | solution.py:196
  40.4 0.8 %copy-start.6 = (bf16[8,128,256]{2,1,0:T(8,128)(2,1)}, bf16[8,128,256]{2,1,0:T(8,128)(2,1)S(1)}, u32[]{:S(2)}) copy-start(bf16[8,128,256]{2,1,0:T(8,128)(2,1)S(1)} %get-tuple-element.46) | copy-start | bytes 1572868
  41.2 14.5 %collective-permute-start.7 = (bf16[2,128,256]{2,1,0:T(8,128)(2,1)}, bf16[2,128,256]{2,1,0:T(8,128)(2,1)S(1)}, u32[]{:S(2)}, u32[]{:S(2)}) collective-permute-start(bf16[2,128,256]{2,1,0:T(8,128)(2,1)} %get-tuple-element.39), channel_id=1, source_target_pairs={{0,1},{1,2},{2,3},{3,0},{4,5},{5,6},{6,7},{7,4},{8,9},{9,10},{10,1... | collective-permute-start | bytes 393224 | tf_op jit(solution)/shard_map/ppermute | solution.py:292
  43.2 12.5 %collective-permute-start.8 = (bf16[2,128,256]{2,1,0:T(8,128)(2,1)S(1)}, bf16[2,128,256]{2,1,0:T(8,128)(2,1)S(1)}, u32[]{:S(2)}, u32[]{:S(2)}) collective-permute-start(bf16[2,128,256]{2,1,0:T(8,128)(2,1)S(1)} %get-tuple-element.40), channel_id=1, source_target_pairs={{0,2},{1,3},{2,0},{3,1},{4,6},{5,7},{6,4},{7,5},{8,10},{9,11},{10,... | collective-permute-start | bytes 393224 | tf_op jit(solution)/shard_map/ppermute | solution.py:292
  45.5 10.2 %collective-permute-start.9 = (bf16[2,128,256]{2,1,0:T(8,128)(2,1)S(1)}, bf16[2,128,256]{2,1,0:T(8,128)(2,1)S(1)}, u32[]{:S(2)}, u32[]{:S(2)}) collective-permute-start(bf16[2,128,256]{2,1,0:T(8,128)(2,1)S(1)} %get-tuple-element.41), channel_id=1, source_target_pairs={{0,3},{1,0},{2,1},{3,2},{4,7},{5,4},{6,5},{7,6},{8,11},{9,8},{10,9... | collective-permute-start | bytes 393224 | tf_op jit(solution)/shard_map/ppermute | solution.py:292
  45.6 25.4 %collective-permute-start.11 = (bf16[8,128,256]{2,1,0:T(8,128)(2,1)}, bf16[8,128,256]{2,1,0:T(8,128)(2,1)S(1)}, u32[]{:S(2)}, u32[]{:S(2)}) collective-permute-start(bf16[8,128,256]{2,1,0:T(8,128)(2,1)} %copy-done.6), channel_id=1, source_target_pairs={{0,16},{8,24},{16,32},{24,40},{32,48},{40,56},{48,64},{56,72},{64,... | collective-permute-start | bytes 1572872 | tf_op jit(solution)/shard_map/ppermute | solution.py:196
  55.8 14.6 %collective-permute-start.10 = (bf16[128,256]{1,0:T(8,128)(2,1)S(1)}, bf16[128,256]{1,0:T(8,128)(2,1)S(1)}, u32[]{:S(2)}, u32[]{:S(2)}) collective-permute-start(bf16[128,256]{1,0:T(8,128)(2,1)S(1)} %fusion), channel_id=1, source_target_pairs={{0,4},{1,5},{2,6},{3,7},{4,0},{5,1},{6,2},{7,3},{8,12},{9,13},{10,... | collective-permute-start | bytes 196616 | tf_op jit(solution)/shard_map/ppermute | solution.py:303
